TPU v7x, 32 devices: a whole 2x2x4 slice. The times are simulated.
32 devices in a mesh: dp: 16 (over z, x, core), tensor: 2 (over y).
Axes of the slice: x: 2, y: 2, z: 4, core: 2. Of those that a mesh axis runs over, the one named last changes fastest.
Arguments:
- activations: bfloat16 [12288, 4096], P('dp'), may hold values from -6 to 6
- grad_out: bfloat16 [12288, 2, 1024], P('dp', None, 'tensor'), may hold values from -0.059814453 to 0.059814453
- weights: float32 [4096, 2, 1024], P('dp', None, 'tensor')
- first_moment: float32 [4096, 2, 1024], P('dp', None, 'tensor'), may hold values from -6 to 6
- second_moment: float32 [4096, 2, 1024], P('dp', None, 'tensor')
- step: int32 [1], replicated, may hold values from 1 to 40
Outputs:
- new_weights: float32 [4096, 2, 1024], P('dp', None, 'tensor')
- new_first: float32 [4096, 2, 1024], P('dp', None, 'tensor')
- new_second: float32 [4096, 2, 1024], P('dp', None, 'tensor')
- ratios: float32 [2], replicated
- new_kv: bfloat16 [12288, 2, 1024], P('dp', None, 'tensor')
All inputs are finite; a program needn't handle non-finite values.
Results may differ from a plain program's by a relative error of at most 0.001.
The roundings to bfloat16 on the way count: a program that leaves them out, or rounds other values in their place, can miss the bound.
Values may be sent and summed in bfloat16 or wider, within the bound.
No kernel may reach another device: no remote copies, remote signals or barrier semaphores. Data moves between devices by JAX's collectives and lax.ppermute only.
A program may use at most 64 MiB of HBM per device.

v0:
```python
import math

import jax
import jax.numpy as jnp
from jax import lax
from jax.sharding import PartitionSpec as P


def optimize(grad, weights, first_moment, second_moment, count):
    new_first = 0.9 * first_moment + 0.1 * grad
    new_second = 0.95 * second_moment + 0.05 * grad * grad
    bias_one = 1.0 - jnp.exp(count * math.log(0.9))
    bias_two = 1.0 - jnp.exp(count * math.log(0.95))
    update = new_first / bias_one / (jnp.sqrt(new_second / bias_two) + 1e-06) + 0.1 * weights
    return (new_first, new_second, update)


def local(activations, grad_out, weights, first_moment, second_moment, step):
    count = step[0].astype(jnp.float32)
    columns = activations
    grad = lax.psum_scatter(
        jnp.einsum("td,tsc->dsc", columns, grad_out, preferred_element_type=jnp.float32),
        "dp",
        scatter_dimension=0,
        tiled=True,
    )
    new_first, new_second, update = optimize(grad, weights, first_moment, second_moment, count)
    partial_sq = jnp.stack(
        [jnp.sum(weights * weights, axis=(0, 2)), jnp.sum(update * update, axis=(0, 2))]
    )
    totals = lax.psum(partial_sq, ("dp", "tensor"))
    ratios = jnp.sqrt(totals[0]) / (jnp.sqrt(totals[1]) + 1e-06)
    new_weights = weights - 0.05 * ratios[None, :, None] * update
    half_weights = new_weights.astype(jnp.bfloat16)
    columns = activations
    fresh = jnp.einsum(
        "td,dsc->tsc",
        columns,
        lax.all_gather(half_weights, "dp", axis=0, tiled=True),
        preferred_element_type=jnp.float32,
    )
    new_kv = fresh.astype(jnp.bfloat16)
    return (new_weights, new_first, new_second, ratios, new_kv)


def solution(mesh):
    in_specs = (
        P("dp", None),
        P("dp", None, "tensor"),
        P("dp", None, "tensor"),
        P("dp", None, "tensor"),
        P("dp", None, "tensor"),
        P(),
    )
    out_specs = (
        P("dp", None, "tensor"),
        P("dp", None, "tensor"),
        P("dp", None, "tensor"),
        P(),
        P("dp", None, "tensor"),
    )
    return jax.shard_map(local, mesh=mesh, in_specs=in_specs, out_specs=out_specs, check_vma=False)
```

profile of v0, /device:TPU:0, one launch (start us, length us, event | category | flops | bytes accessed | tf_op | source)
XLA Modules:
  0.0 345.9 jit_solution(142052019472044811)
XLA Ops:
  7.2 0.0 copy-start
  7.2 0.0 reduce-scatter.2.cloned.1.call-start
  7.2 1.4 copy-done
  8.6 13.1 %fusion.2 = f32[4096,2,512]{2,0,1:T(8,128)} fusion(bf16[768,4096]{1,0:T(8,128)(2,1)} %param.6, bf16[768,2,512]{2,1,0:T(2,128)(2,1)S(1)} %copy-done), kind=kOutput, calls=%fused_computation.2 | convolution fusion | flops 6442450944 | bytes 24641536 | tf_op jit(solution)/shard_map/td,tsc->dsc/dot_general | solution.py:22
  21.7 0.0 copy-start.1
  21.7 0.0 reduce-scatter.2.cloned.1.call-update
  21.7 0.0 all-gather.2.cloned.1.call-start
  22.6 0.4 copy-done.1
  23.0 1.2 multiply_reduce_fusion.1
  24.2 179.0 %reduce-scatter.2.cloned.1.call-done = f32[256,2,512]{2,0,1:T(8,128)} async-done(((f32[4096,2,512]{2,0,1:T(8,128)}), f32[256,2,512]{2,0,1:T(8,128)}) %reduce-scatter.2.cloned.1.call-update) | async-done | bytes 1048592 | tf_op jit(solution)/shard_map/reduce_scatter | solution.py:21
  203.2 4.5 %multiply_reduce_fusion = (f32[2]{0:T(128)S(1)}, f32[256,2,512]{2,0,1:T(8,128)}, f32[256,2,512]{2,0,1:T(8,128)}, f32[256,2,512]{2,0,1:T(8,128)}) fusion(f32[256,2,512]{2,1,0:T(2,128)S(1)} %copy-done.1, f32[]{:T(128)} %bitcast.3, f32[]{:T(128)} %bitcast.2, f32[256,2,512]{2,0,1:T(8,128)} %reduce-scatter.2.cloned.1.call-done, f32[256,2,512]{2,1,0:T(2,128)} %param.10, ...), kind=kLoop, calls=%fused_computation.13 | loop fusion | flops 3932158 | bytes 7340048 | tf_op jit(solution)/shard_map/reduce_sum | solution.py:29
  207.6 39.3 %psum.7 = f32[2,2]{1,0:T(2,128)S(1)} all-reduce(f32[2,2]{1,0:T(2,128)S(1)} %pad_maximum_fusion), channel_id=1, replica_groups=mesh['dp'=16,'tensor'=2] {'dp','tensor'}, use_global_device_ids=true, to_apply=%region_3.0 | all-reduce | flops 4 | bytes 32 | tf_op jit(solution)/shard_map/psum | solution.py:31
  246.9 0.5 broadcast_multiply_fusion
  247.5 2.7 fusion.14
  250.2 0.0 all-gather.2.cloned.1.call-update
  250.2 3.0 copy.18
  253.2 3.0 copy.19
  256.2 3.1 copy.20
  259.3 65.8 %all-gather.2.cloned.1.call-done = bf16[4096,2,512]{2,0,1:T(8,128)(2,1)} async-done(((bf16[256,2,512]{2,0,1:T(8,128)(2,1)}), bf16[4096,2,512]{2,0,1:T(8,128)(2,1)}) %all-gather.2.cloned.1.call-update) | async-done | bytes 8388624 | tf_op jit(solution)/shard_map/all_gather | solution.py:39
  325.0 11.0 %fusion.8 = bf16[768,2,512]{0,2,1:T(8,128)(2,1)S(1)} fusion(bf16[4096,2,512]{2,0,1:T(8,128)(2,1)} %all-gather.2.cloned.1.call-done, bf16[768,4096]{1,0:T(8,128)(2,1)} %param.6), kind=kOutput, calls=%fused_computation.7 | convolution fusion | flops 6443237376 | bytes 16252928 | tf_op jit(solution)/shard_map/td,dsc->tsc/dot_general | solution.py:36
  336.1 3.0 copy.21
  (1 shorter events, 0.0 us)
Async XLA Ops:
  7.2 1.4 copy-start
  7.2 196.0 %reduce-scatter.2.cloned.1.call-start = ((), (), s32[]{:S(2)}) async-start(), calls=%async_computation.1 | async-start | bytes 17825792 | tf_op jit(solution)/shard_map/reduce_scatter | solution.py:21
  21.7 1.2 copy-start.1
  21.7 303.3 %all-gather.2.cloned.1.call-start = ((), (), s32[]{:S(2)}) async-start(), calls=%async_computation.2 | async-start | bytes 8912896 | tf_op jit(solution)/shard_map/all_gather | solution.py:39
Sparse Core Ops, SparseCore 0:
  21.9 181.2 reduce-scatter.1
  250.3 74.6 all-gather.1
where the time goes:
time: 346 us
  waiting for transfers between devices  245 us (71%)
  blocking collectives  39.3 us (11%)
  matrix products  24.2 us (7%)
  between operations  14.9 us (4%)
  local copies, waits for them, and re-layouts  13.8 us (4%)
  other arithmetic  8.91 us (3%)
    reduce_scatter x1, waiting for transfers between devices, local(): lax.psum_scatter(jnp.einsum('td,tsc->dsc', columns, grad_out, preferred_e...  179 us
    all_gather x1, waiting for transfers between devices, local(): lax.all_gather(half_weights, 'dp', axis=0, tiled=True)  65.8 us
    psum x1, blocking collectives, local(): totals = lax.psum(partial_sq, ('dp', 'tensor'))  39.3 us
    unnamed x8, local copies, waits for them, and re-layouts  13.8 us
    dot_general x1, matrix products, local(): jnp.einsum('td,tsc->dsc', columns, grad_out, preferred_element_type=jnp.f...  13.1 us
    dot_general x1, matrix products, local(): jnp.einsum('td,dsc->tsc', columns, lax.all_gather(half_weights, 'dp', axi...  11 us
  transfers between devices with their start and end apart: 2, of which 2 were waited for; matrix products, arithmetic and copies ran while one was open for 3% of the time, Pallas kernels for 0%

commit v1 on v0

v1 whole, which is shorter than its diff:
```python
import math

import jax
import jax.numpy as jnp
from jax import lax
from jax.experimental import pallas as pl
from jax.experimental.pallas import tpu as pltpu
from jax.sharding import PartitionSpec as P

F32 = jnp.float32
LANES = 128


def after(value, *others):
    return lax.optimization_barrier((value, *others))[0]


def pick_blocks(activations, blocks, width):
    if width % LANES:
        return jnp.concatenate(
            [lax.dynamic_slice_in_dim(activations, block * width, width, 1) for block in blocks], axis=1
        )
    count = len(blocks)

    def kernel(places, src, dst, sems):
        copies = [
            pltpu.make_async_copy(
                src.at[:, pl.ds(pl.multiple_of(places[i] * width, width), width)],
                dst.at[:, pl.ds(i * width, width)],
                sems.at[i],
            )
            for i in range(count)
        ]
        for copy in copies:
            copy.start()
        for copy in copies:
            copy.wait()

    return pl.pallas_call(
        kernel,
        out_shape=jax.ShapeDtypeStruct((activations.shape[0], count * width), activations.dtype),
        in_specs=[pl.BlockSpec(memory_space=pltpu.SMEM), pl.BlockSpec(memory_space=pl.ANY)],
        out_specs=pl.BlockSpec(memory_space=pltpu.VMEM),
        scratch_shapes=[pltpu.SemaphoreType.DMA((count,))],
    )(jnp.stack(blocks).astype(jnp.int32), activations)


def make_local(n, t):
    bits = n.bit_length() - 1
    links = list(range(1, bits))
    orders = [links, [links[1], links[0], *links[2:]]]
    others = []
    for place in range(n // 2):
        others.append(
            sum(1 << bit for depth, bit in enumerate(links) if (place >> (len(links) - 1 - depth)) & 1)
        )

    def swap(value, bit):
        return lax.ppermute(value, "dp", [(i, i ^ (1 << bit)) for i in range(n)])

    def total(value):
        for bit in reversed(range(bits)):
            value = value + swap(value, bit)
        for bit in range(t.bit_length() - 1):
            value = value + lax.ppermute(value, "tensor", [(i, i ^ (1 << bit)) for i in range(t)])
        return value

    def dot_t(a, g):
        return lax.dot_general(a, g, (((0,), (0,)), ((), ())), preferred_element_type=F32)

    def dot(a, w):
        return lax.dot_general(a, w, (((1,), (0,)), ((), ())), preferred_element_type=F32)

    def local(activations, grad_out, weights, first_moment, second_moment, step):
        rows, kinds, cols = weights.shape
        cut = cols // 2
        parts = [slice(0, cut), slice(cut, cols)]
        count = step[0].astype(F32)
        bias_one = 1.0 - jnp.exp(count * math.log(0.9))
        bias_two = 1.0 - jnp.exp(count * math.log(0.95))
        me = lax.axis_index("dp")

        theirs = pick_blocks(activations, [me ^ (j + 1) for j in others], rows)
        sibling = swap(theirs, 0)
        grads_out = [grad_out[:, s, :] for s in range(kinds)]
        siblings_out = [swap(g, 0) for g in grads_out]
        mine = pick_blocks(after(activations, theirs), [me ^ j for j in others], rows)

        held, got = {}, {}

        def send(s, k, depth, *gates):
            axes = [b for b in links if b not in orders[k][:depth]]
            bit = orders[k][depth]
            axis = axes.index(bit)
            out = lax.index_in_dim(held[s, k], 1, axis, keepdims=False).astype(jnp.float16)
            held[s, k] = lax.index_in_dim(held[s, k], 0, axis, keepdims=False)
            if gates:
                out = after(out, *gates)
            got[s, k, depth] = swap(out, bit)

        def take(s, k, depth, *gates):
            value = got[s, k, depth]
            if gates:
                value = after(value, *gates)
            held[s, k] = held[s, k] + value.astype(F32)

        chunks = range(len(parts))
        deep = len(links)

        def product(s):
            whole = dot_t(mine, grads_out[s]) + dot_t(sibling, siblings_out[s])
            for k in chunks:
                held[s, k] = whole[:, parts[k]].reshape((2,) * deep + (rows, -1))
            return whole

        lead = product(0)
        weights, first_moment, second_moment = (
            after(x, lead) for x in (weights, first_moment, second_moment)
        )
        for k in chunks:
            send(0, k, 0)
        for s in range(1, kinds):
            product(s)
        for depth in range(deep):
            for s in range(kinds):
                if depth == 0 and s > 0:
                    for k in chunks:
                        send(s, k, 0, *[got[s - 1, j, 0] for j in chunks])
                for k in chunks:
                    gates = [got[s - 1, j, depth + 1] for j in chunks] if s > 0 and depth + 1 < deep else []
                    take(s, k, depth, *gates)
                for k in chunks:
                    if depth + 1 < deep:
                        send(s, k, depth + 1)

        weight_sq = jnp.sum(weights * weights, axis=(0, 2))
        ratios, news, kvs = [], [], []
        for s in range(kinds):
            grad = jnp.concatenate([held[s, k] for k in chunks], axis=1)
            first = 0.9 * first_moment[:, s] + 0.1 * grad
            second = 0.95 * second_moment[:, s] + 0.05 * grad * grad
            update = first / bias_one / (jnp.sqrt(second / bias_two) + 1e-06) + 0.1 * weights[:, s]
            update_sq = jnp.sum(update * update)
            if s == 0:
                sums = total(jnp.stack([update_sq, *[weight_sq[i] for i in range(kinds)]]))
                update_total, weight_totals = sums[0], sums[1:]
            else:
                update_total = total(update_sq[None])[0]
            ratio = jnp.sqrt(weight_totals[s]) / (jnp.sqrt(update_total) + 1e-06)
            ratios.append(ratio)
            fresh = weights[:, s] - 0.05 * ratio * update
            news.append((fresh, first, second))
            half_weights = fresh.astype(jnp.bfloat16)
            gathered = [half_weights[:, part] for part in parts]
            for depth in reversed(range(deep)):
                arrived = [swap(gathered[k], orders[k][depth]) for k in chunks]
                for k in chunks:
                    axes = [b for b in links if b not in orders[k][:depth]]
                    axis = axes.index(orders[k][depth])
                    gathered[k] = jnp.stack([gathered[k], arrived[k]], axis=axis)
            for k in chunks:
                own = gathered[k].reshape(-1, gathered[k].shape[-1])
                other = swap(own, 0)
                kvs.append((dot(mine, own) + dot(theirs, other)).astype(jnp.bfloat16))
        new_kv = jnp.concatenate(kvs, axis=1).reshape(-1, kinds, cols)
        new_weights, new_first, new_second = (jnp.stack(x, axis=1) for x in zip(*news))
        return (new_weights, new_first, new_second, jnp.stack(ratios), new_kv)

    return local


def solution(mesh):
    in_specs = (
        P("dp", None),
        P("dp", None, "tensor"),
        P("dp", None, "tensor"),
        P("dp", None, "tensor"),
        P("dp", None, "tensor"),
        P(),
    )
    out_specs = (
        P("dp", None, "tensor"),
        P("dp", None, "tensor"),
        P("dp", None, "tensor"),
        P(),
        P("dp", None, "tensor"),
    )
    local = make_local(mesh.shape["dp"], mesh.shape["tensor"])
    return jax.shard_map(local, mesh=mesh, in_specs=in_specs, out_specs=out_specs, check_vma=False)
```

time: 346 us -> 198 us (0.57)
  waiting for transfers between devices: 245 us -> 79.2 us
  starting transfers between devices: 0.08 us -> 50.4 us
  blocking collectives: 39.3 us -> 0 us
  Pallas kernels: 0 us -> 8.5 us
  between operations: 14.9 us -> 7.6 us
  local copies, waits for them, and re-layouts: 13.8 us -> 20.6 us
    reduce_scatter x1 -> x0, waiting for transfers between devices: 179 us -> none  [local(): lax.psum_scatter(jnp.einsum('td,tsc->dsc', columns, grad_out, preferred_e...]
    ppermute x0 -> x41, waiting for transfers between devices: none -> 79.2 us  [the longest x39 76.3 us: swap(): return lax.ppermute(value, 'dp', [(i, i ^ 1 << bit) for i in range(n)])]
    all_gather x1 -> x0, waiting for transfers between devices: 65.8 us -> none  [local(): lax.all_gather(half_weights, 'dp', axis=0, tiled=True)]
    ppermute x0 -> x41, starting transfers between devices: none -> 50.4 us  [the longest x39 46.1 us: swap(): return lax.ppermute(value, 'dp', [(i, i ^ 1 << bit) for i in range(n)])]
    psum x1 -> x0, blocking collectives: 39.3 us -> none  [local(): totals = lax.psum(partial_sq, ('dp', 'tensor'))]
    pallas_call x0 -> x2, Pallas kernels: none -> 8.5 us  [pick_blocks(): pl.pallas_call(kernel, out_shape=jax.ShapeDtypeStruct((activations.shape[...]
    slice x0 -> x6, local copies, waits for them, and re-layouts: none -> 6.12 us  [the longest x1 4.61 us: local(): grads_out = [grad_out[:, s, :] for s in range(kinds)]]
    dot_general x2 -> x12, matrix products: 24.2 us -> 22.1 us  [the longest x4 13.2 us: dot_t(): lax.dot_general(a, g, (((0,), (0,)), ((), ())), preferred_element_type=F32)]
  transfers between devices with their start and end apart: 2 -> 41, of which waited for: 2 -> 24; matrix products, arithmetic and copies ran while one was open for 3% -> 21% of each run, Pallas kernels for 0% -> 2%
where the time goes in v1:
time: 198 us; the launch traced here: 197 us
  waiting for transfers between devices  79.2 us (40%)
  starting transfers between devices  50.4 us (25%)
  matrix products  22.1 us (11%)
  local copies, waits for them, and re-layouts  20.6 us (10%)
  other arithmetic  8.66 us (4%)
  Pallas kernels  8.5 us (4%)
  between operations  7.6 us (4%)
    ppermute x39, waiting for transfers between devices, swap(): return lax.ppermute(value, 'dp', [(i, i ^ 1 << bit) for i in range(n)])  76.3 us
    ppermute x39, starting transfers between devices, swap(): return lax.ppermute(value, 'dp', [(i, i ^ 1 << bit) for i in range(n)])  46.1 us
    dot_general x4, matrix products, dot_t(): lax.dot_general(a, g, (((0,), (0,)), ((), ())), preferred_element_type=F32)  13.2 us
    unnamed x16, local copies, waits for them, and re-layouts  12.4 us
    dot_general x8, matrix products, dot(): lax.dot_general(a, w, (((1,), (0,)), ((), ())), preferred_element_type=F32)  8.96 us
    pallas_call x2, Pallas kernels, pick_blocks(): pl.pallas_call(kernel, out_shape=jax.ShapeDtypeStruct((activations.shape[...  8.5 us
    slice x1, local copies, waits for them, and re-layouts, local(): grads_out = [grad_out[:, s, :] for s in range(kinds)]  4.61 us
    ppermute x2, starting transfers between devices, total(): lax.ppermute(value, 'tensor', [(i, i ^ 1 << bit) for i in range(t)])  4.37 us
  transfers between devices with their start and end apart: 41, of which 24 were waited for; matrix products, arithmetic and copies ran while one was open for 21% of the time, Pallas kernels for 2%

profile of v1, /device:TPU:0, one launch (start us, length us, event | category | flops | bytes accessed | tf_op | source)
XLA Modules:
  0.0 197.1 jit_solution(8640557124612888875)
XLA Ops:
  1.2 4.2 %shard_map.101 = bf16[768,2048]{1,0:T(8,128)(2,1)} custom-call(s32[8]{0:T(128)} %stack.206.places, bf16[768,4096]{1,0:T(8,128)(2,1)} %src.2), custom_call_target="tpu_custom_call" | custom-call | tf_op jit(solution)/shard_map/pallas_call | solution.py:39
  6.0 4.6 %fusion.56 = (bf16[768,1,512]{2,1,0:T(2,128)(2,1)S(1)}, bf16[768,1,512]{2,1,0:T(2,128)(2,1)S(1)}) fusion(bf16[768,2,512]{2,1,0:T(2,128)(2,1)} %param.7), kind=kLoop, calls=%fused_computation.131 | loop fusion | bytes 3145728 | tf_op jit(solution)/shard_map/slice | solution.py:85
  14.7 4.3 %shard_map.102 = bf16[768,2048]{1,0:T(8,128)(2,1)} custom-call(s32[8]{0:T(128)} %stack.197.places, bf16[768,4096]{1,0:T(8,128)(2,1)} %src.2), custom_call_target="tpu_custom_call" | custom-call | tf_op jit(solution)/shard_map/pallas_call | solution.py:39
  19.0 4.1 %fusion.58 = f32[2048,512]{1,0:T(8,128)S(1)} fusion(bf16[768,2048]{1,0:T(8,128)(2,1)} %shard_map.102, bf16[768,512]{1,0:T(8,128)(2,1)} %bitcast.202), kind=kOutput, calls=%fused_computation.133 | convolution fusion | flops 1610612736 | bytes 8126464 | tf_op jit(solution)/shard_map/dot_general | solution.py:69
  23.1 3.0 %fusion.59 = f32[2048,512]{1,0:T(8,128)S(1)} fusion(bf16[768,2048]{1,0:T(8,128)(2,1)S(1)} %copy-done.2, bf16[768,512]{1,0:T(8,128)(2,1)} %bitcast.201), kind=kOutput, calls=%fused_computation.134 | convolution fusion | flops 1610612736 | bytes 8126464 | tf_op jit(solution)/shard_map/dot_general | solution.py:69
  26.1 3.0 %convolution_add_fusion.1 = f32[2048,512]{1,0:T(8,128)S(1)} fusion(f32[2048,512]{1,0:T(8,128)S(1)} %fusion.58, bf16[768,2048]{1,0:T(8,128)(2,1)S(1)} %collective-permute-done, bf16[768,512]{1,0:T(8,128)(2,1)} %collective-permute-done.1), kind=kOutput, calls=%fused_computation.1 | convolution fusion | flops 1611661312 | bytes 12320768 | tf_op jit(solution)/shard_map/dot_general | solution.py:69
  29.6 2.6 %collective-permute-start.2 = (f16[2,2,256,256]{3,2,1,0:T(8,128)(2,1)S(1)}, f16[2,2,256,256]{3,2,1,0:T(8,128)(2,1)S(1)}, u32[]{:S(2)}, u32[]{:S(2)}) collective-permute-start(f16[2,2,256,256]{3,2,1,0:T(8,128)(2,1)S(1)} %bitcast.221), channel_id=1, source_target_pairs={{0,4},{2,6},{4,0},{6,2},{8,12},{10,14},{12,8},{14,10},{16,20},{18,... | collective-permute-start | bytes 1572872 | tf_op jit(solution)/shard_map/ppermute | solution.py:59
  32.5 1.6 collective-permute-start.5
  35.5 3.0 %convolution_add_fusion = f32[2048,512]{1,0:T(8,128)S(1)} fusion(f32[2048,512]{1,0:T(8,128)S(1)} %fusion.59, bf16[768,2048]{1,0:T(8,128)(2,1)S(1)} %collective-permute-done, bf16[768,512]{1,0:T(8,128)(2,1)} %collective-permute-done.13), kind=kOutput, calls=%fused_computation | convolution fusion | flops 1611661312 | bytes 12320768 | tf_op jit(solution)/shard_map/dot_general | solution.py:69
  40.9 3.9 %collective-permute-done.2 = f16[2,2,256,256]{3,2,1,0:T(8,128)(2,1)S(1)} collective-permute-done((f16[2,2,256,256]{3,2,1,0:T(8,128)(2,1)S(1)}, f16[2,2,256,256]{3,2,1,0:T(8,128)(2,1)S(1)}, u32[]{:S(2)}, u32[]{:S(2)}) %collective-permute-start.2) | collective-permute-done | bytes 524320 | tf_op jit(solution)/shard_map/ppermute | solution.py:59
  44.9 1.9 collective-permute-start.3
  47.0 1.6 collective-permute-start.6
  50.4 3.7 %collective-permute-done.3 = f16[2,256,256]{2,1,0:T(8,128)(2,1)S(1)} collective-permute-done((f16[2,256,256]{2,1,0:T(8,128)(2,1)S(1)}, f16[2,256,256]{2,1,0:T(8,128)(2,1)S(1)}, u32[]{:S(2)}, u32[]{:S(2)}) %collective-permute-start.3) | collective-permute-done | bytes 262176 | tf_op jit(solution)/shard_map/ppermute | solution.py:59
  54.3 2.9 %collective-permute-start.4 = (f16[256,256]{1,0:T(8,128)(2,1)S(1)}, f16[256,256]{1,0:T(8,128)(2,1)S(1)}, u32[]{:S(2)}, u32[]{:S(2)}) collective-permute-start(f16[256,256]{1,0:T(8,128)(2,1)S(1)} %fusion.38), channel_id=1, source_target_pairs={{0,16},{2,18},{4,20},{6,22},{8,24},{10,26},{12,28},{14,30},{16,0},... | collective-permute-start | bytes 393224 | tf_op jit(solution)/shard_map/ppermute | solution.py:59
  57.3 1.7 collective-permute-start.7
  59.0 8.5 %collective-permute-done.4 = f16[256,256]{1,0:T(8,128)(2,1)S(1)} collective-permute-done((f16[256,256]{1,0:T(8,128)(2,1)S(1)}, f16[256,256]{1,0:T(8,128)(2,1)S(1)}, u32[]{:S(2)}, u32[]{:S(2)}) %collective-permute-start.4) | collective-permute-done | bytes 131104 | tf_op jit(solution)/shard_map/ppermute | solution.py:59
  69.3 3.6 %collective-permute-start.15 = (f16[2,256,256]{2,1,0:T(8,128)(2,1)S(1)}, f16[2,256,256]{2,1,0:T(8,128)(2,1)S(1)}, u32[]{:S(2)}, u32[]{:S(2)}) collective-permute-start(f16[2,256,256]{2,1,0:T(8,128)(2,1)S(1)} %fusion.32), channel_id=1, source_target_pairs={{0,8},{2,10},{4,12},{6,14},{8,0},{10,2},{12,4},{14,6},{16,24},{18,... | collective-permute-start | bytes 786440 | tf_op jit(solution)/shard_map/ppermute | solution.py:59
  73.0 1.6 collective-permute-start.18
  74.6 3.6 %collective-permute-done.15 = f16[2,256,256]{2,1,0:T(8,128)(2,1)S(1)} collective-permute-done((f16[2,256,256]{2,1,0:T(8,128)(2,1)S(1)}, f16[2,256,256]{2,1,0:T(8,128)(2,1)S(1)}, u32[]{:S(2)}, u32[]{:S(2)}) %collective-permute-start.15) | collective-permute-done | bytes 262176 | tf_op jit(solution)/shard_map/ppermute | solution.py:59
  78.2 1.7 collective-permute-start.16
  81.4 8.1 %collective-permute-done.16 = f16[256,256]{1,0:T(8,128)(2,1)S(1)} collective-permute-done((f16[256,256]{1,0:T(8,128)(2,1)S(1)}, f16[256,256]{1,0:T(8,128)(2,1)S(1)}, u32[]{:S(2)}, u32[]{:S(2)}) %collective-permute-start.16) | collective-permute-done | bytes 131104 | tf_op jit(solution)/shard_map/ppermute | solution.py:59
  89.5 1.7 collective-permute-done.19
  93.4 2.9 %collective-permute-start.8 = (f32[3]{0:T(128)S(1)}, f32[3]{0:T(128)S(1)}, u32[]{:S(2)}, u32[]{:S(2)}) collective-permute-start(f32[3]{0:T(128)S(1)} %pad_maximum_fusion.20), channel_id=1, source_target_pairs={{0,16},{2,18},{4,20},{6,22},{8,24},{10,26},{12,28},{14,30},{16,0},... | collective-permute-start | bytes 44 | tf_op jit(solution)/shard_map/ppermute | solution.py:59
  100.0 2.3 %collective-permute-done.21 = f32[1]{0:T(128)} collective-permute-done((f32[1]{0:T(128)}, f32[1]{0:T(128)}, u32[]{:S(2)}, u32[]{:S(2)}) %collective-permute-start.21) | collective-permute-done | bytes 36 | tf_op jit(solution)/shard_map/ppermute | solution.py:59
  102.9 2.9 %collective-permute-start.22 = (f32[1]{0:T(128)}, f32[1]{0:T(128)}, u32[]{:S(2)}, u32[]{:S(2)}) collective-permute-start(f32[1]{0:T(128)} %add.177), channel_id=1, source_target_pairs={{0,4},{2,6},{4,0},{6,2},{8,12},{10,14},{12,8},{14,10},{16,20},{18,... | collective-permute-start | bytes 20 | tf_op jit(solution)/shard_map/ppermute | solution.py:59
  109.5 2.9 %collective-permute-start.24 = (f32[1]{0:T(128)}, f32[1]{0:T(128)}, u32[]{:S(2)}, u32[]{:S(2)}) collective-permute-start(f32[1]{0:T(128)} %add.179), channel_id=1, source_target_pairs={{0,1},{1,0},{2,3},{3,2},{4,5},{5,4},{6,7},{7,6},{8,9},{9,8},{10,11... | collective-permute-start | bytes 20 | tf_op jit(solution)/shard_map/ppermute | solution.py:65
  113.8 1.6 collective-permute-start.10
  115.4 2.0 %collective-permute-done.10 = f32[3]{0:T(128)S(1)} collective-permute-done((f32[3]{0:T(128)S(1)}, f32[3]{0:T(128)S(1)}, u32[]{:S(2)}, u32[]{:S(2)}) %collective-permute-start.10) | collective-permute-done | bytes 44 | tf_op jit(solution)/shard_map/ppermute | solution.py:59
  118.5 1.5 collective-permute-start.12
  120.0 2.0 %collective-permute-done.12 = f32[3]{0:T(128)S(1)} collective-permute-done((f32[3]{0:T(128)S(1)}, f32[3]{0:T(128)S(1)}, u32[]{:S(2)}, u32[]{:S(2)}) %collective-permute-start.12) | collective-permute-done | bytes 44 | tf_op jit(solution)/shard_map/ppermute | solution.py:65
  125.1 1.9 collective-permute-start.25
  128.2 1.9 collective-permute-start.33
  132.2 11.2 %collective-permute-done.25 = bf16[256,256]{1,0:T(8,128)(2,1)S(1)} collective-permute-done((bf16[256,256]{1,0:T(8,128)(2,1)S(1)}, bf16[256,256]{1,0:T(8,128)(2,1)S(1)}, u32[]{:S(2)}, u32[]{:S(2)}) %collective-permute-start.25) | collective-permute-done | bytes 131104 | tf_op jit(solution)/shard_map/ppermute | solution.py:59
  143.5 2.7 %collective-permute-done.29 = bf16[256,256]{1,0:T(8,128)(2,1)S(1)} collective-permute-done((bf16[256,256]{1,0:T(8,128)(2,1)S(1)}, bf16[256,256]{1,0:T(8,128)(2,1)S(1)}, u32[]{:S(2)}, u32[]{:S(2)}) %collective-permute-start.29) | collective-permute-done | bytes 131104 | tf_op jit(solution)/shard_map/ppermute | solution.py:59
  146.2 1.6 collective-permute-start.30
  150.4 1.6 collective-permute-start.38
  152.0 4.0 %collective-permute-done.26 = bf16[2,256,256]{2,1,0:T(8,128)(2,1)S(1)} collective-permute-done((bf16[2,256,256]{2,1,0:T(8,128)(2,1)S(1)}, bf16[2,256,256]{2,1,0:T(8,128)(2,1)S(1)}, u32[]{:S(2)}, u32[]{:S(2)}) %collective-permute-start.26) | collective-permute-done | bytes 262176 | tf_op jit(solution)/shard_map/ppermute | solution.py:59
  156.1 1.6 collective-permute-start.27
  157.8 3.8 %collective-permute-done.34 = bf16[2,256,256]{2,1,0:T(8,128)(2,1)S(1)} collective-permute-done((bf16[2,256,256]{2,1,0:T(8,128)(2,1)S(1)}, bf16[2,256,256]{2,1,0:T(8,128)(2,1)S(1)}, u32[]{:S(2)}, u32[]{:S(2)}) %collective-permute-start.34) | collective-permute-done | bytes 262176 | tf_op jit(solution)/shard_map/ppermute | solution.py:59
  161.7 1.6 collective-permute-start.35
  163.3 1.8 copy.50
  165.1 1.8 copy.48
  166.9 1.8 copy.49
  169.4 1.6 collective-permute-done.27
  171.2 1.7 collective-permute-done.31
  173.1 7.7 %collective-permute-done.35 = bf16[2,2,256,256]{3,2,1,0:T(8,128)(2,1)S(1)} collective-permute-done((bf16[2,2,256,256]{3,2,1,0:T(8,128)(2,1)S(1)}, bf16[2,2,256,256]{3,2,1,0:T(8,128)(2,1)S(1)}, u32[]{:S(2)}, u32[]{:S(2)}) %collective-permute-start.35) | collective-permute-done | bytes 524320 | tf_op jit(solution)/shard_map/ppermute | solution.py:59
  181.0 2.8 %collective-permute-done.39 = bf16[2,2,256,256]{3,2,1,0:T(8,128)(2,1)S(1)} collective-permute-done((bf16[2,2,256,256]{3,2,1,0:T(8,128)(2,1)S(1)}, bf16[2,2,256,256]{3,2,1,0:T(8,128)(2,1)S(1)}, u32[]{:S(2)}, u32[]{:S(2)}) %collective-permute-start.39) | collective-permute-done | bytes 524320 | tf_op jit(solution)/shard_map/ppermute | solution.py:59
  194.0 3.0 %copy.51 = bf16[768,2,512]{2,1,0:T(2,128)(2,1)} copy(bf16[768,2,512]{0,2,1:T(8,128)(2,1)S(1)} %bitcast.205) | data formatting | bytes 3145728
  (129 shorter events, 42.4 us)
Async XLA Ops:
  5.4 20.6 %collective-permute-start = (bf16[768,2048]{1,0:T(8,128)(2,1)}, bf16[768,2048]{1,0:T(8,128)(2,1)S(1)}, u32[]{:S(2)}, u32[]{:S(2)}) collective-permute-start(bf16[768,2048]{1,0:T(8,128)(2,1)} %shard_map.101), channel_id=1, source_target_pairs={{0,2},{2,0},{4,6},{6,4},{8,10},{10,8},{12,14},{14,12},{16,18},{18,... | collective-permute-start | bytes 9437192 | tf_op jit(solution)/shard_map/ppermute | solution.py:59
  11.7 14.4 %collective-permute-start.1 = (bf16[768,512]{1,0:T(8,128)(2,1)}, bf16[768,512]{1,0:T(8,128)(2,1)}, u32[]{:S(2)}, u32[]{:S(2)}) collective-permute-start(bf16[768,512]{1,0:T(8,128)(2,1)} %bitcast.202), channel_id=1, source_target_pairs={{0,2},{2,0},{4,6},{6,4},{8,10},{10,8},{12,14},{14,12},{16,18},{18,... | collective-permute-start | bytes 2359304 | tf_op jit(solution)/shard_map/ppermute | solution.py:59
  12.8 22.7 %collective-permute-start.13 = (bf16[768,512]{1,0:T(8,128)(2,1)}, bf16[768,512]{1,0:T(8,128)(2,1)}, u32[]{:S(2)}, u32[]{:S(2)}) collective-permute-start(bf16[768,512]{1,0:T(8,128)(2,1)} %bitcast.201), channel_id=1, source_target_pairs={{0,2},{2,0},{4,6},{6,4},{8,10},{10,8},{12,14},{14,12},{16,18},{18,... | collective-permute-start | bytes 2359304 | tf_op jit(solution)/shard_map/ppermute | solution.py:59
  18.9 4.1 %copy-start.2 = (bf16[768,2048]{1,0:T(8,128)(2,1)S(1)}, bf16[768,2048]{1,0:T(8,128)(2,1)}, u32[]{:S(2)}) copy-start(bf16[768,2048]{1,0:T(8,128)(2,1)} %shard_map.102) | copy-start | bytes 9437188
  29.6 4.6 %copy-start = (f32[256,2,512]{2,1,0:T(2,128)S(1)}, f32[256,2,512]{2,1,0:T(2,128)}, u32[]{:S(2)}) copy-start(f32[256,2,512]{2,1,0:T(2,128)} %param.8) | copy-start | bytes 3145732
  29.6 15.2 %collective-permute-start.2 = (f16[2,2,256,256]{3,2,1,0:T(8,128)(2,1)S(1)}, f16[2,2,256,256]{3,2,1,0:T(8,128)(2,1)S(1)}, u32[]{:S(2)}, u32[]{:S(2)}) collective-permute-start(f16[2,2,256,256]{3,2,1,0:T(8,128)(2,1)S(1)} %bitcast.221), channel_id=1, source_target_pairs={{0,4},{2,6},{4,0},{6,2},{8,12},{10,14},{12,8},{14,10},{16,20},{18,... | collective-permute-start | bytes 1572872 | tf_op jit(solution)/shard_map/ppermute | solution.py:59
  32.5 14.3 %collective-permute-start.5 = (f16[2,2,256,256]{3,2,1,0:T(8,128)(2,1)S(1)}, f16[2,2,256,256]{3,2,1,0:T(8,128)(2,1)S(1)}, u32[]{:S(2)}, u32[]{:S(2)}) collective-permute-start(f16[2,2,256,256]{3,2,1,0:T(8,128)(2,1)S(1)} %fusion.20), channel_id=1, source_target_pairs={{0,8},{2,10},{4,12},{6,14},{8,0},{10,2},{12,4},{14,6},{16,24},{18,... | collective-permute-start | bytes 1572872 | tf_op jit(solution)/shard_map/ppermute | solution.py:59
  38.8 1.2 copy-start.3
  38.9 1.5 copy-start.4
  44.9 9.2 %collective-permute-start.3 = (f16[2,256,256]{2,1,0:T(8,128)(2,1)S(1)}, f16[2,256,256]{2,1,0:T(8,128)(2,1)S(1)}, u32[]{:S(2)}, u32[]{:S(2)}) collective-permute-start(f16[2,256,256]{2,1,0:T(8,128)(2,1)S(1)} %fusion.30), channel_id=1, source_target_pairs={{0,8},{2,10},{4,12},{6,14},{8,0},{10,2},{12,4},{14,6},{16,24},{18,... | collective-permute-start | bytes 786440 | tf_op jit(solution)/shard_map/ppermute | solution.py:59
  47.0 10.2 %collective-permute-start.6 = (f16[2,256,256]{2,1,0:T(8,128)(2,1)S(1)}, f16[2,256,256]{2,1,0:T(8,128)(2,1)S(1)}, u32[]{:S(2)}, u32[]{:S(2)}) collective-permute-start(f16[2,256,256]{2,1,0:T(8,128)(2,1)S(1)} %fusion.31), channel_id=1, source_target_pairs={{0,4},{2,6},{4,0},{6,2},{8,12},{10,14},{12,8},{14,10},{16,20},{18,... | collective-permute-start | bytes 786440 | tf_op jit(solution)/shard_map/ppermute | solution.py:59
  48.5 20.6 %collective-permute-start.14 = (f16[2,2,256,256]{3,2,1,0:T(8,128)(2,1)S(1)}, f16[2,2,256,256]{3,2,1,0:T(8,128)(2,1)S(1)}, u32[]{:S(2)}, u32[]{:S(2)}) collective-permute-start(f16[2,2,256,256]{3,2,1,0:T(8,128)(2,1)S(1)} %bitcast.220), channel_id=1, source_target_pairs={{0,4},{2,6},{4,0},{6,2},{8,12},{10,14},{12,8},{14,10},{16,20},{18,... | collective-permute-start | bytes 1572872 | tf_op jit(solution)/shard_map/ppermute | solution.py:59
  49.1 23.8 %collective-permute-start.17 = (f16[2,2,256,256]{3,2,1,0:T(8,128)(2,1)S(1)}, f16[2,2,256,256]{3,2,1,0:T(8,128)(2,1)S(1)}, u32[]{:S(2)}, u32[]{:S(2)}) collective-permute-start(f16[2,2,256,256]{3,2,1,0:T(8,128)(2,1)S(1)} %fusion.21), channel_id=1, source_target_pairs={{0,8},{2,10},{4,12},{6,14},{8,0},{10,2},{12,4},{14,6},{16,24},{18,... | collective-permute-start | bytes 1572872 | tf_op jit(solution)/shard_map/ppermute | solution.py:59
  54.3 13.3 %collective-permute-start.4 = (f16[256,256]{1,0:T(8,128)(2,1)S(1)}, f16[256,256]{1,0:T(8,128)(2,1)S(1)}, u32[]{:S(2)}, u32[]{:S(2)}) collective-permute-start(f16[256,256]{1,0:T(8,128)(2,1)S(1)} %fusion.38), channel_id=1, source_target_pairs={{0,16},{2,18},{4,20},{6,22},{8,24},{10,26},{12,28},{14,30},{16,0},... | collective-permute-start | bytes 393224 | tf_op jit(solution)/shard_map/ppermute | solution.py:59
  57.3 11.8 %collective-permute-start.7 = (f16[256,256]{1,0:T(8,128)(2,1)S(1)}, f16[256,256]{1,0:T(8,128)(2,1)S(1)}, u32[]{:S(2)}, u32[]{:S(2)}) collective-permute-start(f16[256,256]{1,0:T(8,128)(2,1)S(1)} %fusion.39), channel_id=1, source_target_pairs={{0,16},{2,18},{4,20},{6,22},{8,24},{10,26},{12,28},{14,30},{16,0},... | collective-permute-start | bytes 393224 | tf_op jit(solution)/shard_map/ppermute | solution.py:59
  69.3 8.9 %collective-permute-start.15 = (f16[2,256,256]{2,1,0:T(8,128)(2,1)S(1)}, f16[2,256,256]{2,1,0:T(8,128)(2,1)S(1)}, u32[]{:S(2)}, u32[]{:S(2)}) collective-permute-start(f16[2,256,256]{2,1,0:T(8,128)(2,1)S(1)} %fusion.32), channel_id=1, source_target_pairs={{0,8},{2,10},{4,12},{6,14},{8,0},{10,2},{12,4},{14,6},{16,24},{18,... | collective-permute-start | bytes 786440 | tf_op jit(solution)/shard_map/ppermute | solution.py:59
  73.0 6.9 %collective-permute-start.18 = (f16[2,256,256]{2,1,0:T(8,128)(2,1)S(1)}, f16[2,256,256]{2,1,0:T(8,128)(2,1)S(1)}, u32[]{:S(2)}, u32[]{:S(2)}) collective-permute-start(f16[2,256,256]{2,1,0:T(8,128)(2,1)S(1)} %fusion.33), channel_id=1, source_target_pairs={{0,4},{2,6},{4,0},{6,2},{8,12},{10,14},{12,8},{14,10},{16,20},{18,... | collective-permute-start | bytes 786440 | tf_op jit(solution)/shard_map/ppermute | solution.py:59
  78.2 11.2 %collective-permute-start.16 = (f16[256,256]{1,0:T(8,128)(2,1)S(1)}, f16[256,256]{1,0:T(8,128)(2,1)S(1)}, u32[]{:S(2)}, u32[]{:S(2)}) collective-permute-start(f16[256,256]{1,0:T(8,128)(2,1)S(1)} %fusion.40), channel_id=1, source_target_pairs={{0,16},{2,18},{4,20},{6,22},{8,24},{10,26},{12,28},{14,30},{16,0},... | collective-permute-start | bytes 393224 | tf_op jit(solution)/shard_map/ppermute | solution.py:59
  80.0 11.2 %collective-permute-start.19 = (f16[256,256]{1,0:T(8,128)(2,1)S(1)}, f16[256,256]{1,0:T(8,128)(2,1)S(1)}, u32[]{:S(2)}, u32[]{:S(2)}) collective-permute-start(f16[256,256]{1,0:T(8,128)(2,1)S(1)} %fusion.41), channel_id=1, source_target_pairs={{0,16},{2,18},{4,20},{6,22},{8,24},{10,26},{12,28},{14,30},{16,0},... | collective-permute-start | bytes 393224 | tf_op jit(solution)/shard_map/ppermute | solution.py:59
  92.7 4.7 %collective-permute-start.20 = (f32[1]{0:T(128)}, f32[1]{0:T(128)}, u32[]{:S(2)}, u32[]{:S(2)}) collective-permute-start(f32[1]{0:T(128)} %bitcast.56), channel_id=1, source_target_pairs={{0,16},{2,18},{4,20},{6,22},{8,24},{10,26},{12,28},{14,30},{16,0},... | collective-permute-start | bytes 20 | tf_op jit(solution)/shard_map/ppermute | solution.py:59
  93.4 14.7 %collective-permute-start.8 = (f32[3]{0:T(128)S(1)}, f32[3]{0:T(128)S(1)}, u32[]{:S(2)}, u32[]{:S(2)}) collective-permute-start(f32[3]{0:T(128)S(1)} %pad_maximum_fusion.20), channel_id=1, source_target_pairs={{0,16},{2,18},{4,20},{6,22},{8,24},{10,26},{12,28},{14,30},{16,0},... | collective-permute-start | bytes 44 | tf_op jit(solution)/shard_map/ppermute | solution.py:59
  98.6 3.7 %collective-permute-start.21 = (f32[1]{0:T(128)}, f32[1]{0:T(128)}, u32[]{:S(2)}, u32[]{:S(2)}) collective-permute-start(f32[1]{0:T(128)} %add.176), channel_id=1, source_target_pairs={{0,8},{2,10},{4,12},{6,14},{8,0},{10,2},{12,4},{14,6},{16,24},{18,... | collective-permute-start | bytes 20 | tf_op jit(solution)/shard_map/ppermute | solution.py:59
  102.9 3.7 %collective-permute-start.22 = (f32[1]{0:T(128)}, f32[1]{0:T(128)}, u32[]{:S(2)}, u32[]{:S(2)}) collective-permute-start(f32[1]{0:T(128)} %add.177), channel_id=1, source_target_pairs={{0,4},{2,6},{4,0},{6,2},{8,12},{10,14},{12,8},{14,10},{16,20},{18,... | collective-permute-start | bytes 20 | tf_op jit(solution)/shard_map/ppermute | solution.py:59
  107.1 1.8 collective-permute-start.23
  108.9 4.9 %collective-permute-start.9 = (f32[3]{0:T(128)S(1)}, f32[3]{0:T(128)S(1)}, u32[]{:S(2)}, u32[]{:S(2)}) collective-permute-start(f32[3]{0:T(128)S(1)} %fusion.88), channel_id=1, source_target_pairs={{0,8},{2,10},{4,12},{6,14},{8,0},{10,2},{12,4},{14,6},{16,24},{18,... | collective-permute-start | bytes 44 | tf_op jit(solution)/shard_map/ppermute | solution.py:59
  109.5 3.7 %collective-permute-start.24 = (f32[1]{0:T(128)}, f32[1]{0:T(128)}, u32[]{:S(2)}, u32[]{:S(2)}) collective-permute-start(f32[1]{0:T(128)} %add.179), channel_id=1, source_target_pairs={{0,1},{1,0},{2,3},{3,2},{4,5},{5,4},{6,7},{7,6},{8,9},{9,8},{10,11... | collective-permute-start | bytes 20 | tf_op jit(solution)/shard_map/ppermute | solution.py:65
  113.8 3.6 %collective-permute-start.10 = (f32[3]{0:T(128)S(1)}, f32[3]{0:T(128)S(1)}, u32[]{:S(2)}, u32[]{:S(2)}) collective-permute-start(f32[3]{0:T(128)S(1)} %add.156), channel_id=1, source_target_pairs={{0,4},{2,6},{4,0},{6,2},{8,12},{10,14},{12,8},{14,10},{16,20},{18,... | collective-permute-start | bytes 44 | tf_op jit(solution)/shard_map/ppermute | solution.py:59
  117.4 1.1 collective-permute-start.11
  118.5 3.5 %collective-permute-start.12 = (f32[3]{0:T(128)S(1)}, f32[3]{0:T(128)S(1)}, u32[]{:S(2)}, u32[]{:S(2)}) collective-permute-start(f32[3]{0:T(128)S(1)} %add.158), channel_id=1, source_target_pairs={{0,1},{1,0},{2,3},{3,2},{4,5},{5,4},{6,7},{7,6},{8,9},{9,8},{10,11... | collective-permute-start | bytes 44 | tf_op jit(solution)/shard_map/ppermute | solution.py:65
  125.1 18.2 %collective-permute-start.25 = (bf16[256,256]{1,0:T(8,128)(2,1)S(1)}, bf16[256,256]{1,0:T(8,128)(2,1)S(1)}, u32[]{:S(2)}, u32[]{:S(2)}) collective-permute-start(bf16[256,256]{1,0:T(8,128)(2,1)S(1)} %get-tuple-element.75), channel_id=1, source_target_pairs={{0,16},{2,18},{4,20},{6,22},{8,24},{10,26},{12,28},{14,30},{16,0},... | collective-permute-start | bytes 393224 | tf_op jit(solution)/shard_map/ppermute | solution.py:59
  127.1 19.1 %collective-permute-start.29 = (bf16[256,256]{1,0:T(8,128)(2,1)S(1)}, bf16[256,256]{1,0:T(8,128)(2,1)S(1)}, u32[]{:S(2)}, u32[]{:S(2)}) collective-permute-start(bf16[256,256]{1,0:T(8,128)(2,1)S(1)} %get-tuple-element.74), channel_id=1, source_target_pairs={{0,16},{2,18},{4,20},{6,22},{8,24},{10,26},{12,28},{14,30},{16,0},... | collective-permute-start | bytes 393224 | tf_op jit(solution)/shard_map/ppermute | solution.py:59
  128.2 20.8 %collective-permute-start.33 = (bf16[256,256]{1,0:T(8,128)(2,1)S(1)}, bf16[256,256]{1,0:T(8,128)(2,1)S(1)}, u32[]{:S(2)}, u32[]{:S(2)}) collective-permute-start(bf16[256,256]{1,0:T(8,128)(2,1)S(1)} %get-tuple-element.83), channel_id=1, source_target_pairs={{0,16},{2,18},{4,20},{6,22},{8,24},{10,26},{12,28},{14,30},{16,0},... | collective-permute-start | bytes 393224 | tf_op jit(solution)/shard_map/ppermute | solution.py:59
  130.1 20.3 %collective-permute-start.37 = (bf16[256,256]{1,0:T(8,128)(2,1)S(1)}, bf16[256,256]{1,0:T(8,128)(2,1)S(1)}, u32[]{:S(2)}, u32[]{:S(2)}) collective-permute-start(bf16[256,256]{1,0:T(8,128)(2,1)S(1)} %get-tuple-element.82), channel_id=1, source_target_pairs={{0,16},{2,18},{4,20},{6,22},{8,24},{10,26},{12,28},{14,30},{16,0},... | collective-permute-start | bytes 393224 | tf_op jit(solution)/shard_map/ppermute | solution.py:59
  143.4 12.6 %collective-permute-start.26 = (bf16[2,256,256]{2,1,0:T(8,128)(2,1)S(1)}, bf16[2,256,256]{2,1,0:T(8,128)(2,1)S(1)}, u32[]{:S(2)}, u32[]{:S(2)}) collective-permute-start(bf16[2,256,256]{2,1,0:T(8,128)(2,1)S(1)} %get-tuple-element.71), channel_id=1, source_target_pairs={{0,8},{2,10},{4,12},{6,14},{8,0},{10,2},{12,4},{14,6},{16,24},{18,... | collective-permute-start | bytes 786440 | tf_op jit(solution)/shard_map/ppermute | solution.py:59
  146.2 11.4 %collective-permute-start.30 = (bf16[2,256,256]{2,1,0:T(8,128)(2,1)S(1)}, bf16[2,256,256]{2,1,0:T(8,128)(2,1)S(1)}, u32[]{:S(2)}, u32[]{:S(2)}) collective-permute-start(bf16[2,256,256]{2,1,0:T(8,128)(2,1)S(1)} %get-tuple-element.77), channel_id=1, source_target_pairs={{0,4},{2,6},{4,0},{6,2},{8,12},{10,14},{12,8},{14,10},{16,20},{18,... | collective-permute-start | bytes 786440 | tf_op jit(solution)/shard_map/ppermute | solution.py:59
  149.0 12.6 %collective-permute-start.34 = (bf16[2,256,256]{2,1,0:T(8,128)(2,1)S(1)}, bf16[2,256,256]{2,1,0:T(8,128)(2,1)S(1)}, u32[]{:S(2)}, u32[]{:S(2)}) collective-permute-start(bf16[2,256,256]{2,1,0:T(8,128)(2,1)S(1)} %get-tuple-element.79), channel_id=1, source_target_pairs={{0,8},{2,10},{4,12},{6,14},{8,0},{10,2},{12,4},{14,6},{16,24},{18,... | collective-permute-start | bytes 786440 | tf_op jit(solution)/shard_map/ppermute | solution.py:59
  150.4 18.2 %collective-permute-start.38 = (bf16[2,256,256]{2,1,0:T(8,128)(2,1)S(1)}, bf16[2,256,256]{2,1,0:T(8,128)(2,1)S(1)}, u32[]{:S(2)}, u32[]{:S(2)}) collective-permute-start(bf16[2,256,256]{2,1,0:T(8,128)(2,1)S(1)} %get-tuple-element.85), channel_id=1, source_target_pairs={{0,4},{2,6},{4,0},{6,2},{8,12},{10,14},{12,8},{14,10},{16,20},{18,... | collective-permute-start | bytes 786440 | tf_op jit(solution)/shard_map/ppermute | solution.py:59
  156.1 14.9 %collective-permute-start.27 = (bf16[2,2,256,256]{3,2,1,0:T(8,128)(2,1)S(1)}, bf16[2,2,256,256]{3,2,1,0:T(8,128)(2,1)S(1)}, u32[]{:S(2)}, u32[]{:S(2)}) collective-permute-start(bf16[2,2,256,256]{3,2,1,0:T(8,128)(2,1)S(1)} %get-tuple-element.63), channel_id=1, source_target_pairs={{0,4},{2,6},{4,0},{6,2},{8,12},{10,14},{12,8},{14,10},{16,20},{18,... | collective-permute-start | bytes 1572872 | tf_op jit(solution)/shard_map/ppermute | solution.py:59
  157.7 15.1 %collective-permute-start.31 = (bf16[2,2,256,256]{3,2,1,0:T(8,128)(2,1)S(1)}, bf16[2,2,256,256]{3,2,1,0:T(8,128)(2,1)S(1)}, u32[]{:S(2)}, u32[]{:S(2)}) collective-permute-start(bf16[2,2,256,256]{3,2,1,0:T(8,128)(2,1)S(1)} %get-tuple-element.65), channel_id=1, source_target_pairs={{0,8},{2,10},{4,12},{6,14},{8,0},{10,2},{12,4},{14,6},{16,24},{18,... | collective-permute-start | bytes 1572872 | tf_op jit(solution)/shard_map/ppermute | solution.py:59
  161.7 19.1 %collective-permute-start.35 = (bf16[2,2,256,256]{3,2,1,0:T(8,128)(2,1)S(1)}, bf16[2,2,256,256]{3,2,1,0:T(8,128)(2,1)S(1)}, u32[]{:S(2)}, u32[]{:S(2)}) collective-permute-start(bf16[2,2,256,256]{3,2,1,0:T(8,128)(2,1)S(1)} %get-tuple-element.67), channel_id=1, source_target_pairs={{0,4},{2,6},{4,0},{6,2},{8,12},{10,14},{12,8},{14,10},{16,20},{18,... | collective-permute-start | bytes 1572872 | tf_op jit(solution)/shard_map/ppermute | solution.py:59
  168.7 15.1 %collective-permute-start.39 = (bf16[2,2,256,256]{3,2,1,0:T(8,128)(2,1)S(1)}, bf16[2,2,256,256]{3,2,1,0:T(8,128)(2,1)S(1)}, u32[]{:S(2)}, u32[]{:S(2)}) collective-permute-start(bf16[2,2,256,256]{3,2,1,0:T(8,128)(2,1)S(1)} %get-tuple-element.69), channel_id=1, source_target_pairs={{0,8},{2,10},{4,12},{6,14},{8,0},{10,2},{12,4},{14,6},{16,24},{18,... | collective-permute-start | bytes 1572872 | tf_op jit(solution)/shard_map/ppermute | solution.py:59
  171.1 15.2 %collective-permute-start.28 = (bf16[2048,256]{1,0:T(8,128)(2,1)S(1)}, bf16[2048,256]{1,0:T(8,128)(2,1)S(1)}, u32[]{:S(2)}, u32[]{:S(2)}) collective-permute-start(bf16[2048,256]{1,0:T(8,128)(2,1)S(1)} %bitcast.212), channel_id=1, source_target_pairs={{0,2},{2,0},{4,6},{6,4},{8,10},{10,8},{12,14},{14,12},{16,18},{18,... | collective-permute-start | bytes 3145736 | tf_op jit(solution)/shard_map/ppermute | solution.py:59
  173.0 18.7 %collective-permute-start.32 = (bf16[2048,256]{1,0:T(8,128)(2,1)S(1)}, bf16[2048,256]{1,0:T(8,128)(2,1)S(1)}, u32[]{:S(2)}, u32[]{:S(2)}) collective-permute-start(bf16[2048,256]{1,0:T(8,128)(2,1)S(1)} %bitcast.214), channel_id=1, source_target_pairs={{0,2},{2,0},{4,6},{6,4},{8,10},{10,8},{12,14},{14,12},{16,18},{18,... | collective-permute-start | bytes 3145736 | tf_op jit(solution)/shard_map/ppermute | solution.py:59
  180.9 8.6 %collective-permute-start.36 = (bf16[2048,256]{1,0:T(8,128)(2,1)S(1)}, bf16[2048,256]{1,0:T(8,128)(2,1)S(1)}, u32[]{:S(2)}, u32[]{:S(2)}) collective-permute-start(bf16[2048,256]{1,0:T(8,128)(2,1)S(1)} %bitcast.216), channel_id=1, source_target_pairs={{0,2},{2,0},{4,6},{6,4},{8,10},{10,8},{12,14},{14,12},{16,18},{18,... | collective-permute-start | bytes 3145736 | tf_op jit(solution)/shard_map/ppermute | solution.py:59
  184.0 8.8 %collective-permute-start.40 = (bf16[2048,256]{1,0:T(8,128)(2,1)S(1)}, bf16[2048,256]{1,0:T(8,128)(2,1)S(1)}, u32[]{:S(2)}, u32[]{:S(2)}) collective-permute-start(bf16[2048,256]{1,0:T(8,128)(2,1)S(1)} %bitcast.218), channel_id=1, source_target_pairs={{0,2},{2,0},{4,6},{6,4},{8,10},{10,8},{12,14},{14,12},{16,18},{18,... | collective-permute-start | bytes 3145736 | tf_op jit(solution)/shard_map/ppermute | solution.py:59
  185.2 1.9 copy-start.1

commit v2 on v0

v2 whole, which is shorter than its diff:
```python
import math

import jax
import jax.numpy as jnp
from jax import lax
from jax.experimental import pallas as pl
from jax.experimental.layout import Layout, with_layout_constraint
from jax.experimental.pallas import tpu as pltpu
from jax.sharding import PartitionSpec as P

F32 = jnp.float32
LANES = 128
CHUNKS = ((0, 0, 0), (0, 1, 1), (1, 0, 0), (1, 1, 1))


def sums_plan(deep):
    plan = [("P", 0, 0), ("S", 0, 0), ("S", 1, 0), ("P", 1, 0), ("S", 2, 0), ("S", 3, 0)]
    return plan + [("T", i, depth) for depth in range(deep) for i in range(len(CHUNKS))]


def gathers_plan(deep):
    last = deep - 1
    plan = [("G", 0, 0), ("G", 1, 0), ("J", 0, last), ("J", 1, last), ("G", 2, 0), ("G", 3, 0), ("O", 0, 0)]
    for depth in reversed(range(1, last)):
        plan += [("J", 0, depth), ("J", 1, depth), ("J", 2, depth + 1), ("J", 3, depth + 1)]
    plan += [("J", 2, 1), ("J", 3, 1)]
    for pair in ((0, 1), (2, 3)):
        plan += [("J", i, 0) for i in pair]
        plan += [(kind, i, 0) for i in pair for kind in "HK"]
    return plan


def after(value, *others):
    return lax.optimization_barrier((value, *others))[0]


def pick_blocks(activations, others, width):
    half = len(others) // 2
    me = lax.axis_index("dp")
    if width % LANES:
        return [
            jnp.concatenate(
                [lax.dynamic_slice_in_dim(activations, (me ^ j) * width, width, 1) for j in side], axis=1
            )
            for side in (others[:half], others[half:])
        ]
    tokens, count = activations.shape[0], len(others)

    def kernel(src, low, high, held, in_sems, out_sems):
        me = lax.axis_index("dp")
        copies = []
        for i, j in enumerate(others):
            place = held.at[:, pl.ds(i * width, width)]
            block = src.at[:, pl.ds(pl.multiple_of((me ^ j) * width, width), width)]
            dst = (low, high)[i // half].at[:, pl.ds(i % half * width, width)]
            copies.append(
                (
                    pltpu.make_async_copy(block, place, in_sems.at[i]),
                    pltpu.make_async_copy(place, dst, out_sems.at[i]),
                )
            )
        for fetch, _ in copies:
            fetch.start()
        for fetch, store in copies:
            fetch.wait()
            store.start()
        for _, store in copies:
            store.wait()

    return pl.pallas_call(
        kernel,
        out_shape=[jax.ShapeDtypeStruct((tokens, half * width), activations.dtype)] * 2,
        in_specs=[pl.BlockSpec(memory_space=pl.ANY)],
        out_specs=[pl.BlockSpec(memory_space=pl.ANY)] * 2,
        scratch_shapes=[
            pltpu.VMEM((tokens, count * width), activations.dtype),
            pltpu.SemaphoreType.DMA((count,)),
            pltpu.SemaphoreType.DMA((count,)),
        ],
        compiler_params=pltpu.CompilerParams(vmem_limit_bytes=16 * 2**20),
        cost_estimate=pl.CostEstimate(flops=0, bytes_accessed=0, transcendentals=0),
    )(activations)


def multiply(pairs, start=None, over_rows=False, dtype=F32):
    axis = 1 if over_rows else 0
    height, wide = pairs[0][0].shape[axis], pairs[0][1].shape[1]
    tile = math.gcd(height, 256)
    operands = [x for pair in pairs for x in pair] + ([] if start is None else [start])
    dims = (((1 - axis,), (0,)), ((), ()))

    def kernel(*refs):
        *ins, out = refs

        @pl.loop(0, height // tile)
        def _(i):
            here = pl.ds(pl.multiple_of(i * tile, tile), tile)
            value = sum(
                lax.dot_general(
                    a[:, here] if over_rows else a[here, :], b[...], dims, preferred_element_type=F32
                )
                for a, b in zip(ins[0 : 2 * len(pairs) : 2], ins[1 : 2 * len(pairs) : 2])
            )
            if start is not None:
                value = ins[-1][here, :] + value
            out[here, :] = value.astype(dtype)

    return pl.pallas_call(
        kernel,
        out_shape=jax.ShapeDtypeStruct((height, wide), dtype),
        in_specs=[pl.BlockSpec(memory_space=pltpu.VMEM)] * len(operands),
        out_specs=pl.BlockSpec(memory_space=pltpu.VMEM),
        compiler_params=pltpu.CompilerParams(vmem_limit_bytes=24 * 2**20),
        cost_estimate=pl.CostEstimate(flops=0, bytes_accessed=0, transcendentals=0),
    )(*operands)


def rows_first(value):
    return with_layout_constraint(value, Layout(major_to_minor=(0, 1, 2)))


def make_local(n, t):
    bits = n.bit_length() - 1
    links = list(range(1, bits))
    deep = len(links)
    orders = [links, [links[1], links[0], *links[2:]]]

    def blocks_of(order):
        return [
            sum(1 << bit for depth, bit in enumerate(order) if (place >> (deep - 1 - depth)) & 1)
            for place in range(n // 2)
        ]

    def swap(value, bit):
        return lax.ppermute(value, "dp", [(i, i ^ (1 << bit)) for i in range(n)])

    def total(value, fillers):
        hops = [("tensor", bit, t) for bit in range(t.bit_length() - 1)] + [("dp", bit, n) for bit in range(bits)]
        for i, (axis, bit, size) in enumerate(hops):
            other = lax.ppermute(value, axis, [(i, i ^ (1 << bit)) for i in range(size)])
            if i + len(fillers) >= len(hops):
                other = after(other, fillers[i - len(hops)])
            value = value + other
        return value

    def dot_t(a, g):
        return lax.dot_general(a, g, (((0,), (0,)), ((), ())), preferred_element_type=F32)

    def dot(a, w):
        return lax.dot_general(a, w, (((1,), (0,)), ((), ())), preferred_element_type=F32)

    def local(activations, grad_out, weights, first_moment, second_moment, step):
        rows, kinds, cols = weights.shape
        cut = cols // 2
        parts = [slice(0, cut), slice(cut, cols)]
        chunks = [(s, k) for s, k, _ in CHUNKS]
        plans = [plan for *_, plan in CHUNKS]
        amount = len(chunks)
        count = step[0].astype(F32)
        bias_one = 1.0 - jnp.exp(count * math.log(0.9))
        bias_two = 1.0 - jnp.exp(count * math.log(0.95))

        grad_out = lax.optimization_barrier(jnp.transpose(grad_out, (1, 0, 2)))
        shares = blocks_of(orders[0])
        sibling_out = [swap(grad_out[0], 0)]
        theirs = [pick_blocks(after(activations, grad_out), [j + 1 for j in shares], rows)]
        sibling = [swap(side, 0) for side in reversed(theirs[0])][::-1]
        mine = [pick_blocks(after(activations, *theirs[0]), shares, rows)]

        whole, held, got = {}, {}, {}
        last = [grad_out]

        def gated(value):
            return after(value, last[0])

        def product(s):
            if s:
                sibling_out.append(swap(gated(grad_out[s]), 0))
            for side in (1, 0):
                g = gated(grad_out[s])
                pairs = [(mine[0][side], g), (sibling[side], sibling_out[s])]
                if s:
                    whole[s, side] = multiply(pairs, over_rows=True)
                else:
                    whole[s, side] = sum(dot_t(*pair) for pair in pairs)
                last[0] = whole[s, side]

        def halve(i, depth):
            order = orders[plans[i]]
            if depth == 0:
                s, k = chunks[i]
                low, high = (whole[s, side][:, parts[k]] for side in (0, 1))
                if plans[i] == 0:
                    keep, out = low, high
                else:
                    keep, out = (
                        jnp.concatenate(
                            [x.reshape(2, -1, x.shape[1])[side] for x in (low, high)], axis=0
                        )
                        for side in (0, 1)
                    )
            else:
                keep, out = held[i].reshape(2, -1, held[i].shape[1])
            out = out.astype(jnp.float16)
            held[i] = keep
            got[i, depth] = swap(out, order[depth])
            last[0] = out

        def take(i, depth):
            held[i] = held[i] + gated(got[i, depth]).astype(F32)
            if depth + 1 < deep:
                halve(i, depth + 1)
            else:
                last[0] = held[i]

        for kind, i, depth in sums_plan(deep):
            if kind == "P":
                product(i)
            elif kind == "S":
                halve(i, 0)
            else:
                take(i, depth)
                if depth == 0 and i == 0:
                    weights, first_moment, second_moment = (
                        gated(x) for x in (weights, first_moment, second_moment)
                    )
                    theirs.append(pick_blocks(gated(activations), [j + 1 for j in blocks_of(orders[1])], rows))
                    last[0] = theirs[1][0]
                    mine.append(pick_blocks(gated(activations), blocks_of(orders[1]), rows))
                    last[0] = mine[1][0]

        states, sums = [], []
        for s in range(kinds):
            places = sorted((i for i in range(amount) if chunks[i][0] == s), key=lambda i: chunks[i])
            grad = jnp.concatenate([held[i] for i in places], axis=1)
            first = 0.9 * first_moment[:, s] + 0.1 * grad
            second = 0.95 * second_moment[:, s] + 0.05 * grad * grad
            update = first / bias_one / (jnp.sqrt(second / bias_two) + 1e-06) + 0.1 * weights[:, s]
            states.append((first, second, update))
            sums.append(jnp.sum(update * update, axis=0))
        firsts, seconds, updates = zip(*states)
        new_first, new_second = (rows_first(jnp.stack(x, axis=1)) for x in (firsts, seconds))
        weight_sq = jnp.sum(weights * weights, axis=0)
        sums = total(jnp.concatenate([jnp.stack(sums), weight_sq], axis=0), [new_first, new_second])
        sums = jnp.sum(sums, axis=1, keepdims=True)
        ratios = jnp.sqrt(sums[kinds:]) / (jnp.sqrt(sums[:kinds]) + 1e-06)
        scales = lax.optimization_barrier(jnp.broadcast_to(0.05 * ratios, (kinds, cols)))
        ratios = ratios[:, 0]
        news = [weights[:, s] - scales[s][None, :] * updates[s] for s in range(kinds)]
        halves = [fresh.astype(jnp.bfloat16) for fresh in news]
        new_weights = rows_first(jnp.stack(news, axis=1))

        gathered, arrived, sums_of, other, added = {}, {}, {}, {}, set()

        def spread(i, depth):
            arrived[i, depth] = swap(gathered[i], orders[plans[i]][depth])
            last[0] = gathered[i]

        for kind, i, depth in gathers_plan(deep):
            if kind == "G":
                s, k = chunks[i]
                gathered[i] = halves[s][:, parts[k]]
                spread(i, deep - 1)
            elif kind == "O":
                new_weights = gated(new_weights)
                last[0] = new_weights
            elif kind == "J":
                value = gated(arrived[i, depth])
                if depth:
                    gathered[i] = jnp.concatenate([gathered[i], value], axis=0)
                    spread(i, depth - 1)
                else:
                    arrived[i, 0] = value
                    other[i] = swap(jnp.concatenate([gathered[i], value], axis=0), 0)
                    last[0] = value
            elif kind == "H":
                sums_of[i] = multiply([(mine[plans[i]][0], gated(gathered[i]))])
                last[0] = sums_of[i]
            elif kind == "M":
                sums_of[i] = multiply([(mine[plans[i]][1], gated(arrived[i, 0]))], sums_of[i])
                last[0] = sums_of[i]
                added.add(i)
            else:
                pairs = [] if i in added else [(mine[plans[i]][1], arrived[i, 0])]
                sides = gated(other[i]).reshape(2, -1, other[i].shape[1])
                pairs += [(theirs[plans[i]][side], sides[side]) for side in (0, 1)]
                sums_of[i] = multiply(pairs, sums_of[i], dtype=jnp.bfloat16)
                last[0] = sums_of[i]
        places = sorted(range(amount), key=lambda i: chunks[i])
        new_kv = jnp.concatenate([sums_of[i] for i in places], axis=1)
        return (new_weights, new_first, new_second, ratios, new_kv.reshape(-1, kinds, cols))

    return local


def solution(mesh):
    in_specs = (
        P("dp", None),
        P("dp", None, "tensor"),
        P("dp", None, "tensor"),
        P("dp", None, "tensor"),
        P("dp", None, "tensor"),
        P(),
    )
    out_specs = (
        P("dp", None, "tensor"),
        P("dp", None, "tensor"),
        P("dp", None, "tensor"),
        P(),
        P("dp", None, "tensor"),
    )
    local = make_local(mesh.shape["dp"], mesh.shape["tensor"])
    return jax.shard_map(local, mesh=mesh, in_specs=in_specs, out_specs=out_specs, check_vma=False)
```

time: 346 us -> 167 us (0.48)
  waiting for transfers between devices: 245 us -> 80.2 us
  blocking collectives: 39.3 us -> 0 us
  starting transfers between devices: 0.08 us -> 39 us
  Pallas kernels: 0 us -> 21 us
  matrix products: 24.2 us -> 4.12 us
  between operations: 14.9 us -> 2.01 us
    reduce_scatter x1 -> x0, waiting for transfers between devices: 179 us -> none  [local(): lax.psum_scatter(jnp.einsum('td,tsc->dsc', columns, grad_out, preferred_e...]
    ppermute x0 -> x37, waiting for transfers between devices: none -> 80.2 us  [the longest x32 71.8 us: swap(): return lax.ppermute(value, 'dp', [(i, i ^ 1 << bit) for i in range(n)])]
    all_gather x1 -> x0, waiting for transfers between devices: 65.8 us -> none  [local(): lax.all_gather(half_weights, 'dp', axis=0, tiled=True)]
    psum x1 -> x0, blocking collectives: 39.3 us -> none  [local(): totals = lax.psum(partial_sq, ('dp', 'tensor'))]
    ppermute x0 -> x37, starting transfers between devices: none -> 39 us  [the longest x32 34.6 us: swap(): return lax.ppermute(value, 'dp', [(i, i ^ 1 << bit) for i in range(n)])]
    pallas_call x0 -> x14, Pallas kernels: none -> 21 us  [the longest x10 15.5 us: multiply(): pl.pallas_call(kernel, out_shape=jax.ShapeDtypeStruct((height, wide), dty...]
    dot_general x2 -> x4, matrix products: 24.2 us -> 4.12 us  [dot_t(): lax.dot_general(a, g, (((0,), (0,)), ((), ())), preferred_element_type=F32)]
    unnamed x8 -> x11, local copies, waits for them, and re-layouts: 13.8 us -> 4.98 us
  transfers between devices with their start and end apart: 2 -> 37, of which waited for: 2 -> 23; matrix products, arithmetic and copies ran while one was open for 3% -> 8% of each run, Pallas kernels for 0% -> 11%
where the time goes in v2:
time: 167 us
  waiting for transfers between devices  80.2 us (48%)
  starting transfers between devices  39 us (23%)
  Pallas kernels  21 us (13%)
  local copies, waits for them, and re-layouts  14.2 us (9%)
  other arithmetic  6.08 us (4%)
  matrix products  4.12 us (2%)
  between operations  2.01 us (1%)
    ppermute x32, waiting for transfers between devices, swap(): return lax.ppermute(value, 'dp', [(i, i ^ 1 << bit) for i in range(n)])  71.8 us
    ppermute x32, starting transfers between devices, swap(): return lax.ppermute(value, 'dp', [(i, i ^ 1 << bit) for i in range(n)])  34.6 us
    pallas_call x10, Pallas kernels, multiply(): pl.pallas_call(kernel, out_shape=jax.ShapeDtypeStruct((height, wide), dty...  15.5 us
    ppermute x5, waiting for transfers between devices, total(): other = lax.ppermute(value, axis, [(i, i ^ 1 << bit) for i in range(size)])  8.34 us
    pallas_call x4, Pallas kernels, pick_blocks(): pl.pallas_call(kernel, out_shape=[jax.ShapeDtypeStruct((tokens, half * wi...  5.45 us
    unnamed x11, local copies, waits for them, and re-layouts  4.98 us
    ppermute x5, starting transfers between devices, total(): other = lax.ppermute(value, axis, [(i, i ^ 1 << bit) for i in range(size)])  4.41 us
    dot_general x4, matrix products, dot_t(): lax.dot_general(a, g, (((0,), (0,)), ((), ())), preferred_element_type=F32)  4.12 us
  transfers between devices with their start and end apart: 37, of which 23 were waited for; matrix products, arithmetic and copies ran while one was open for 8% of the time, Pallas kernels for 11%

profile of v2, /device:TPU:0, one launch (start us, length us, event | category | flops | bytes accessed | tf_op | source)
XLA Modules:
  0.0 166.5 jit_solution(13130215810358353299)
XLA Ops:
  0.6 1.7 copy.32
  2.3 2.8 %copy-done = bf16[768,4096]{1,0:T(8,128)(2,1)S(1)} copy-done((bf16[768,4096]{1,0:T(8,128)(2,1)S(1)}, bf16[768,4096]{1,0:T(8,128)(2,1)}, u32[]{:S(2)}) %copy-start) | copy-done | bytes 6291480
  5.1 1.3 shard_map.101
  7.9 1.3 shard_map.102
  10.2 3.1 %collective-permute-done.1 = bf16[768,512]{1,0:T(8,128)(2,1)S(1)} collective-permute-done((bf16[768,512]{1,0:T(8,128)(2,1)S(1)}, bf16[768,512]{1,0:T(8,128)(2,1)S(1)}, u32[]{:S(2)}, u32[]{:S(2)}) %collective-permute-start.1) | collective-permute-done | bytes 786464 | tf_op jit(solution)/shard_map/ppermute | solution.py:135
  17.3 2.6 %collective-permute-start.3 = (f16[1024,256]{1,0:T(8,128)(2,1)S(1)}, f16[1024,256]{1,0:T(8,128)(2,1)S(1)}, u32[]{:S(2)}, u32[]{:S(2)}) collective-permute-start(f16[1024,256]{1,0:T(8,128)(2,1)S(1)} %slice.218), channel_id=1, source_target_pairs={{0,4},{2,6},{4,0},{6,2},{8,12},{10,14},{12,8},{14,10},{16,20},{18,... | collective-permute-start | bytes 1572872 | tf_op jit(solution)/shard_map/ppermute | solution.py:135
  20.6 1.7 %collective-permute-start.8 = (f16[1024,256]{1,0:T(8,128)(2,1)S(1)}, f16[1024,256]{1,0:T(8,128)(2,1)S(1)}, u32[]{:S(2)}, u32[]{:S(2)}) collective-permute-start(f16[1024,256]{1,0:T(8,128)(2,1)S(1)} %pad_maximum_fusion.8), channel_id=1, source_target_pairs={{0,8},{2,10},{4,12},{6,14},{8,0},{10,2},{12,4},{14,6},{16,24},{18,... | collective-permute-start | bytes 1572872 | tf_op jit(solution)/shard_map/ppermute | solution.py:135
  22.4 2.5 %shard_map.103 = f32[1024,512]{1,0:T(8,128)S(1)} custom-call(bf16[768,1024]{1,0:T(8,128)(2,1)S(1)} %get-tuple-element.64.refs_0_, bf16[768,512]{1,0:T(8,128)(2,1)S(1)} %get-tuple-element.68.refs_1_, bf16[768,1024]{1,0:T(8,128)(2,1)S(1)} %collective-permute-done.refs_2_, bf16[768,512]{1,0:T(8,128)(2,1)S(1)} %collective-permute-done.4.refs_3_), custom_call_target="tpu_custom_call" | custom-call | tf_op jit(solution)/shard_map/pallas_call | solution.py:108
  25.4 2.5 %shard_map.104 = f32[1024,512]{1,0:T(8,128)S(1)} custom-call(bf16[768,1024]{1,0:T(8,128)(2,1)S(1)} %get-tuple-element.63.refs_0_, bf16[768,512]{1,0:T(8,128)(2,1)S(1)} %get-tuple-element.68.refs_1_, bf16[768,1024]{1,0:T(8,128)(2,1)S(1)} %collective-permute-done.2.refs_2_, bf16[768,512]{1,0:T(8,128)(2,1)S(1)} %collective-permute-done.4.refs_3_), custom_call_target="tpu_custom_call" | custom-call | tf_op jit(solution)/shard_map/pallas_call | solution.py:108
  28.6 3.8 %collective-permute-done.3 = f16[1024,256]{1,0:T(8,128)(2,1)S(1)} collective-permute-done((f16[1024,256]{1,0:T(8,128)(2,1)S(1)}, f16[1024,256]{1,0:T(8,128)(2,1)S(1)}, u32[]{:S(2)}, u32[]{:S(2)}) %collective-permute-start.3) | collective-permute-done | bytes 524320 | tf_op jit(solution)/shard_map/ppermute | solution.py:135
  32.5 1.9 %collective-permute-start.5 = (f16[512,256]{1,0:T(8,128)(2,1)S(1)}, f16[512,256]{1,0:T(8,128)(2,1)S(1)}, u32[]{:S(2)}, u32[]{:S(2)}) collective-permute-start(f16[512,256]{1,0:T(8,128)(2,1)S(1)} %slice_convert_fusion.3), channel_id=1, source_target_pairs={{0,8},{2,10},{4,12},{6,14},{8,0},{10,2},{12,4},{14,6},{16,24},{18,... | collective-permute-start | bytes 786440 | tf_op jit(solution)/shard_map/ppermute | solution.py:135
  34.4 1.4 shard_map.105
  35.8 1.6 shard_map.106
  37.4 1.3 collective-permute-start.7
  41.1 11.2 %collective-permute-done.7 = f16[1024,256]{1,0:T(8,128)(2,1)S(1)} collective-permute-done((f16[1024,256]{1,0:T(8,128)(2,1)S(1)}, f16[1024,256]{1,0:T(8,128)(2,1)S(1)}, u32[]{:S(2)}, u32[]{:S(2)}) %collective-permute-start.7) | collective-permute-done | bytes 524320 | tf_op jit(solution)/shard_map/ppermute | solution.py:135
  52.8 1.6 collective-permute-start.10
  54.5 2.7 %collective-permute-start.9 = (f16[256,256]{1,0:T(8,128)(2,1)S(1)}, f16[256,256]{1,0:T(8,128)(2,1)S(1)}, u32[]{:S(2)}, u32[]{:S(2)}) collective-permute-start(f16[256,256]{1,0:T(8,128)(2,1)S(1)} %slice_convert_fusion.9), channel_id=1, source_target_pairs={{0,16},{2,18},{4,20},{6,22},{8,24},{10,26},{12,28},{14,30},{16,0},... | collective-permute-start | bytes 393224 | tf_op jit(solution)/shard_map/ppermute | solution.py:135
  58.0 2.7 %collective-permute-start.13 = (f16[256,256]{1,0:T(8,128)(2,1)S(1)}, f16[256,256]{1,0:T(8,128)(2,1)S(1)}, u32[]{:S(2)}, u32[]{:S(2)}) collective-permute-start(f16[256,256]{1,0:T(8,128)(2,1)S(1)} %slice_convert_fusion.8), channel_id=1, source_target_pairs={{0,16},{2,18},{4,20},{6,22},{8,24},{10,26},{12,28},{14,30},{16,0},... | collective-permute-start | bytes 393224 | tf_op jit(solution)/shard_map/ppermute | solution.py:135
  60.8 3.8 %collective-permute-start.14 = (f16[256,256]{1,0:T(8,128)(2,1)S(1)}, f16[256,256]{1,0:T(8,128)(2,1)S(1)}, u32[]{:S(2)}, u32[]{:S(2)}) collective-permute-start(f16[256,256]{1,0:T(8,128)(2,1)S(1)} %slice_convert_fusion.7), channel_id=1, source_target_pairs={{0,16},{2,18},{4,20},{6,22},{8,24},{10,26},{12,28},{14,30},{16,0},... | collective-permute-start | bytes 393224 | tf_op jit(solution)/shard_map/ppermute | solution.py:135
  64.8 6.3 %collective-permute-done.9 = f16[256,256]{1,0:T(8,128)(2,1)S(1)} collective-permute-done((f16[256,256]{1,0:T(8,128)(2,1)S(1)}, f16[256,256]{1,0:T(8,128)(2,1)S(1)}, u32[]{:S(2)}, u32[]{:S(2)}) %collective-permute-start.9) | collective-permute-done | bytes 131104 | tf_op jit(solution)/shard_map/ppermute | solution.py:135
  71.1 2.8 %collective-permute-done.13 = f16[256,256]{1,0:T(8,128)(2,1)S(1)} collective-permute-done((f16[256,256]{1,0:T(8,128)(2,1)S(1)}, f16[256,256]{1,0:T(8,128)(2,1)S(1)}, u32[]{:S(2)}, u32[]{:S(2)}) %collective-permute-start.13) | collective-permute-done | bytes 131104 | tf_op jit(solution)/shard_map/ppermute | solution.py:135
  73.9 2.4 %collective-permute-done.14 = f16[256,256]{1,0:T(8,128)(2,1)S(1)} collective-permute-done((f16[256,256]{1,0:T(8,128)(2,1)S(1)}, f16[256,256]{1,0:T(8,128)(2,1)S(1)}, u32[]{:S(2)}, u32[]{:S(2)}) %collective-permute-start.14) | collective-permute-done | bytes 131104 | tf_op jit(solution)/shard_map/ppermute | solution.py:135
  76.3 1.4 collective-permute-done.15
  78.6 1.6 collective-permute-start.16
  80.2 2.1 %collective-permute-done.16 = f32[4,512]{1,0:T(4,128)S(1)} collective-permute-done((f32[4,512]{1,0:T(4,128)S(1)}, f32[4,512]{1,0:T(4,128)S(1)}, u32[]{:S(2)}, u32[]{:S(2)}) %collective-permute-start.16) | collective-permute-done | bytes 8224 | tf_op jit(solution)/shard_map/ppermute | solution.py:140
  85.1 2.1 %collective-permute-done.18 = f32[4,512]{1,0:T(4,128)S(1)} collective-permute-done((f32[4,512]{1,0:T(4,128)S(1)}, f32[4,512]{1,0:T(4,128)S(1)}, u32[]{:S(2)}, u32[]{:S(2)}) %collective-permute-start.18) | collective-permute-done | bytes 8224 | tf_op jit(solution)/shard_map/ppermute | solution.py:140
  87.3 1.8 %copy.28 = f32[256,2,512]{2,1,0:T(2,128)} copy(f32[256,2,512]{2,0,1:T(8,128)S(1)} %pad_maximum_fusion.1) | data formatting | bytes 2097152 | tf_op jit(solution)/shard_map/stack | solution.py:242
  89.1 1.8 %collective-permute-done.19 = f32[4,512]{1,0:T(4,128)S(1)} collective-permute-done((f32[4,512]{1,0:T(4,128)S(1)}, f32[4,512]{1,0:T(4,128)S(1)}, u32[]{:S(2)}, u32[]{:S(2)}) %collective-permute-start.19) | collective-permute-done | bytes 8224 | tf_op jit(solution)/shard_map/ppermute | solution.py:140
  90.9 1.5 collective-permute-start.20
  92.4 1.8 %copy.29 = f32[256,2,512]{2,1,0:T(2,128)} copy(f32[256,2,512]{2,0,1:T(8,128)S(1)} %pad_maximum_fusion.2) | data formatting | bytes 2097152 | tf_op jit(solution)/shard_map/stack | solution.py:242
  97.1 1.6 collective-permute-start.21
  98.7 1.4 collective-permute-start.26
  100.1 1.8 %copy.30 = f32[256,2,512]{2,1,0:T(2,128)} copy(f32[256,2,512]{2,0,1:T(8,128)S(1)} %pad_maximum_fusion.3) | data formatting | bytes 2097152 | tf_op jit(solution)/shard_map/stack | solution.py:251
  101.9 5.4 %collective-permute-done.21 = bf16[256,256]{1,0:T(8,128)(2,1)S(1)} collective-permute-done((bf16[256,256]{1,0:T(8,128)(2,1)S(1)}, bf16[256,256]{1,0:T(8,128)(2,1)S(1)}, u32[]{:S(2)}, u32[]{:S(2)}) %collective-permute-start.21) | collective-permute-done | bytes 131104 | tf_op jit(solution)/shard_map/ppermute | solution.py:135
  107.4 1.8 %collective-permute-done.26 = bf16[256,256]{1,0:T(8,128)(2,1)S(1)} collective-permute-done((bf16[256,256]{1,0:T(8,128)(2,1)S(1)}, bf16[256,256]{1,0:T(8,128)(2,1)S(1)}, u32[]{:S(2)}, u32[]{:S(2)}) %collective-permute-start.26) | collective-permute-done | bytes 131104 | tf_op jit(solution)/shard_map/ppermute | solution.py:135
  111.8 1.7 %collective-permute-start.25 = (bf16[256,256]{1,0:T(8,128)(2,1)S(1)}, bf16[256,256]{1,0:T(8,128)(2,1)S(1)}, u32[]{:S(2)}, u32[]{:S(2)}) collective-permute-start(bf16[256,256]{1,0:T(8,128)(2,1)S(1)} %get-tuple-element.147), channel_id=1, source_target_pairs={{0,16},{2,18},{4,20},{6,22},{8,24},{10,26},{12,28},{14,30},{16,0},... | collective-permute-start | bytes 393224 | tf_op jit(solution)/shard_map/ppermute | solution.py:135
  113.5 3.1 %collective-permute-done.22 = bf16[512,256]{1,0:T(8,128)(2,1)S(1)} collective-permute-done((bf16[512,256]{1,0:T(8,128)(2,1)S(1)}, bf16[512,256]{1,0:T(8,128)(2,1)S(1)}, u32[]{:S(2)}, u32[]{:S(2)}) %collective-permute-start.22) | collective-permute-done | bytes 262176 | tf_op jit(solution)/shard_map/ppermute | solution.py:135
  116.7 1.5 collective-permute-start.23
  118.2 5.4 %collective-permute-done.25 = bf16[256,256]{1,0:T(8,128)(2,1)S(1)} collective-permute-done((bf16[256,256]{1,0:T(8,128)(2,1)S(1)}, bf16[256,256]{1,0:T(8,128)(2,1)S(1)}, u32[]{:S(2)}, u32[]{:S(2)}) %collective-permute-start.25) | collective-permute-done | bytes 131104 | tf_op jit(solution)/shard_map/ppermute | solution.py:135
  124.7 2.0 %collective-permute-start.31 = (bf16[1024,256]{1,0:T(8,128)(2,1)S(1)}, bf16[1024,256]{1,0:T(8,128)(2,1)S(1)}, u32[]{:S(2)}, u32[]{:S(2)}) collective-permute-start(bf16[1024,256]{1,0:T(8,128)(2,1)S(1)} %pad_maximum_fusion.15.refs_1_), channel_id=1, source_target_pairs={{0,8},{2,10},{4,12},{6,14},{8,0},{10,2},{12,4},{14,6},{16,24},{18,... | collective-permute-start | bytes 1572872 | tf_op jit(solution)/shard_map/ppermute | solution.py:135
  126.7 6.2 %collective-permute-done.29 = bf16[512,256]{1,0:T(8,128)(2,1)S(1)} collective-permute-done((bf16[512,256]{1,0:T(8,128)(2,1)S(1)}, bf16[512,256]{1,0:T(8,128)(2,1)S(1)}, u32[]{:S(2)}, u32[]{:S(2)}) %collective-permute-start.29) | collective-permute-done | bytes 262176 | tf_op jit(solution)/shard_map/ppermute | solution.py:135
  133.7 8.4 %collective-permute-done.31.refs_1_ = bf16[1024,256]{1,0:T(8,128)(2,1)S(1)} collective-permute-done((bf16[1024,256]{1,0:T(8,128)(2,1)S(1)}, bf16[1024,256]{1,0:T(8,128)(2,1)S(1)}, u32[]{:S(2)}, u32[]{:S(2)}) %collective-permute-start.31) | collective-permute-done | bytes 524320 | tf_op jit(solution)/shard_map/ppermute | solution.py:135
  144.5 1.7 %shard_map.108 = bf16[768,256]{1,0:T(8,128)(2,1)S(1)} custom-call(bf16[768,1024]{1,0:T(8,128)(2,1)S(1)} %get-tuple-element.64.refs_0_, bf16[1024,256]{1,0:T(8,128)(2,1)S(1)} %collective-permute-done.23.refs_1_, bf16[768,1024]{1,0:T(8,128)(2,1)S(1)} %get-tuple-element.60.refs_2_, bf16[1024,256]{1,0:T(8,128)(2,1)S(1)} %get-tuple-element.134.refs_3_, ...), custom_call_target="tpu_custom_call" | custom-call | tf_op jit(solution)/shard_map/pallas_call | solution.py:108
  147.3 1.7 %shard_map.110 = bf16[768,256]{1,0:T(8,128)(2,1)S(1)} custom-call(bf16[768,1024]{1,0:T(8,128)(2,1)S(1)} %get-tuple-element.103.refs_0_, bf16[1024,256]{1,0:T(8,128)(2,1)S(1)} %collective-permute-done.31.refs_1_, bf16[768,1024]{1,0:T(8,128)(2,1)S(1)} %get-tuple-element.73.refs_2_, bf16[1024,256]{1,0:T(8,128)(2,1)S(1)} %get-tuple-element.132.refs_3_, ...), custom_call_target="tpu_custom_call" | custom-call | tf_op jit(solution)/shard_map/pallas_call | solution.py:108
  149.0 7.6 %collective-permute-done.33.refs_1_ = bf16[1024,256]{1,0:T(8,128)(2,1)S(1)} collective-permute-done((bf16[1024,256]{1,0:T(8,128)(2,1)S(1)}, bf16[1024,256]{1,0:T(8,128)(2,1)S(1)}, u32[]{:S(2)}, u32[]{:S(2)}) %collective-permute-start.33) | collective-permute-done | bytes 524320 | tf_op jit(solution)/shard_map/ppermute | solution.py:135
  159.5 1.7 %shard_map.112 = bf16[768,256]{1,0:T(8,128)(2,1)S(1)} custom-call(bf16[768,1024]{1,0:T(8,128)(2,1)S(1)} %get-tuple-element.64.refs_0_, bf16[1024,256]{1,0:T(8,128)(2,1)S(1)} %collective-permute-done.33.refs_1_, bf16[768,1024]{1,0:T(8,128)(2,1)S(1)} %get-tuple-element.60.refs_2_, bf16[1024,256]{1,0:T(8,128)(2,1)S(1)} %get-tuple-element.130.refs_3_, ...), custom_call_target="tpu_custom_call" | custom-call | tf_op jit(solution)/shard_map/pallas_call | solution.py:108
  162.2 1.7 %shard_map.114 = bf16[768,256]{1,0:T(8,128)(2,1)S(1)} custom-call(bf16[768,1024]{1,0:T(8,128)(2,1)S(1)} %get-tuple-element.103.refs_0_, bf16[1024,256]{1,0:T(8,128)(2,1)S(1)} %collective-permute-done.35.refs_1_, bf16[768,1024]{1,0:T(8,128)(2,1)S(1)} %get-tuple-element.73.refs_2_, bf16[1024,256]{1,0:T(8,128)(2,1)S(1)} %get-tuple-element.128.refs_3_, ...), custom_call_target="tpu_custom_call" | custom-call | tf_op jit(solution)/shard_map/pallas_call | solution.py:108
  164.1 2.4 %reshape.311 = bf16[768,2,512]{2,1,0:T(2,128)(2,1)} reshape(bf16[768,1024]{1,0:T(8,128)(2,1)S(1)} %pad_maximum_fusion) | data formatting | bytes 3145728 | tf_op jit(solution)/shard_map/reshape | solution.py:291
  (130 shorter events, 30.5 us)
Async XLA Ops:
  2.3 2.8 %copy-start = (bf16[768,4096]{1,0:T(8,128)(2,1)S(1)}, bf16[768,4096]{1,0:T(8,128)(2,1)}, u32[]{:S(2)}) copy-start(bf16[768,4096]{1,0:T(8,128)(2,1)} %src.3) | copy-start | bytes 18874372
  5.1 2.8 %copy-start.1 = (bf16[768,4096]{1,0:T(8,128)(2,1)S(1)}, bf16[768,4096]{1,0:T(8,128)(2,1)}, u32[]{:S(2)}) copy-start(bf16[768,4096]{1,0:T(8,128)(2,1)} %src.3) | copy-start | bytes 18874372
  6.4 6.9 %collective-permute-start = (bf16[768,1024]{1,0:T(8,128)(2,1)S(1)}, bf16[768,1024]{1,0:T(8,128)(2,1)S(1)}, u32[]{:S(2)}, u32[]{:S(2)}) collective-permute-start(bf16[768,1024]{1,0:T(8,128)(2,1)S(1)} %get-tuple-element.61.refs_4_), channel_id=1, source_target_pairs={{0,2},{2,0},{4,6},{6,4},{8,10},{10,8},{12,14},{14,12},{16,18},{18,... | collective-permute-start | bytes 4718600 | tf_op jit(solution)/shard_map/ppermute | solution.py:135
  6.9 8.5 %collective-permute-start.2 = (bf16[768,1024]{1,0:T(8,128)(2,1)S(1)}, bf16[768,1024]{1,0:T(8,128)(2,1)S(1)}, u32[]{:S(2)}, u32[]{:S(2)}) collective-permute-start(bf16[768,1024]{1,0:T(8,128)(2,1)S(1)} %get-tuple-element.60.refs_2_), channel_id=1, source_target_pairs={{0,2},{2,0},{4,6},{6,4},{8,10},{10,8},{12,14},{14,12},{16,18},{18,... | collective-permute-start | bytes 4718600 | tf_op jit(solution)/shard_map/ppermute | solution.py:135
  7.1 6.2 %collective-permute-start.1 = (bf16[768,512]{1,0:T(8,128)(2,1)S(1)}, bf16[768,512]{1,0:T(8,128)(2,1)S(1)}, u32[]{:S(2)}, u32[]{:S(2)}) collective-permute-start(bf16[768,512]{1,0:T(8,128)(2,1)S(1)} %get-tuple-element.66), channel_id=1, source_target_pairs={{0,2},{2,0},{4,6},{6,4},{8,10},{10,8},{12,14},{14,12},{16,18},{18,... | collective-permute-start | bytes 2359304 | tf_op jit(solution)/shard_map/ppermute | solution.py:135
  16.7 5.7 %collective-permute-start.4 = (bf16[768,512]{1,0:T(8,128)(2,1)S(1)}, bf16[768,512]{1,0:T(8,128)(2,1)S(1)}, u32[]{:S(2)}, u32[]{:S(2)}) collective-permute-start(bf16[768,512]{1,0:T(8,128)(2,1)S(1)} %get-tuple-element.68.refs_1_), channel_id=1, source_target_pairs={{0,2},{2,0},{4,6},{6,4},{8,10},{10,8},{12,14},{14,12},{16,18},{18,... | collective-permute-start | bytes 2359304 | tf_op jit(solution)/shard_map/ppermute | solution.py:135
  17.3 15.1 %collective-permute-start.3 = (f16[1024,256]{1,0:T(8,128)(2,1)S(1)}, f16[1024,256]{1,0:T(8,128)(2,1)S(1)}, u32[]{:S(2)}, u32[]{:S(2)}) collective-permute-start(f16[1024,256]{1,0:T(8,128)(2,1)S(1)} %slice.218), channel_id=1, source_target_pairs={{0,4},{2,6},{4,0},{6,2},{8,12},{10,14},{12,8},{14,10},{16,20},{18,... | collective-permute-start | bytes 1572872 | tf_op jit(solution)/shard_map/ppermute | solution.py:135
  20.6 16.8 %collective-permute-start.8 = (f16[1024,256]{1,0:T(8,128)(2,1)S(1)}, f16[1024,256]{1,0:T(8,128)(2,1)S(1)}, u32[]{:S(2)}, u32[]{:S(2)}) collective-permute-start(f16[1024,256]{1,0:T(8,128)(2,1)S(1)} %pad_maximum_fusion.8), channel_id=1, source_target_pairs={{0,8},{2,10},{4,12},{6,14},{8,0},{10,2},{12,4},{14,6},{16,24},{18,... | collective-permute-start | bytes 1572872 | tf_op jit(solution)/shard_map/ppermute | solution.py:135
  28.1 24.5 %collective-permute-start.6 = (f16[1024,256]{1,0:T(8,128)(2,1)S(1)}, f16[1024,256]{1,0:T(8,128)(2,1)S(1)}, u32[]{:S(2)}, u32[]{:S(2)}) collective-permute-start(f16[1024,256]{1,0:T(8,128)(2,1)S(1)} %pad_maximum_fusion.9), channel_id=1, source_target_pairs={{0,8},{2,10},{4,12},{6,14},{8,0},{10,2},{12,4},{14,6},{16,24},{18,... | collective-permute-start | bytes 1572872 | tf_op jit(solution)/shard_map/ppermute | solution.py:135
  32.5 21.9 %collective-permute-start.5 = (f16[512,256]{1,0:T(8,128)(2,1)S(1)}, f16[512,256]{1,0:T(8,128)(2,1)S(1)}, u32[]{:S(2)}, u32[]{:S(2)}) collective-permute-start(f16[512,256]{1,0:T(8,128)(2,1)S(1)} %slice_convert_fusion.3), channel_id=1, source_target_pairs={{0,8},{2,10},{4,12},{6,14},{8,0},{10,2},{12,4},{14,6},{16,24},{18,... | collective-permute-start | bytes 786440 | tf_op jit(solution)/shard_map/ppermute | solution.py:135
  37.4 2.4 %copy-start.3 = (f32[256,2,512]{2,1,0:T(2,128)S(1)}, f32[256,2,512]{2,1,0:T(2,128)}, u32[]{:S(2)}) copy-start(f32[256,2,512]{2,1,0:T(2,128)} %param.9) | copy-start | bytes 3145732
  37.4 14.9 %collective-permute-start.7 = (f16[1024,256]{1,0:T(8,128)(2,1)S(1)}, f16[1024,256]{1,0:T(8,128)(2,1)S(1)}, u32[]{:S(2)}, u32[]{:S(2)}) collective-permute-start(f16[1024,256]{1,0:T(8,128)(2,1)S(1)} %slice.229), channel_id=1, source_target_pairs={{0,4},{2,6},{4,0},{6,2},{8,12},{10,14},{12,8},{14,10},{16,20},{18,... | collective-permute-start | bytes 1572872 | tf_op jit(solution)/shard_map/ppermute | solution.py:135
  38.8 1.2 copy-start.4
  38.9 1.5 copy-start.2
  38.9 19.1 %collective-permute-start.12 = (f16[512,256]{1,0:T(8,128)(2,1)S(1)}, f16[512,256]{1,0:T(8,128)(2,1)S(1)}, u32[]{:S(2)}, u32[]{:S(2)}) collective-permute-start(f16[512,256]{1,0:T(8,128)(2,1)S(1)} %slice_convert_fusion.2), channel_id=1, source_target_pairs={{0,4},{2,6},{4,0},{6,2},{8,12},{10,14},{12,8},{14,10},{16,20},{18,... | collective-permute-start | bytes 786440 | tf_op jit(solution)/shard_map/ppermute | solution.py:135
  52.5 8.2 %collective-permute-start.11 = (f16[512,256]{1,0:T(8,128)(2,1)S(1)}, f16[512,256]{1,0:T(8,128)(2,1)S(1)}, u32[]{:S(2)}, u32[]{:S(2)}) collective-permute-start(f16[512,256]{1,0:T(8,128)(2,1)S(1)} %slice_convert_fusion.1), channel_id=1, source_target_pairs={{0,8},{2,10},{4,12},{6,14},{8,0},{10,2},{12,4},{14,6},{16,24},{18,... | collective-permute-start | bytes 786440 | tf_op jit(solution)/shard_map/ppermute | solution.py:135
  52.8 11.8 %collective-permute-start.10 = (f16[512,256]{1,0:T(8,128)(2,1)S(1)}, f16[512,256]{1,0:T(8,128)(2,1)S(1)}, u32[]{:S(2)}, u32[]{:S(2)}) collective-permute-start(f16[512,256]{1,0:T(8,128)(2,1)S(1)} %slice_convert_fusion), channel_id=1, source_target_pairs={{0,4},{2,6},{4,0},{6,2},{8,12},{10,14},{12,8},{14,10},{16,20},{18,... | collective-permute-start | bytes 786440 | tf_op jit(solution)/shard_map/ppermute | solution.py:135
  54.5 16.5 %collective-permute-start.9 = (f16[256,256]{1,0:T(8,128)(2,1)S(1)}, f16[256,256]{1,0:T(8,128)(2,1)S(1)}, u32[]{:S(2)}, u32[]{:S(2)}) collective-permute-start(f16[256,256]{1,0:T(8,128)(2,1)S(1)} %slice_convert_fusion.9), channel_id=1, source_target_pairs={{0,16},{2,18},{4,20},{6,22},{8,24},{10,26},{12,28},{14,30},{16,0},... | collective-permute-start | bytes 393224 | tf_op jit(solution)/shard_map/ppermute | solution.py:135
  58.0 15.8 %collective-permute-start.13 = (f16[256,256]{1,0:T(8,128)(2,1)S(1)}, f16[256,256]{1,0:T(8,128)(2,1)S(1)}, u32[]{:S(2)}, u32[]{:S(2)}) collective-permute-start(f16[256,256]{1,0:T(8,128)(2,1)S(1)} %slice_convert_fusion.8), channel_id=1, source_target_pairs={{0,16},{2,18},{4,20},{6,22},{8,24},{10,26},{12,28},{14,30},{16,0},... | collective-permute-start | bytes 393224 | tf_op jit(solution)/shard_map/ppermute | solution.py:135
  60.8 15.5 %collective-permute-start.14 = (f16[256,256]{1,0:T(8,128)(2,1)S(1)}, f16[256,256]{1,0:T(8,128)(2,1)S(1)}, u32[]{:S(2)}, u32[]{:S(2)}) collective-permute-start(f16[256,256]{1,0:T(8,128)(2,1)S(1)} %slice_convert_fusion.7), channel_id=1, source_target_pairs={{0,16},{2,18},{4,20},{6,22},{8,24},{10,26},{12,28},{14,30},{16,0},... | collective-permute-start | bytes 393224 | tf_op jit(solution)/shard_map/ppermute | solution.py:135
  64.7 13.0 %collective-permute-start.15 = (f16[256,256]{1,0:T(8,128)(2,1)S(1)}, f16[256,256]{1,0:T(8,128)(2,1)S(1)}, u32[]{:S(2)}, u32[]{:S(2)}) collective-permute-start(f16[256,256]{1,0:T(8,128)(2,1)S(1)} %slice_convert_fusion.6), channel_id=1, source_target_pairs={{0,16},{2,18},{4,20},{6,22},{8,24},{10,26},{12,28},{14,30},{16,0},... | collective-permute-start | bytes 393224 | tf_op jit(solution)/shard_map/ppermute | solution.py:135
  78.6 3.7 %collective-permute-start.16 = (f32[4,512]{1,0:T(4,128)S(1)}, f32[4,512]{1,0:T(4,128)S(1)}, u32[]{:S(2)}, u32[]{:S(2)}) collective-permute-start(f32[4,512]{1,0:T(4,128)S(1)} %pad_maximum_fusion.22), channel_id=1, source_target_pairs={{0,1},{1,0},{2,3},{3,2},{4,5},{5,4},{6,7},{7,6},{8,9},{9,8},{10,11... | collective-permute-start | bytes 24584 | tf_op jit(solution)/shard_map/ppermute | solution.py:140
  82.3 1.2 collective-permute-start.17
  83.5 3.7 %collective-permute-start.18 = (f32[4,512]{1,0:T(4,128)S(1)}, f32[4,512]{1,0:T(4,128)S(1)}, u32[]{:S(2)}, u32[]{:S(2)}) collective-permute-start(f32[4,512]{1,0:T(4,128)S(1)} %add.136), channel_id=1, source_target_pairs={{0,4},{2,6},{4,0},{6,2},{8,12},{10,14},{12,8},{14,10},{16,20},{18,... | collective-permute-start | bytes 24584 | tf_op jit(solution)/shard_map/ppermute | solution.py:140
  87.2 3.7 %collective-permute-start.19 = (f32[4,512]{1,0:T(4,128)S(1)}, f32[4,512]{1,0:T(4,128)S(1)}, u32[]{:S(2)}, u32[]{:S(2)}) collective-permute-start(f32[4,512]{1,0:T(4,128)S(1)} %add.137), channel_id=1, source_target_pairs={{0,8},{2,10},{4,12},{6,14},{8,0},{10,2},{12,4},{14,6},{16,24},{18,... | collective-permute-start | bytes 24584 | tf_op jit(solution)/shard_map/ppermute | solution.py:140
  90.9 4.5 %collective-permute-start.20 = (f32[4,512]{1,0:T(4,128)S(1)}, f32[4,512]{1,0:T(4,128)S(1)}, u32[]{:S(2)}, u32[]{:S(2)}) collective-permute-start(f32[4,512]{1,0:T(4,128)S(1)} %add.140), channel_id=1, source_target_pairs={{0,16},{2,18},{4,20},{6,22},{8,24},{10,26},{12,28},{14,30},{16,0},... | collective-permute-start | bytes 24584 | tf_op jit(solution)/shard_map/ppermute | solution.py:140
  97.1 10.2 %collective-permute-start.21 = (bf16[256,256]{1,0:T(8,128)(2,1)S(1)}, bf16[256,256]{1,0:T(8,128)(2,1)S(1)}, u32[]{:S(2)}, u32[]{:S(2)}) collective-permute-start(bf16[256,256]{1,0:T(8,128)(2,1)S(1)} %get-tuple-element.145), channel_id=1, source_target_pairs={{0,16},{2,18},{4,20},{6,22},{8,24},{10,26},{12,28},{14,30},{16,0},... | collective-permute-start | bytes 393224 | tf_op jit(solution)/shard_map/ppermute | solution.py:135
  98.7 10.6 %collective-permute-start.26 = (bf16[256,256]{1,0:T(8,128)(2,1)S(1)}, bf16[256,256]{1,0:T(8,128)(2,1)S(1)}, u32[]{:S(2)}, u32[]{:S(2)}) collective-permute-start(bf16[256,256]{1,0:T(8,128)(2,1)S(1)} %get-tuple-element.146), channel_id=1, source_target_pairs={{0,16},{2,18},{4,20},{6,22},{8,24},{10,26},{12,28},{14,30},{16,0},... | collective-permute-start | bytes 393224 | tf_op jit(solution)/shard_map/ppermute | solution.py:135
  107.3 9.3 %collective-permute-start.22 = (bf16[512,256]{1,0:T(8,128)(2,1)S(1)}, bf16[512,256]{1,0:T(8,128)(2,1)S(1)}, u32[]{:S(2)}, u32[]{:S(2)}) collective-permute-start(bf16[512,256]{1,0:T(8,128)(2,1)S(1)} %pad_maximum_fusion.18), channel_id=1, source_target_pairs={{0,8},{2,10},{4,12},{6,14},{8,0},{10,2},{12,4},{14,6},{16,24},{18,... | collective-permute-start | bytes 786440 | tf_op jit(solution)/shard_map/ppermute | solution.py:135
  109.3 8.9 %collective-permute-start.27 = (bf16[512,256]{1,0:T(8,128)(2,1)S(1)}, bf16[512,256]{1,0:T(8,128)(2,1)S(1)}, u32[]{:S(2)}, u32[]{:S(2)}) collective-permute-start(bf16[512,256]{1,0:T(8,128)(2,1)S(1)} %pad_maximum_fusion.19), channel_id=1, source_target_pairs={{0,4},{2,6},{4,0},{6,2},{8,12},{10,14},{12,8},{14,10},{16,20},{18,... | collective-permute-start | bytes 786440 | tf_op jit(solution)/shard_map/ppermute | solution.py:135
  110.5 13.2 %collective-permute-start.24 = (bf16[256,256]{1,0:T(8,128)(2,1)S(1)}, bf16[256,256]{1,0:T(8,128)(2,1)S(1)}, u32[]{:S(2)}, u32[]{:S(2)}) collective-permute-start(bf16[256,256]{1,0:T(8,128)(2,1)S(1)} %get-tuple-element.148), channel_id=1, source_target_pairs={{0,16},{2,18},{4,20},{6,22},{8,24},{10,26},{12,28},{14,30},{16,0},... | collective-permute-start | bytes 393224 | tf_op jit(solution)/shard_map/ppermute | solution.py:135
  111.8 11.8 %collective-permute-start.25 = (bf16[256,256]{1,0:T(8,128)(2,1)S(1)}, bf16[256,256]{1,0:T(8,128)(2,1)S(1)}, u32[]{:S(2)}, u32[]{:S(2)}) collective-permute-start(bf16[256,256]{1,0:T(8,128)(2,1)S(1)} %get-tuple-element.147), channel_id=1, source_target_pairs={{0,16},{2,18},{4,20},{6,22},{8,24},{10,26},{12,28},{14,30},{16,0},... | collective-permute-start | bytes 393224 | tf_op jit(solution)/shard_map/ppermute | solution.py:135
  116.7 16.8 %collective-permute-start.23 = (bf16[1024,256]{1,0:T(8,128)(2,1)S(1)}, bf16[1024,256]{1,0:T(8,128)(2,1)S(1)}, u32[]{:S(2)}, u32[]{:S(2)}) collective-permute-start(bf16[1024,256]{1,0:T(8,128)(2,1)S(1)} %pad_maximum_fusion.14.refs_1_), channel_id=1, source_target_pairs={{0,4},{2,6},{4,0},{6,2},{8,12},{10,14},{12,8},{14,10},{16,20},{18,... | collective-permute-start | bytes 1572872 | tf_op jit(solution)/shard_map/ppermute | solution.py:135
  123.6 9.3 %collective-permute-start.29 = (bf16[512,256]{1,0:T(8,128)(2,1)S(1)}, bf16[512,256]{1,0:T(8,128)(2,1)S(1)}, u32[]{:S(2)}, u32[]{:S(2)}) collective-permute-start(bf16[512,256]{1,0:T(8,128)(2,1)S(1)} %pad_maximum_fusion.20), channel_id=1, source_target_pairs={{0,8},{2,10},{4,12},{6,14},{8,0},{10,2},{12,4},{14,6},{16,24},{18,... | collective-permute-start | bytes 786440 | tf_op jit(solution)/shard_map/ppermute | solution.py:135
  123.7 9.7 %collective-permute-start.28 = (bf16[512,256]{1,0:T(8,128)(2,1)S(1)}, bf16[512,256]{1,0:T(8,128)(2,1)S(1)}, u32[]{:S(2)}, u32[]{:S(2)}) collective-permute-start(bf16[512,256]{1,0:T(8,128)(2,1)S(1)} %pad_maximum_fusion.21), channel_id=1, source_target_pairs={{0,4},{2,6},{4,0},{6,2},{8,12},{10,14},{12,8},{14,10},{16,20},{18,... | collective-permute-start | bytes 786440 | tf_op jit(solution)/shard_map/ppermute | solution.py:135
  124.7 17.4 %collective-permute-start.31 = (bf16[1024,256]{1,0:T(8,128)(2,1)S(1)}, bf16[1024,256]{1,0:T(8,128)(2,1)S(1)}, u32[]{:S(2)}, u32[]{:S(2)}) collective-permute-start(bf16[1024,256]{1,0:T(8,128)(2,1)S(1)} %pad_maximum_fusion.15.refs_1_), channel_id=1, source_target_pairs={{0,8},{2,10},{4,12},{6,14},{8,0},{10,2},{12,4},{14,6},{16,24},{18,... | collective-permute-start | bytes 1572872 | tf_op jit(solution)/shard_map/ppermute | solution.py:135
  133.6 10.8 %collective-permute-start.30 = (bf16[2048,256]{1,0:T(8,128)(2,1)S(1)}, bf16[2048,256]{1,0:T(8,128)(2,1)S(1)}, u32[]{:S(2)}, u32[]{:S(2)}) collective-permute-start(bf16[2048,256]{1,0:T(8,128)(2,1)S(1)} %pad_maximum_fusion.4), channel_id=1, source_target_pairs={{0,2},{2,0},{4,6},{6,4},{8,10},{10,8},{12,14},{14,12},{16,18},{18,... | collective-permute-start | bytes 3145736 | tf_op jit(solution)/shard_map/ppermute | solution.py:135
  142.2 5.0 %collective-permute-start.32 = (bf16[2048,256]{1,0:T(8,128)(2,1)S(1)}, bf16[2048,256]{1,0:T(8,128)(2,1)S(1)}, u32[]{:S(2)}, u32[]{:S(2)}) collective-permute-start(bf16[2048,256]{1,0:T(8,128)(2,1)S(1)} %pad_maximum_fusion.5), channel_id=1, source_target_pairs={{0,2},{2,0},{4,6},{6,4},{8,10},{10,8},{12,14},{14,12},{16,18},{18,... | collective-permute-start | bytes 3145736 | tf_op jit(solution)/shard_map/ppermute | solution.py:135
  142.2 14.3 %collective-permute-start.33 = (bf16[1024,256]{1,0:T(8,128)(2,1)S(1)}, bf16[1024,256]{1,0:T(8,128)(2,1)S(1)}, u32[]{:S(2)}, u32[]{:S(2)}) collective-permute-start(bf16[1024,256]{1,0:T(8,128)(2,1)S(1)} %pad_maximum_fusion.16.refs_1_), channel_id=1, source_target_pairs={{0,4},{2,6},{4,0},{6,2},{8,12},{10,14},{12,8},{14,10},{16,20},{18,... | collective-permute-start | bytes 1572872 | tf_op jit(solution)/shard_map/ppermute | solution.py:135
  143.2 14.0 %collective-permute-start.35 = (bf16[1024,256]{1,0:T(8,128)(2,1)S(1)}, bf16[1024,256]{1,0:T(8,128)(2,1)S(1)}, u32[]{:S(2)}, u32[]{:S(2)}) collective-permute-start(bf16[1024,256]{1,0:T(8,128)(2,1)S(1)} %pad_maximum_fusion.17.refs_1_), channel_id=1, source_target_pairs={{0,8},{2,10},{4,12},{6,14},{8,0},{10,2},{12,4},{14,6},{16,24},{18,... | collective-permute-start | bytes 1572872 | tf_op jit(solution)/shard_map/ppermute | solution.py:135
  156.7 2.7 %collective-permute-start.34 = (bf16[2048,256]{1,0:T(8,128)(2,1)S(1)}, bf16[2048,256]{1,0:T(8,128)(2,1)S(1)}, u32[]{:S(2)}, u32[]{:S(2)}) collective-permute-start(bf16[2048,256]{1,0:T(8,128)(2,1)S(1)} %pad_maximum_fusion.6), channel_id=1, source_target_pairs={{0,2},{2,0},{4,6},{6,4},{8,10},{10,8},{12,14},{14,12},{16,18},{18,... | collective-permute-start | bytes 3145736 | tf_op jit(solution)/shard_map/ppermute | solution.py:135
  157.3 4.8 %collective-permute-start.36 = (bf16[2048,256]{1,0:T(8,128)(2,1)S(1)}, bf16[2048,256]{1,0:T(8,128)(2,1)S(1)}, u32[]{:S(2)}, u32[]{:S(2)}) collective-permute-start(bf16[2048,256]{1,0:T(8,128)(2,1)S(1)} %pad_maximum_fusion.7), channel_id=1, source_target_pairs={{0,2},{2,0},{4,6},{6,4},{8,10},{10,8},{12,14},{14,12},{16,18},{18,... | collective-permute-start | bytes 3145736 | tf_op jit(solution)/shard_map/ppermute | solution.py:135

commit v3 on v2

--- a/solution.py
+++ b/solution.py
@@ -10,24 +10,26 @@
 
 F32 = jnp.float32
 LANES = 128
-CHUNKS = ((0, 0, 0), (0, 1, 1), (1, 0, 0), (1, 1, 1))
+PICK_MIB = 6
+DOT_MIB = 8
+SUM_CHUNKS = ((0, 0, 2, 0), (0, 2, 4, 1), (1, 0, 2, 0), (1, 2, 4, 1))
+GATHER_CHUNKS = ((0, 0, 2, 0), (0, 2, 4, 1), (1, 0, 2, 0), (1, 2, 4, 1))
 
 
 def sums_plan(deep):
     plan = [("P", 0, 0), ("S", 0, 0), ("S", 1, 0), ("P", 1, 0), ("S", 2, 0), ("S", 3, 0)]
-    return plan + [("T", i, depth) for depth in range(deep) for i in range(len(CHUNKS))]
+    plan += [("T", i, depth) for depth in range(deep - 1) for i in range(len(SUM_CHUNKS))]
+    return plan + [("T", i, deep - 1) for i in (1, 0, 2, 3)]
 
 
 def gathers_plan(deep):
     last = deep - 1
-    plan = [("G", 0, 0), ("G", 1, 0), ("J", 0, last), ("J", 1, last), ("G", 2, 0), ("G", 3, 0), ("O", 0, 0)]
+    plan = [("G", 0, 0), ("G", 1, 0), ("J", 0, last), ("J", 1, last), ("G", 2, 0), ("G", 3, 0)]
     for depth in reversed(range(1, last)):
         plan += [("J", 0, depth), ("J", 1, depth), ("J", 2, depth + 1), ("J", 3, depth + 1)]
-    plan += [("J", 2, 1), ("J", 3, 1)]
-    for pair in ((0, 1), (2, 3)):
-        plan += [("J", i, 0) for i in pair]
-        plan += [(kind, i, 0) for i in pair for kind in "HK"]
-    return plan
+    plan += [("O", 0, 0), ("J", 2, 1), ("J", 3, 1), ("J", 0, 0), ("J", 1, 0)]
+    plan += [("H", 0, 0), ("K", 0, 0), ("H", 1, 0), ("M", 1, 0), ("K", 1, 0), ("H", 2, 0), ("H", 3, 0)]
+    return plan + [("J", 2, 0), ("J", 3, 0), ("M", 2, 0), ("M", 3, 0), ("K", 2, 0), ("K", 3, 0)]
 
 
 def after(value, *others):
@@ -77,7 +79,7 @@
             pltpu.SemaphoreType.DMA((count,)),
             pltpu.SemaphoreType.DMA((count,)),
         ],
-        compiler_params=pltpu.CompilerParams(vmem_limit_bytes=16 * 2**20),
+        compiler_params=pltpu.CompilerParams(vmem_limit_bytes=PICK_MIB * 2**20),
         cost_estimate=pl.CostEstimate(flops=0, bytes_accessed=0, transcendentals=0),
     )(activations)
 
@@ -110,7 +112,7 @@
         out_shape=jax.ShapeDtypeStruct((height, wide), dtype),
         in_specs=[pl.BlockSpec(memory_space=pltpu.VMEM)] * len(operands),
         out_specs=pl.BlockSpec(memory_space=pltpu.VMEM),
-        compiler_params=pltpu.CompilerParams(vmem_limit_bytes=24 * 2**20),
+        compiler_params=pltpu.CompilerParams(vmem_limit_bytes=DOT_MIB * 2**20),
         cost_estimate=pl.CostEstimate(flops=0, bytes_accessed=0, transcendentals=0),
     )(*operands)
 
@@ -135,12 +137,28 @@
         return lax.ppermute(value, "dp", [(i, i ^ (1 << bit)) for i in range(n)])
 
     def total(value, fillers):
-        hops = [("tensor", bit, t) for bit in range(t.bit_length() - 1)] + [("dp", bit, n) for bit in range(bits)]
-        for i, (axis, bit, size) in enumerate(hops):
-            other = lax.ppermute(value, axis, [(i, i ^ (1 << bit)) for i in range(size)])
-            if i + len(fillers) >= len(hops):
-                other = after(other, fillers[i - len(hops)])
-            value = value + other
+        hops = [("dp", 1 << bit) for bit in range(bits)] + [("tensor", 1 << bit) for bit in range(t.bit_length() - 1)]
+        hops = hops[:1] + [hop for pair in zip(hops[bits:], hops[1:bits]) for hop in pair] + [
+            hop for hop in hops[1:] if hop not in [x for pair in zip(hops[bits:], hops[1:bits]) for x in pair]
+        ]
+        rounds = [hops[:1]] + [hops[i : i + 2] for i in range(1, len(hops), 2)]
+
+        def fetch(*flips):
+            flip = {"dp": 0, "tensor": 0}
+            for axis, amount in flips:
+                flip[axis] ^= amount
+            perm = [(i, ((i // t) ^ flip["dp"]) * t + ((i % t) ^ flip["tensor"])) for i in range(n * t)]
+            return lax.ppermute(value, ("dp", "tensor"), perm)
+
+        for i, around in enumerate(rounds):
+            others = [fetch(around[0])]
+            if len(around) > 1:
+                others += [fetch(around[1]), fetch(*around)]
+            if i + len(fillers) >= len(rounds):
+                others[0] = after(others[0], fillers[i - len(rounds)])
+            value = value + others[0]
+            if len(around) > 1:
+                value = value + (others[1] + others[2])
         return value
 
     def dot_t(a, g):
@@ -151,19 +169,16 @@
 
     def local(activations, grad_out, weights, first_moment, second_moment, step):
         rows, kinds, cols = weights.shape
-        cut = cols // 2
-        parts = [slice(0, cut), slice(cut, cols)]
-        chunks = [(s, k) for s, k, _ in CHUNKS]
-        plans = [plan for *_, plan in CHUNKS]
-        amount = len(chunks)
+        chunks = [(s, slice(low * cols // 4, high * cols // 4)) for s, low, high, _ in SUM_CHUNKS]
+        plans = [plan for *_, plan in SUM_CHUNKS]
         count = step[0].astype(F32)
         bias_one = 1.0 - jnp.exp(count * math.log(0.9))
         bias_two = 1.0 - jnp.exp(count * math.log(0.95))
 
         grad_out = lax.optimization_barrier(jnp.transpose(grad_out, (1, 0, 2)))
+        sibling_out = [swap(grad_out[0], 0)]
         shares = blocks_of(orders[0])
-        sibling_out = [swap(grad_out[0], 0)]
-        theirs = [pick_blocks(after(activations, grad_out), [j + 1 for j in shares], rows)]
+        theirs = [pick_blocks(after(activations, sibling_out[0]), [j + 1 for j in shares], rows)]
         sibling = [swap(side, 0) for side in reversed(theirs[0])][::-1]
         mine = [pick_blocks(after(activations, *theirs[0]), shares, rows)]
 
@@ -188,8 +203,8 @@
         def halve(i, depth):
             order = orders[plans[i]]
             if depth == 0:
-                s, k = chunks[i]
-                low, high = (whole[s, side][:, parts[k]] for side in (0, 1))
+                s, part = chunks[i]
+                low, high = (whole[s, side][:, part] for side in (0, 1))
                 if plans[i] == 0:
                     keep, out = low, high
                 else:
@@ -231,8 +246,8 @@
 
         states, sums = [], []
         for s in range(kinds):
-            places = sorted((i for i in range(amount) if chunks[i][0] == s), key=lambda i: chunks[i])
-            grad = jnp.concatenate([held[i] for i in places], axis=1)
+            places = sorted((part.start, i) for i, (kind, part) in enumerate(chunks) if kind == s)
+            grad = jnp.concatenate([held[i] for _, i in places], axis=1)
             first = 0.9 * first_moment[:, s] + 0.1 * grad
             second = 0.95 * second_moment[:, s] + 0.05 * grad * grad
             update = first / bias_one / (jnp.sqrt(second / bias_two) + 1e-06) + 0.1 * weights[:, s]
@@ -250,6 +265,8 @@
         halves = [fresh.astype(jnp.bfloat16) for fresh in news]
         new_weights = rows_first(jnp.stack(news, axis=1))
 
+        chunks = [(s, slice(low * cols // 4, high * cols // 4)) for s, low, high, _ in GATHER_CHUNKS]
+        plans = [plan for *_, plan in GATHER_CHUNKS]
         gathered, arrived, sums_of, other, added = {}, {}, {}, {}, set()
 
         def spread(i, depth):
@@ -258,8 +275,8 @@
 
         for kind, i, depth in gathers_plan(deep):
             if kind == "G":
-                s, k = chunks[i]
-                gathered[i] = halves[s][:, parts[k]]
+                s, part = chunks[i]
+                gathered[i] = halves[s][:, part]
                 spread(i, deep - 1)
             elif kind == "O":
                 new_weights = gated(new_weights)
@@ -286,8 +303,8 @@
                 pairs += [(theirs[plans[i]][side], sides[side]) for side in (0, 1)]
                 sums_of[i] = multiply(pairs, sums_of[i], dtype=jnp.bfloat16)
                 last[0] = sums_of[i]
-        places = sorted(range(amount), key=lambda i: chunks[i])
-        new_kv = jnp.concatenate([sums_of[i] for i in places], axis=1)
+        places = sorted((s, part.start, i) for i, (s, part) in enumerate(chunks))
+        new_kv = jnp.concatenate([sums_of[i] for *_, i in places], axis=1)
         return (new_weights, new_first, new_second, ratios, new_kv.reshape(-1, kinds, cols))
 
     return local

time: 167 us -> 155 us (0.928)
  waiting for transfers between devices: 80.2 us -> 66.1 us
  starting transfers between devices: 39 us -> 43.2 us
  local copies, waits for them, and re-layouts: 14.2 us -> 11.5 us
    ppermute x32, waiting for transfers between devices: 71.8 us -> 60.9 us  [swap(): return lax.ppermute(value, 'dp', [(i, i ^ 1 << bit) for i in range(n)])]
    ppermute x5 -> x7, starting transfers between devices: 4.41 us -> 8.06 us  [fetch(): return lax.ppermute(value, ('dp', 'tensor'), perm)]
    ppermute x5 -> x7, waiting for transfers between devices: 8.34 us -> 5.15 us  [fetch(): return lax.ppermute(value, ('dp', 'tensor'), perm)]
    unnamed x11 -> x9, local copies, waits for them, and re-layouts: 4.98 us -> 2.29 us
    pallas_call x10 -> x13, Pallas kernels: 15.5 us -> 17.1 us  [multiply(): pl.pallas_call(kernel, out_shape=jax.ShapeDtypeStruct((height, wide), dty...]
  transfers between devices with their start and end apart: 37 -> 39, of which waited for: 23 -> 23; matrix products, arithmetic and copies ran while one was open for 8% -> 9% of each run, Pallas kernels for 11% -> 12%
where the time goes in v3:
time: 155 us; the launch traced here: 154 us
  waiting for transfers between devices  66.1 us (43%)
  starting transfers between devices  43.2 us (28%)
  Pallas kernels  21.4 us (14%)
  local copies, waits for them, and re-layouts  11.5 us (7%)
  other arithmetic  6.14 us (4%)
  matrix products  4.05 us (3%)
  between operations  2.02 us (1%)
    ppermute x32, waiting for transfers between devices, swap(): return lax.ppermute(value, 'dp', [(i, i ^ 1 << bit) for i in range(n)])  60.9 us
    ppermute x32, starting transfers between devices, swap(): return lax.ppermute(value, 'dp', [(i, i ^ 1 << bit) for i in range(n)])  35.1 us
    pallas_call x13, Pallas kernels, multiply(): pl.pallas_call(kernel, out_shape=jax.ShapeDtypeStruct((height, wide), dty...  17.1 us
    ppermute x7, starting transfers between devices, fetch(): return lax.ppermute(value, ('dp', 'tensor'), perm)  8.06 us
    ppermute x7, waiting for transfers between devices, fetch(): return lax.ppermute(value, ('dp', 'tensor'), perm)  5.15 us
    pallas_call x4, Pallas kernels, pick_blocks(): pl.pallas_call(kernel, out_shape=[jax.ShapeDtypeStruct((tokens, half * wi...  4.27 us
    dot_general x4, matrix products, dot_t(): lax.dot_general(a, g, (((0,), (0,)), ((), ())), preferred_element_type=F32)  4.05 us
    another operation x2, local copies, waits for them, and re-layouts, local(): jnp.stack(x, axis=1)  3.56 us
  transfers between devices with their start and end apart: 39, of which 23 were waited for; matrix products, arithmetic and copies ran while one was open for 9% of the time, Pallas kernels for 12%

profile of v3, /device:TPU:0, one launch (start us, length us, event | category | flops | bytes accessed | tf_op | source)
XLA Modules:
  0.0 154.3 jit_solution(14838571107007559778)
XLA Ops:
  0.6 1.8 %copy.32 = bf16[768,2,512]{2,0,1:T(8,128)(2,1)S(1)} copy(bf16[768,2,512]{2,1,0:T(2,128)(2,1)} %param.7) | data formatting | bytes 3145728 | tf_op args[1]
  3.1 1.9 %collective-permute-done = bf16[768,512]{1,0:T(8,128)(2,1)S(1)} collective-permute-done((bf16[768,512]{1,0:T(8,128)(2,1)S(1)}, bf16[768,512]{1,0:T(8,128)(2,1)S(1)}, u32[]{:S(2)}, u32[]{:S(2)}) %collective-permute-start) | collective-permute-done | bytes 786464 | tf_op jit(solution)/shard_map/ppermute | solution.py:137
  6.6 1.1 shard_map.102
  13.7 2.7 %collective-permute-start.3 = (f16[1024,256]{1,0:T(8,128)(2,1)S(1)}, f16[1024,256]{1,0:T(8,128)(2,1)S(1)}, u32[]{:S(2)}, u32[]{:S(2)}) collective-permute-start(f16[1024,256]{1,0:T(8,128)(2,1)S(1)} %slice.218), channel_id=1, source_target_pairs={{0,4},{2,6},{4,0},{6,2},{8,12},{10,14},{12,8},{14,10},{16,20},{18,... | collective-permute-start | bytes 1572872 | tf_op jit(solution)/shard_map/ppermute | solution.py:137
  17.2 1.6 %collective-permute-start.8 = (f16[1024,256]{1,0:T(8,128)(2,1)S(1)}, f16[1024,256]{1,0:T(8,128)(2,1)S(1)}, u32[]{:S(2)}, u32[]{:S(2)}) collective-permute-start(f16[1024,256]{1,0:T(8,128)(2,1)S(1)} %pad_maximum_fusion.8), channel_id=1, source_target_pairs={{0,8},{2,10},{4,12},{6,14},{8,0},{10,2},{12,4},{14,6},{16,24},{18,... | collective-permute-start | bytes 1572872 | tf_op jit(solution)/shard_map/ppermute | solution.py:137
  18.8 2.5 %shard_map.103 = f32[1024,512]{1,0:T(8,128)S(1)} custom-call(bf16[768,1024]{1,0:T(8,128)(2,1)S(1)} %get-tuple-element.67.refs_0_, bf16[768,512]{1,0:T(8,128)(2,1)S(1)} %get-tuple-element.71.refs_1_, bf16[768,1024]{1,0:T(8,128)(2,1)S(1)} %collective-permute-done.1.refs_2_, bf16[768,512]{1,0:T(8,128)(2,1)S(1)} %collective-permute-done.4.refs_3_), custom_call_target="tpu_custom_call" | custom-call | tf_op jit(solution)/shard_map/pallas_call | solution.py:110
  21.8 2.5 %shard_map.104 = f32[1024,512]{1,0:T(8,128)S(1)} custom-call(bf16[768,1024]{1,0:T(8,128)(2,1)S(1)} %get-tuple-element.66.refs_0_, bf16[768,512]{1,0:T(8,128)(2,1)S(1)} %get-tuple-element.71.refs_1_, bf16[768,1024]{1,0:T(8,128)(2,1)S(1)} %collective-permute-done.2.refs_2_, bf16[768,512]{1,0:T(8,128)(2,1)S(1)} %collective-permute-done.4.refs_3_), custom_call_target="tpu_custom_call" | custom-call | tf_op jit(solution)/shard_map/pallas_call | solution.py:110
  25.1 3.8 %collective-permute-done.3 = f16[1024,256]{1,0:T(8,128)(2,1)S(1)} collective-permute-done((f16[1024,256]{1,0:T(8,128)(2,1)S(1)}, f16[1024,256]{1,0:T(8,128)(2,1)S(1)}, u32[]{:S(2)}, u32[]{:S(2)}) %collective-permute-start.3) | collective-permute-done | bytes 524320 | tf_op jit(solution)/shard_map/ppermute | solution.py:137
  29.1 1.9 %collective-permute-start.5 = (f16[512,256]{1,0:T(8,128)(2,1)S(1)}, f16[512,256]{1,0:T(8,128)(2,1)S(1)}, u32[]{:S(2)}, u32[]{:S(2)}) collective-permute-start(f16[512,256]{1,0:T(8,128)(2,1)S(1)} %slice_convert_fusion.3), channel_id=1, source_target_pairs={{0,8},{2,10},{4,12},{6,14},{8,0},{10,2},{12,4},{14,6},{16,24},{18,... | collective-permute-start | bytes 786440 | tf_op jit(solution)/shard_map/ppermute | solution.py:137
  32.0 1.2 shard_map.106
  33.2 1.6 %collective-permute-start.7 = (f16[1024,256]{1,0:T(8,128)(2,1)S(1)}, f16[1024,256]{1,0:T(8,128)(2,1)S(1)}, u32[]{:S(2)}, u32[]{:S(2)}) collective-permute-start(f16[1024,256]{1,0:T(8,128)(2,1)S(1)} %slice.229), channel_id=1, source_target_pairs={{0,4},{2,6},{4,0},{6,2},{8,12},{10,14},{12,8},{14,10},{16,20},{18,... | collective-permute-start | bytes 1572872 | tf_op jit(solution)/shard_map/ppermute | solution.py:137
  37.1 11.0 %collective-permute-done.7 = f16[1024,256]{1,0:T(8,128)(2,1)S(1)} collective-permute-done((f16[1024,256]{1,0:T(8,128)(2,1)S(1)}, f16[1024,256]{1,0:T(8,128)(2,1)S(1)}, u32[]{:S(2)}, u32[]{:S(2)}) %collective-permute-start.7) | collective-permute-done | bytes 524320 | tf_op jit(solution)/shard_map/ppermute | solution.py:137
  49.0 1.7 %collective-permute-start.12 = (f16[512,256]{1,0:T(8,128)(2,1)S(1)}, f16[512,256]{1,0:T(8,128)(2,1)S(1)}, u32[]{:S(2)}, u32[]{:S(2)}) collective-permute-start(f16[512,256]{1,0:T(8,128)(2,1)S(1)} %slice_convert_fusion), channel_id=1, source_target_pairs={{0,4},{2,6},{4,0},{6,2},{8,12},{10,14},{12,8},{14,10},{16,20},{18,... | collective-permute-start | bytes 786440 | tf_op jit(solution)/shard_map/ppermute | solution.py:137
  50.8 2.7 %collective-permute-start.9 = (f16[256,256]{1,0:T(8,128)(2,1)S(1)}, f16[256,256]{1,0:T(8,128)(2,1)S(1)}, u32[]{:S(2)}, u32[]{:S(2)}) collective-permute-start(f16[256,256]{1,0:T(8,128)(2,1)S(1)} %slice_convert_fusion.9), channel_id=1, source_target_pairs={{0,16},{2,18},{4,20},{6,22},{8,24},{10,26},{12,28},{14,30},{16,0},... | collective-permute-start | bytes 393224 | tf_op jit(solution)/shard_map/ppermute | solution.py:137
  53.8 2.7 %collective-permute-start.11 = (f16[256,256]{1,0:T(8,128)(2,1)S(1)}, f16[256,256]{1,0:T(8,128)(2,1)S(1)}, u32[]{:S(2)}, u32[]{:S(2)}) collective-permute-start(f16[256,256]{1,0:T(8,128)(2,1)S(1)} %slice_convert_fusion.8), channel_id=1, source_target_pairs={{0,16},{2,18},{4,20},{6,22},{8,24},{10,26},{12,28},{14,30},{16,0},... | collective-permute-start | bytes 393224 | tf_op jit(solution)/shard_map/ppermute | solution.py:137
  56.6 3.8 %collective-permute-start.14 = (f16[256,256]{1,0:T(8,128)(2,1)S(1)}, f16[256,256]{1,0:T(8,128)(2,1)S(1)}, u32[]{:S(2)}, u32[]{:S(2)}) collective-permute-start(f16[256,256]{1,0:T(8,128)(2,1)S(1)} %slice_convert_fusion.7), channel_id=1, source_target_pairs={{0,16},{2,18},{4,20},{6,22},{8,24},{10,26},{12,28},{14,30},{16,0},... | collective-permute-start | bytes 393224 | tf_op jit(solution)/shard_map/ppermute | solution.py:137
  60.6 9.7 %collective-permute-done.11 = f16[256,256]{1,0:T(8,128)(2,1)S(1)} collective-permute-done((f16[256,256]{1,0:T(8,128)(2,1)S(1)}, f16[256,256]{1,0:T(8,128)(2,1)S(1)}, u32[]{:S(2)}, u32[]{:S(2)}) %collective-permute-start.11) | collective-permute-done | bytes 131104 | tf_op jit(solution)/shard_map/ppermute | solution.py:137
  70.4 2.1 %collective-permute-done.14 = f16[256,256]{1,0:T(8,128)(2,1)S(1)} collective-permute-done((f16[256,256]{1,0:T(8,128)(2,1)S(1)}, f16[256,256]{1,0:T(8,128)(2,1)S(1)}, u32[]{:S(2)}, u32[]{:S(2)}) %collective-permute-start.14) | collective-permute-done | bytes 131104 | tf_op jit(solution)/shard_map/ppermute | solution.py:137
  72.5 1.4 collective-permute-done.15
  76.0 1.6 %collective-permute-start.17 = (f32[4,512]{1,0:T(4,128)S(1)}, f32[4,512]{1,0:T(4,128)S(1)}, u32[]{:S(2)}, u32[]{:S(2)}) collective-permute-start(f32[4,512]{1,0:T(4,128)S(1)} %fusion.18), channel_id=1, source_target_pairs={{0,1},{1,0},{2,3},{3,2},{4,5},{5,4},{6,7},{7,6},{8,9},{9,8},{10,11... | collective-permute-start | bytes 24584 | tf_op jit(solution)/shard_map/ppermute | solution.py:151
  77.6 1.2 collective-permute-start.18
  79.7 1.8 %copy.28 = f32[256,2,512]{2,1,0:T(2,128)} copy(f32[256,2,512]{2,0,1:T(8,128)S(1)} %pad_maximum_fusion.1) | data formatting | bytes 2097152 | tf_op jit(solution)/shard_map/stack | solution.py:257
  81.4 1.9 %collective-permute-done.19 = f32[4,512]{1,0:T(4,128)S(1)} collective-permute-done((f32[4,512]{1,0:T(4,128)S(1)}, f32[4,512]{1,0:T(4,128)S(1)}, u32[]{:S(2)}, u32[]{:S(2)}) %collective-permute-start.19) | collective-permute-done | bytes 8224 | tf_op jit(solution)/shard_map/ppermute | solution.py:151
  83.4 3.2 %collective-permute-start.21 = (f32[4,512]{1,0:T(4,128)S(1)}, f32[4,512]{1,0:T(4,128)S(1)}, u32[]{:S(2)}, u32[]{:S(2)}) collective-permute-start(f32[4,512]{1,0:T(4,128)S(1)} %add_add_fusion), channel_id=1, source_target_pairs={{0,16},{1,17},{2,18},{3,19},{4,20},{5,21},{6,22},{7,23},{8,24},{9,... | collective-permute-start | bytes 24584 | tf_op jit(solution)/shard_map/ppermute | solution.py:151
  86.6 1.2 collective-permute-start.22
  87.9 1.8 %copy.29 = f32[256,2,512]{2,1,0:T(2,128)} copy(f32[256,2,512]{2,0,1:T(8,128)S(1)} %pad_maximum_fusion.2) | data formatting | bytes 2097152 | tf_op jit(solution)/shard_map/stack | solution.py:257
  89.7 2.4 %collective-permute-done.22 = f32[4,512]{1,0:T(4,128)S(1)} collective-permute-done((f32[4,512]{1,0:T(4,128)S(1)}, f32[4,512]{1,0:T(4,128)S(1)}, u32[]{:S(2)}, u32[]{:S(2)}) %collective-permute-start.22) | collective-permute-done | bytes 8224 | tf_op jit(solution)/shard_map/ppermute | solution.py:151
  93.3 2.9 %collective-permute-start.25 = (bf16[256,256]{1,0:T(8,128)(2,1)S(1)}, bf16[256,256]{1,0:T(8,128)(2,1)S(1)}, u32[]{:S(2)}, u32[]{:S(2)}) collective-permute-start(bf16[256,256]{1,0:T(8,128)(2,1)S(1)} %get-tuple-element.152), channel_id=1, source_target_pairs={{0,16},{2,18},{4,20},{6,22},{8,24},{10,26},{12,28},{14,30},{16,0},... | collective-permute-start | bytes 393224 | tf_op jit(solution)/shard_map/ppermute | solution.py:137
  96.2 5.8 %collective-permute-done.26 = bf16[256,256]{1,0:T(8,128)(2,1)S(1)} collective-permute-done((bf16[256,256]{1,0:T(8,128)(2,1)S(1)}, bf16[256,256]{1,0:T(8,128)(2,1)S(1)}, u32[]{:S(2)}, u32[]{:S(2)}) %collective-permute-start.26) | collective-permute-done | bytes 131104 | tf_op jit(solution)/shard_map/ppermute | solution.py:137
  102.1 1.3 collective-permute-done.25
  103.5 1.2 collective-permute-start.27
  104.7 1.7 %collective-permute-start.24 = (bf16[256,256]{1,0:T(8,128)(2,1)S(1)}, bf16[256,256]{1,0:T(8,128)(2,1)S(1)}, u32[]{:S(2)}, u32[]{:S(2)}) collective-permute-start(bf16[256,256]{1,0:T(8,128)(2,1)S(1)} %get-tuple-element.153), channel_id=1, source_target_pairs={{0,16},{2,18},{4,20},{6,22},{8,24},{10,26},{12,28},{14,30},{16,0},... | collective-permute-start | bytes 393224 | tf_op jit(solution)/shard_map/ppermute | solution.py:137
  106.3 1.3 collective-permute-start.23
  107.7 3.6 %collective-permute-done.28 = bf16[512,256]{1,0:T(8,128)(2,1)S(1)} collective-permute-done((bf16[512,256]{1,0:T(8,128)(2,1)S(1)}, bf16[512,256]{1,0:T(8,128)(2,1)S(1)}, u32[]{:S(2)}, u32[]{:S(2)}) %collective-permute-start.28) | collective-permute-done | bytes 262176 | tf_op jit(solution)/shard_map/ppermute | solution.py:137
  111.3 1.4 collective-permute-start.29
  112.7 3.6 %collective-permute-done.24 = bf16[256,256]{1,0:T(8,128)(2,1)S(1)} collective-permute-done((bf16[256,256]{1,0:T(8,128)(2,1)S(1)}, bf16[256,256]{1,0:T(8,128)(2,1)S(1)}, u32[]{:S(2)}, u32[]{:S(2)}) %collective-permute-start.24) | collective-permute-done | bytes 131104 | tf_op jit(solution)/shard_map/ppermute | solution.py:137
  117.0 2.1 %collective-permute-start.33 = (bf16[1024,256]{1,0:T(8,128)(2,1)S(1)}, bf16[1024,256]{1,0:T(8,128)(2,1)S(1)}, u32[]{:S(2)}, u32[]{:S(2)}) collective-permute-start(bf16[1024,256]{1,0:T(8,128)(2,1)S(1)} %pad_maximum_fusion.15.refs_1_), channel_id=1, source_target_pairs={{0,8},{2,10},{4,12},{6,14},{8,0},{10,2},{12,4},{14,6},{16,24},{18,... | collective-permute-start | bytes 1572872 | tf_op jit(solution)/shard_map/ppermute | solution.py:137
  119.1 1.1 collective-permute-start.30
  120.3 1.8 %copy.30 = f32[256,2,512]{2,1,0:T(2,128)} copy(f32[256,2,512]{2,0,1:T(8,128)S(1)} %pad_maximum_fusion.3) | data formatting | bytes 2097152 | tf_op jit(solution)/shard_map/stack | solution.py:266
  122.1 3.6 %collective-permute-done.31 = bf16[512,256]{1,0:T(8,128)(2,1)S(1)} collective-permute-done((bf16[512,256]{1,0:T(8,128)(2,1)S(1)}, bf16[512,256]{1,0:T(8,128)(2,1)S(1)}, u32[]{:S(2)}, u32[]{:S(2)}) %collective-permute-start.31) | collective-permute-done | bytes 262176 | tf_op jit(solution)/shard_map/ppermute | solution.py:137
  125.7 1.5 collective-permute-done.30
  127.4 4.2 %collective-permute-done.33.refs_1_ = bf16[1024,256]{1,0:T(8,128)(2,1)S(1)} collective-permute-done((bf16[1024,256]{1,0:T(8,128)(2,1)S(1)}, bf16[1024,256]{1,0:T(8,128)(2,1)S(1)}, u32[]{:S(2)}, u32[]{:S(2)}) %collective-permute-start.33) | collective-permute-done | bytes 524320 | tf_op jit(solution)/shard_map/ppermute | solution.py:137
  133.8 1.8 %shard_map.108 = bf16[768,256]{1,0:T(8,128)(2,1)S(1)} custom-call(bf16[768,1024]{1,0:T(8,128)(2,1)S(1)} %get-tuple-element.67.refs_0_, bf16[1024,256]{1,0:T(8,128)(2,1)S(1)} %collective-permute-done.29.refs_1_, bf16[768,1024]{1,0:T(8,128)(2,1)S(1)} %get-tuple-element.63.refs_2_.refs_0_, bf16[1024,256]{1,0:T(8,128)(2,1)S(1)} %get-tuple-element.140.refs_3_, ...), custom_call_target="tpu_custom_call" | custom-call | tf_op jit(solution)/shard_map/pallas_call | solution.py:110
  137.5 1.3 shard_map.111
  140.6 5.4 %collective-permute-done.35.refs_1_ = bf16[1024,256]{1,0:T(8,128)(2,1)S(1)} collective-permute-done((bf16[1024,256]{1,0:T(8,128)(2,1)S(1)}, bf16[1024,256]{1,0:T(8,128)(2,1)S(1)}, u32[]{:S(2)}, u32[]{:S(2)}) %collective-permute-start.35) | collective-permute-done | bytes 524320 | tf_op jit(solution)/shard_map/ppermute | solution.py:137
  148.9 1.3 shard_map.116
  150.4 1.3 shard_map.117
  152.0 2.4 %reshape.311 = bf16[768,2,512]{2,1,0:T(2,128)(2,1)} reshape(bf16[768,1024]{1,0:T(8,128)(2,1)S(1)} %pad_maximum_fusion) | data formatting | bytes 3145728 | tf_op jit(solution)/shard_map/reshape | solution.py:308
  (133 shorter events, 29.3 us)
Async XLA Ops:
  0.6 4.4 %copy-start = (bf16[768,4096]{1,0:T(8,128)(2,1)S(1)}, bf16[768,4096]{1,0:T(8,128)(2,1)}, u32[]{:S(2)}) copy-start(bf16[768,4096]{1,0:T(8,128)(2,1)} %src.3) | copy-start | bytes 18874372
  2.6 2.4 %collective-permute-start = (bf16[768,512]{1,0:T(8,128)(2,1)S(1)}, bf16[768,512]{1,0:T(8,128)(2,1)S(1)}, u32[]{:S(2)}, u32[]{:S(2)}) collective-permute-start(bf16[768,512]{1,0:T(8,128)(2,1)S(1)} %get-tuple-element.69), channel_id=1, source_target_pairs={{0,2},{2,0},{4,6},{6,4},{8,10},{10,8},{12,14},{14,12},{16,18},{18,... | collective-permute-start | bytes 2359304 | tf_op jit(solution)/shard_map/ppermute | solution.py:137
  6.0 3.5 %collective-permute-start.1 = (bf16[768,1024]{1,0:T(8,128)(2,1)S(1)}, bf16[768,1024]{1,0:T(8,128)(2,1)S(1)}, u32[]{:S(2)}, u32[]{:S(2)}) collective-permute-start(bf16[768,1024]{1,0:T(8,128)(2,1)S(1)} %get-tuple-element.64.refs_4_.refs_2_), channel_id=1, source_target_pairs={{0,2},{2,0},{4,6},{6,4},{8,10},{10,8},{12,14},{14,12},{16,18},{18,... | collective-permute-start | bytes 4718600 | tf_op jit(solution)/shard_map/ppermute | solution.py:137
  6.5 5.3 %collective-permute-start.2 = (bf16[768,1024]{1,0:T(8,128)(2,1)S(1)}, bf16[768,1024]{1,0:T(8,128)(2,1)S(1)}, u32[]{:S(2)}, u32[]{:S(2)}) collective-permute-start(bf16[768,1024]{1,0:T(8,128)(2,1)S(1)} %get-tuple-element.63.refs_2_.refs_0_), channel_id=1, source_target_pairs={{0,2},{2,0},{4,6},{6,4},{8,10},{10,8},{12,14},{14,12},{16,18},{18,... | collective-permute-start | bytes 4718600 | tf_op jit(solution)/shard_map/ppermute | solution.py:137
  13.1 5.7 %collective-permute-start.4 = (bf16[768,512]{1,0:T(8,128)(2,1)S(1)}, bf16[768,512]{1,0:T(8,128)(2,1)S(1)}, u32[]{:S(2)}, u32[]{:S(2)}) collective-permute-start(bf16[768,512]{1,0:T(8,128)(2,1)S(1)} %get-tuple-element.71.refs_1_), channel_id=1, source_target_pairs={{0,2},{2,0},{4,6},{6,4},{8,10},{10,8},{12,14},{14,12},{16,18},{18,... | collective-permute-start | bytes 2359304 | tf_op jit(solution)/shard_map/ppermute | solution.py:137
  13.7 15.2 %collective-permute-start.3 = (f16[1024,256]{1,0:T(8,128)(2,1)S(1)}, f16[1024,256]{1,0:T(8,128)(2,1)S(1)}, u32[]{:S(2)}, u32[]{:S(2)}) collective-permute-start(f16[1024,256]{1,0:T(8,128)(2,1)S(1)} %slice.218), channel_id=1, source_target_pairs={{0,4},{2,6},{4,0},{6,2},{8,12},{10,14},{12,8},{14,10},{16,20},{18,... | collective-permute-start | bytes 1572872 | tf_op jit(solution)/shard_map/ppermute | solution.py:137
  17.2 16.0 %collective-permute-start.8 = (f16[1024,256]{1,0:T(8,128)(2,1)S(1)}, f16[1024,256]{1,0:T(8,128)(2,1)S(1)}, u32[]{:S(2)}, u32[]{:S(2)}) collective-permute-start(f16[1024,256]{1,0:T(8,128)(2,1)S(1)} %pad_maximum_fusion.8), channel_id=1, source_target_pairs={{0,8},{2,10},{4,12},{6,14},{8,0},{10,2},{12,4},{14,6},{16,24},{18,... | collective-permute-start | bytes 1572872 | tf_op jit(solution)/shard_map/ppermute | solution.py:137
  24.5 24.3 %collective-permute-start.6 = (f16[1024,256]{1,0:T(8,128)(2,1)S(1)}, f16[1024,256]{1,0:T(8,128)(2,1)S(1)}, u32[]{:S(2)}, u32[]{:S(2)}) collective-permute-start(f16[1024,256]{1,0:T(8,128)(2,1)S(1)} %pad_maximum_fusion.9), channel_id=1, source_target_pairs={{0,8},{2,10},{4,12},{6,14},{8,0},{10,2},{12,4},{14,6},{16,24},{18,... | collective-permute-start | bytes 1572872 | tf_op jit(solution)/shard_map/ppermute | solution.py:137
  29.1 21.6 %collective-permute-start.5 = (f16[512,256]{1,0:T(8,128)(2,1)S(1)}, f16[512,256]{1,0:T(8,128)(2,1)S(1)}, u32[]{:S(2)}, u32[]{:S(2)}) collective-permute-start(f16[512,256]{1,0:T(8,128)(2,1)S(1)} %slice_convert_fusion.3), channel_id=1, source_target_pairs={{0,8},{2,10},{4,12},{6,14},{8,0},{10,2},{12,4},{14,6},{16,24},{18,... | collective-permute-start | bytes 786440 | tf_op jit(solution)/shard_map/ppermute | solution.py:137
  33.2 2.4 %copy-start.2 = (f32[256,2,512]{2,1,0:T(2,128)S(1)}, f32[256,2,512]{2,1,0:T(2,128)}, u32[]{:S(2)}) copy-start(f32[256,2,512]{2,1,0:T(2,128)} %param.9) | copy-start | bytes 3145732
  33.2 14.9 %collective-permute-start.7 = (f16[1024,256]{1,0:T(8,128)(2,1)S(1)}, f16[1024,256]{1,0:T(8,128)(2,1)S(1)}, u32[]{:S(2)}, u32[]{:S(2)}) collective-permute-start(f16[1024,256]{1,0:T(8,128)(2,1)S(1)} %slice.229), channel_id=1, source_target_pairs={{0,4},{2,6},{4,0},{6,2},{8,12},{10,14},{12,8},{14,10},{16,20},{18,... | collective-permute-start | bytes 1572872 | tf_op jit(solution)/shard_map/ppermute | solution.py:137
  34.9 1.2 copy-start.3
  34.9 1.5 copy-start.1
  34.9 18.8 %collective-permute-start.10 = (f16[512,256]{1,0:T(8,128)(2,1)S(1)}, f16[512,256]{1,0:T(8,128)(2,1)S(1)}, u32[]{:S(2)}, u32[]{:S(2)}) collective-permute-start(f16[512,256]{1,0:T(8,128)(2,1)S(1)} %slice_convert_fusion.2), channel_id=1, source_target_pairs={{0,4},{2,6},{4,0},{6,2},{8,12},{10,14},{12,8},{14,10},{16,20},{18,... | collective-permute-start | bytes 786440 | tf_op jit(solution)/shard_map/ppermute | solution.py:137
  48.4 8.1 %collective-permute-start.13 = (f16[512,256]{1,0:T(8,128)(2,1)S(1)}, f16[512,256]{1,0:T(8,128)(2,1)S(1)}, u32[]{:S(2)}, u32[]{:S(2)}) collective-permute-start(f16[512,256]{1,0:T(8,128)(2,1)S(1)} %slice_convert_fusion.1), channel_id=1, source_target_pairs={{0,8},{2,10},{4,12},{6,14},{8,0},{10,2},{12,4},{14,6},{16,24},{18,... | collective-permute-start | bytes 786440 | tf_op jit(solution)/shard_map/ppermute | solution.py:137
  49.0 11.5 %collective-permute-start.12 = (f16[512,256]{1,0:T(8,128)(2,1)S(1)}, f16[512,256]{1,0:T(8,128)(2,1)S(1)}, u32[]{:S(2)}, u32[]{:S(2)}) collective-permute-start(f16[512,256]{1,0:T(8,128)(2,1)S(1)} %slice_convert_fusion), channel_id=1, source_target_pairs={{0,4},{2,6},{4,0},{6,2},{8,12},{10,14},{12,8},{14,10},{16,20},{18,... | collective-permute-start | bytes 786440 | tf_op jit(solution)/shard_map/ppermute | solution.py:137
  50.8 19.6 %collective-permute-start.9 = (f16[256,256]{1,0:T(8,128)(2,1)S(1)}, f16[256,256]{1,0:T(8,128)(2,1)S(1)}, u32[]{:S(2)}, u32[]{:S(2)}) collective-permute-start(f16[256,256]{1,0:T(8,128)(2,1)S(1)} %slice_convert_fusion.9), channel_id=1, source_target_pairs={{0,16},{2,18},{4,20},{6,22},{8,24},{10,26},{12,28},{14,30},{16,0},... | collective-permute-start | bytes 393224 | tf_op jit(solution)/shard_map/ppermute | solution.py:137
  53.8 16.5 %collective-permute-start.11 = (f16[256,256]{1,0:T(8,128)(2,1)S(1)}, f16[256,256]{1,0:T(8,128)(2,1)S(1)}, u32[]{:S(2)}, u32[]{:S(2)}) collective-permute-start(f16[256,256]{1,0:T(8,128)(2,1)S(1)} %slice_convert_fusion.8), channel_id=1, source_target_pairs={{0,16},{2,18},{4,20},{6,22},{8,24},{10,26},{12,28},{14,30},{16,0},... | collective-permute-start | bytes 393224 | tf_op jit(solution)/shard_map/ppermute | solution.py:137
  56.6 15.9 %collective-permute-start.14 = (f16[256,256]{1,0:T(8,128)(2,1)S(1)}, f16[256,256]{1,0:T(8,128)(2,1)S(1)}, u32[]{:S(2)}, u32[]{:S(2)}) collective-permute-start(f16[256,256]{1,0:T(8,128)(2,1)S(1)} %slice_convert_fusion.7), channel_id=1, source_target_pairs={{0,16},{2,18},{4,20},{6,22},{8,24},{10,26},{12,28},{14,30},{16,0},... | collective-permute-start | bytes 393224 | tf_op jit(solution)/shard_map/ppermute | solution.py:137
  60.5 13.3 %collective-permute-start.15 = (f16[256,256]{1,0:T(8,128)(2,1)S(1)}, f16[256,256]{1,0:T(8,128)(2,1)S(1)}, u32[]{:S(2)}, u32[]{:S(2)}) collective-permute-start(f16[256,256]{1,0:T(8,128)(2,1)S(1)} %slice_convert_fusion.6), channel_id=1, source_target_pairs={{0,16},{2,18},{4,20},{6,22},{8,24},{10,26},{12,28},{14,30},{16,0},... | collective-permute-start | bytes 393224 | tf_op jit(solution)/shard_map/ppermute | solution.py:137
  74.7 1.2 collective-permute-start.16
  76.0 5.4 %collective-permute-start.17 = (f32[4,512]{1,0:T(4,128)S(1)}, f32[4,512]{1,0:T(4,128)S(1)}, u32[]{:S(2)}, u32[]{:S(2)}) collective-permute-start(f32[4,512]{1,0:T(4,128)S(1)} %fusion.18), channel_id=1, source_target_pairs={{0,1},{1,0},{2,3},{3,2},{4,5},{5,4},{6,7},{7,6},{8,9},{9,8},{10,11... | collective-permute-start | bytes 24584 | tf_op jit(solution)/shard_map/ppermute | solution.py:151
  77.6 3.9 %collective-permute-start.18 = (f32[4,512]{1,0:T(4,128)S(1)}, f32[4,512]{1,0:T(4,128)S(1)}, u32[]{:S(2)}, u32[]{:S(2)}) collective-permute-start(f32[4,512]{1,0:T(4,128)S(1)} %fusion.18), channel_id=1, source_target_pairs={{0,4},{1,5},{2,6},{3,7},{4,0},{5,1},{6,2},{7,3},{8,12},{9,13},{10,... | collective-permute-start | bytes 24584 | tf_op jit(solution)/shard_map/ppermute | solution.py:151
  78.8 4.5 %collective-permute-start.19 = (f32[4,512]{1,0:T(4,128)S(1)}, f32[4,512]{1,0:T(4,128)S(1)}, u32[]{:S(2)}, u32[]{:S(2)}) collective-permute-start(f32[4,512]{1,0:T(4,128)S(1)} %fusion.18), channel_id=1, source_target_pairs={{0,5},{1,4},{2,7},{3,6},{4,1},{5,0},{6,3},{7,2},{8,13},{9,12},{10,... | collective-permute-start | bytes 24584 | tf_op jit(solution)/shard_map/ppermute | solution.py:151
  83.4 6.3 %collective-permute-start.20 = (f32[4,512]{1,0:T(4,128)S(1)}, f32[4,512]{1,0:T(4,128)S(1)}, u32[]{:S(2)}, u32[]{:S(2)}) collective-permute-start(f32[4,512]{1,0:T(4,128)S(1)} %add_add_fusion), channel_id=1, source_target_pairs={{0,8},{1,9},{2,10},{3,11},{4,12},{5,13},{6,14},{7,15},{8,0},{9,1},... | collective-permute-start | bytes 24584 | tf_op jit(solution)/shard_map/ppermute | solution.py:151
  83.4 6.2 %collective-permute-start.21 = (f32[4,512]{1,0:T(4,128)S(1)}, f32[4,512]{1,0:T(4,128)S(1)}, u32[]{:S(2)}, u32[]{:S(2)}) collective-permute-start(f32[4,512]{1,0:T(4,128)S(1)} %add_add_fusion), channel_id=1, source_target_pairs={{0,16},{1,17},{2,18},{3,19},{4,20},{5,21},{6,22},{7,23},{8,24},{9,... | collective-permute-start | bytes 24584 | tf_op jit(solution)/shard_map/ppermute | solution.py:151
  86.6 5.5 %collective-permute-start.22 = (f32[4,512]{1,0:T(4,128)S(1)}, f32[4,512]{1,0:T(4,128)S(1)}, u32[]{:S(2)}, u32[]{:S(2)}) collective-permute-start(f32[4,512]{1,0:T(4,128)S(1)} %add_add_fusion), channel_id=1, source_target_pairs={{0,24},{1,25},{2,26},{3,27},{4,28},{5,29},{6,30},{7,31},{8,16},{9,... | collective-permute-start | bytes 24584 | tf_op jit(solution)/shard_map/ppermute | solution.py:151
  93.2 8.8 %collective-permute-start.26 = (bf16[256,256]{1,0:T(8,128)(2,1)S(1)}, bf16[256,256]{1,0:T(8,128)(2,1)S(1)}, u32[]{:S(2)}, u32[]{:S(2)}) collective-permute-start(bf16[256,256]{1,0:T(8,128)(2,1)S(1)} %get-tuple-element.151), channel_id=1, source_target_pairs={{0,16},{2,18},{4,20},{6,22},{8,24},{10,26},{12,28},{14,30},{16,0},... | collective-permute-start | bytes 393224 | tf_op jit(solution)/shard_map/ppermute | solution.py:137
  93.3 10.2 %collective-permute-start.25 = (bf16[256,256]{1,0:T(8,128)(2,1)S(1)}, bf16[256,256]{1,0:T(8,128)(2,1)S(1)}, u32[]{:S(2)}, u32[]{:S(2)}) collective-permute-start(bf16[256,256]{1,0:T(8,128)(2,1)S(1)} %get-tuple-element.152), channel_id=1, source_target_pairs={{0,16},{2,18},{4,20},{6,22},{8,24},{10,26},{12,28},{14,30},{16,0},... | collective-permute-start | bytes 393224 | tf_op jit(solution)/shard_map/ppermute | solution.py:137
  102.1 9.2 %collective-permute-start.28 = (bf16[512,256]{1,0:T(8,128)(2,1)S(1)}, bf16[512,256]{1,0:T(8,128)(2,1)S(1)}, u32[]{:S(2)}, u32[]{:S(2)}) collective-permute-start(bf16[512,256]{1,0:T(8,128)(2,1)S(1)} %pad_maximum_fusion.18), channel_id=1, source_target_pairs={{0,8},{2,10},{4,12},{6,14},{8,0},{10,2},{12,4},{14,6},{16,24},{18,... | collective-permute-start | bytes 786440 | tf_op jit(solution)/shard_map/ppermute | solution.py:137
  103.5 9.2 %collective-permute-start.27 = (bf16[512,256]{1,0:T(8,128)(2,1)S(1)}, bf16[512,256]{1,0:T(8,128)(2,1)S(1)}, u32[]{:S(2)}, u32[]{:S(2)}) collective-permute-start(bf16[512,256]{1,0:T(8,128)(2,1)S(1)} %pad_maximum_fusion.19), channel_id=1, source_target_pairs={{0,4},{2,6},{4,0},{6,2},{8,12},{10,14},{12,8},{14,10},{16,20},{18,... | collective-permute-start | bytes 786440 | tf_op jit(solution)/shard_map/ppermute | solution.py:137
  104.7 11.7 %collective-permute-start.24 = (bf16[256,256]{1,0:T(8,128)(2,1)S(1)}, bf16[256,256]{1,0:T(8,128)(2,1)S(1)}, u32[]{:S(2)}, u32[]{:S(2)}) collective-permute-start(bf16[256,256]{1,0:T(8,128)(2,1)S(1)} %get-tuple-element.153), channel_id=1, source_target_pairs={{0,16},{2,18},{4,20},{6,22},{8,24},{10,26},{12,28},{14,30},{16,0},... | collective-permute-start | bytes 393224 | tf_op jit(solution)/shard_map/ppermute | solution.py:137
  106.3 12.7 %collective-permute-start.23 = (bf16[256,256]{1,0:T(8,128)(2,1)S(1)}, bf16[256,256]{1,0:T(8,128)(2,1)S(1)}, u32[]{:S(2)}, u32[]{:S(2)}) collective-permute-start(bf16[256,256]{1,0:T(8,128)(2,1)S(1)} %get-tuple-element.154), channel_id=1, source_target_pairs={{0,16},{2,18},{4,20},{6,22},{8,24},{10,26},{12,28},{14,30},{16,0},... | collective-permute-start | bytes 393224 | tf_op jit(solution)/shard_map/ppermute | solution.py:137
  111.3 15.9 %collective-permute-start.29 = (bf16[1024,256]{1,0:T(8,128)(2,1)S(1)}, bf16[1024,256]{1,0:T(8,128)(2,1)S(1)}, u32[]{:S(2)}, u32[]{:S(2)}) collective-permute-start(bf16[1024,256]{1,0:T(8,128)(2,1)S(1)} %pad_maximum_fusion.14.refs_1_), channel_id=1, source_target_pairs={{0,4},{2,6},{4,0},{6,2},{8,12},{10,14},{12,8},{14,10},{16,20},{18,... | collective-permute-start | bytes 1572872 | tf_op jit(solution)/shard_map/ppermute | solution.py:137
  116.3 9.3 %collective-permute-start.31 = (bf16[512,256]{1,0:T(8,128)(2,1)S(1)}, bf16[512,256]{1,0:T(8,128)(2,1)S(1)}, u32[]{:S(2)}, u32[]{:S(2)}) collective-permute-start(bf16[512,256]{1,0:T(8,128)(2,1)S(1)} %pad_maximum_fusion.20), channel_id=1, source_target_pairs={{0,8},{2,10},{4,12},{6,14},{8,0},{10,2},{12,4},{14,6},{16,24},{18,... | collective-permute-start | bytes 786440 | tf_op jit(solution)/shard_map/ppermute | solution.py:137
  117.0 14.6 %collective-permute-start.33 = (bf16[1024,256]{1,0:T(8,128)(2,1)S(1)}, bf16[1024,256]{1,0:T(8,128)(2,1)S(1)}, u32[]{:S(2)}, u32[]{:S(2)}) collective-permute-start(bf16[1024,256]{1,0:T(8,128)(2,1)S(1)} %pad_maximum_fusion.15.refs_1_), channel_id=1, source_target_pairs={{0,8},{2,10},{4,12},{6,14},{8,0},{10,2},{12,4},{14,6},{16,24},{18,... | collective-permute-start | bytes 1572872 | tf_op jit(solution)/shard_map/ppermute | solution.py:137
  119.1 8.1 %collective-permute-start.30 = (bf16[512,256]{1,0:T(8,128)(2,1)S(1)}, bf16[512,256]{1,0:T(8,128)(2,1)S(1)}, u32[]{:S(2)}, u32[]{:S(2)}) collective-permute-start(bf16[512,256]{1,0:T(8,128)(2,1)S(1)} %pad_maximum_fusion.21), channel_id=1, source_target_pairs={{0,4},{2,6},{4,0},{6,2},{8,12},{10,14},{12,8},{14,10},{16,20},{18,... | collective-permute-start | bytes 786440 | tf_op jit(solution)/shard_map/ppermute | solution.py:137
  127.3 6.4 %collective-permute-start.32 = (bf16[2048,256]{1,0:T(8,128)(2,1)S(1)}, bf16[2048,256]{1,0:T(8,128)(2,1)S(1)}, u32[]{:S(2)}, u32[]{:S(2)}) collective-permute-start(bf16[2048,256]{1,0:T(8,128)(2,1)S(1)} %pad_maximum_fusion.4), channel_id=1, source_target_pairs={{0,2},{2,0},{4,6},{6,4},{8,10},{10,8},{12,14},{14,12},{16,18},{18,... | collective-permute-start | bytes 3145736 | tf_op jit(solution)/shard_map/ppermute | solution.py:137
  131.6 5.7 %collective-permute-start.34 = (bf16[2048,256]{1,0:T(8,128)(2,1)S(1)}, bf16[2048,256]{1,0:T(8,128)(2,1)S(1)}, u32[]{:S(2)}, u32[]{:S(2)}) collective-permute-start(bf16[2048,256]{1,0:T(8,128)(2,1)S(1)} %pad_maximum_fusion.5), channel_id=1, source_target_pairs={{0,2},{2,0},{4,6},{6,4},{8,10},{10,8},{12,14},{14,12},{16,18},{18,... | collective-permute-start | bytes 3145736 | tf_op jit(solution)/shard_map/ppermute | solution.py:137
  131.7 14.3 %collective-permute-start.35 = (bf16[1024,256]{1,0:T(8,128)(2,1)S(1)}, bf16[1024,256]{1,0:T(8,128)(2,1)S(1)}, u32[]{:S(2)}, u32[]{:S(2)}) collective-permute-start(bf16[1024,256]{1,0:T(8,128)(2,1)S(1)} %pad_maximum_fusion.16.refs_1_), channel_id=1, source_target_pairs={{0,4},{2,6},{4,0},{6,2},{8,12},{10,14},{12,8},{14,10},{16,20},{18,... | collective-permute-start | bytes 1572872 | tf_op jit(solution)/shard_map/ppermute | solution.py:137
  132.8 14.0 %collective-permute-start.37 = (bf16[1024,256]{1,0:T(8,128)(2,1)S(1)}, bf16[1024,256]{1,0:T(8,128)(2,1)S(1)}, u32[]{:S(2)}, u32[]{:S(2)}) collective-permute-start(bf16[1024,256]{1,0:T(8,128)(2,1)S(1)} %pad_maximum_fusion.17.refs_1_), channel_id=1, source_target_pairs={{0,8},{2,10},{4,12},{6,14},{8,0},{10,2},{12,4},{14,6},{16,24},{18,... | collective-permute-start | bytes 1572872 | tf_op jit(solution)/shard_map/ppermute | solution.py:137
  146.1 2.7 %collective-permute-start.36 = (bf16[2048,256]{1,0:T(8,128)(2,1)S(1)}, bf16[2048,256]{1,0:T(8,128)(2,1)S(1)}, u32[]{:S(2)}, u32[]{:S(2)}) collective-permute-start(bf16[2048,256]{1,0:T(8,128)(2,1)S(1)} %pad_maximum_fusion.6), channel_id=1, source_target_pairs={{0,2},{2,0},{4,6},{6,4},{8,10},{10,8},{12,14},{14,12},{16,18},{18,... | collective-permute-start | bytes 3145736 | tf_op jit(solution)/shard_map/ppermute | solution.py:137
  146.8 3.5 %collective-permute-start.38 = (bf16[2048,256]{1,0:T(8,128)(2,1)S(1)}, bf16[2048,256]{1,0:T(8,128)(2,1)S(1)}, u32[]{:S(2)}, u32[]{:S(2)}) collective-permute-start(bf16[2048,256]{1,0:T(8,128)(2,1)S(1)} %pad_maximum_fusion.7), channel_id=1, source_target_pairs={{0,2},{2,0},{4,6},{6,4},{8,10},{10,8},{12,14},{14,12},{16,18},{18,... | collective-permute-start | bytes 3145736 | tf_op jit(solution)/shard_map/ppermute | solution.py:137

commit v4 on v3

--- a/solution.py
+++ b/solution.py
@@ -10,6 +10,7 @@
 
 F32 = jnp.float32
 LANES = 128
+PLAIN = (2, 3)
 PICK_MIB = 6
 DOT_MIB = 8
 SUM_CHUNKS = ((0, 0, 2, 0), (0, 2, 4, 1), (1, 0, 2, 0), (1, 2, 4, 1))
@@ -17,18 +18,22 @@
 
 
 def sums_plan(deep):
-    plan = [("P", 0, 0), ("S", 0, 0), ("S", 1, 0), ("P", 1, 0), ("S", 2, 0), ("S", 3, 0)]
-    plan += [("T", i, depth) for depth in range(deep - 1) for i in range(len(SUM_CHUNKS))]
-    return plan + [("T", i, deep - 1) for i in (1, 0, 2, 3)]
+    plan = [("P", 0, 1), ("P", 0, 0), ("S", 0, 0), ("S", 1, 0), ("P", 1, 1), ("S", 2, 0), ("P", 1, 0), ("W", 0, 0)]
+    plan += [("T", 0, 0), ("S", 3, 0), ("T", 1, 0)]
+    for depth in range(1, deep):
+        first = [("T", 0, depth), ("T", 1, depth)]
+        second = [("T", 2, depth - 1), ("T", 3, depth - 1)]
+        plan += [x for pair in zip(first, second) for x in pair] if depth == 1 else second + first
+    return plan + [("T", 2, deep - 1), ("T", 3, deep - 1)]
 
 
 def gathers_plan(deep):
     last = deep - 1
-    plan = [("G", 0, 0), ("G", 1, 0), ("J", 0, last), ("J", 1, last), ("G", 2, 0), ("G", 3, 0)]
+    plan = [("G", 0, 0), ("O", 1, 0), ("G", 1, 0), ("J", 0, last), ("G", 2, 0), ("J", 1, last), ("G", 3, 0)]
     for depth in reversed(range(1, last)):
         plan += [("J", 0, depth), ("J", 1, depth), ("J", 2, depth + 1), ("J", 3, depth + 1)]
     plan += [("O", 0, 0), ("J", 2, 1), ("J", 3, 1), ("J", 0, 0), ("J", 1, 0)]
-    plan += [("H", 0, 0), ("K", 0, 0), ("H", 1, 0), ("M", 1, 0), ("K", 1, 0), ("H", 2, 0), ("H", 3, 0)]
+    plan += [("H", 0, 0), ("K", 0, 0), ("H", 1, 0), ("M", 1, 0), ("K", 1, 0), ("H", 2, 0), ("H", 3, 0), ("O", 2, 0)]
     return plan + [("J", 2, 0), ("J", 3, 0), ("M", 2, 0), ("M", 3, 0), ("K", 2, 0), ("K", 3, 0)]
 
 
@@ -136,7 +141,7 @@
     def swap(value, bit):
         return lax.ppermute(value, "dp", [(i, i ^ (1 << bit)) for i in range(n)])
 
-    def total(value, fillers):
+    def total(value):
         hops = [("dp", 1 << bit) for bit in range(bits)] + [("tensor", 1 << bit) for bit in range(t.bit_length() - 1)]
         hops = hops[:1] + [hop for pair in zip(hops[bits:], hops[1:bits]) for hop in pair] + [
             hop for hop in hops[1:] if hop not in [x for pair in zip(hops[bits:], hops[1:bits]) for x in pair]
@@ -150,12 +155,10 @@
             perm = [(i, ((i // t) ^ flip["dp"]) * t + ((i % t) ^ flip["tensor"])) for i in range(n * t)]
             return lax.ppermute(value, ("dp", "tensor"), perm)
 
-        for i, around in enumerate(rounds):
+        for around in rounds:
             others = [fetch(around[0])]
             if len(around) > 1:
                 others += [fetch(around[1]), fetch(*around)]
-            if i + len(fillers) >= len(rounds):
-                others[0] = after(others[0], fillers[i - len(rounds)])
             value = value + others[0]
             if len(around) > 1:
                 value = value + (others[1] + others[2])
@@ -188,40 +191,43 @@
         def gated(value):
             return after(value, last[0])
 
-        def product(s):
+        def product(s, side):
+            if len(sibling_out) <= s:
+                sibling_out.append(swap(gated(grad_out[s]), 0))
+            g = gated(grad_out[s])
+            pairs = [(mine[0][side], g), (sibling[side], sibling_out[s])]
             if s:
-                sibling_out.append(swap(gated(grad_out[s]), 0))
-            for side in (1, 0):
-                g = gated(grad_out[s])
-                pairs = [(mine[0][side], g), (sibling[side], sibling_out[s])]
-                if s:
-                    whole[s, side] = multiply(pairs, over_rows=True)
-                else:
-                    whole[s, side] = sum(dot_t(*pair) for pair in pairs)
-                last[0] = whole[s, side]
+                whole[s, side] = multiply(pairs, over_rows=True)
+            else:
+                whole[s, side] = sum(dot_t(*pair) for pair in pairs)
+            last[0] = whole[s, side]
 
         def halve(i, depth):
             order = orders[plans[i]]
             if depth == 0:
                 s, part = chunks[i]
-                low, high = (whole[s, side][:, part] for side in (0, 1))
                 if plans[i] == 0:
-                    keep, out = low, high
+                    out = whole[s, 1][:, part]
                 else:
-                    keep, out = (
+                    low, high = (whole[s, side][:, part] for side in (0, 1))
+                    held[i], out = (
                         jnp.concatenate(
                             [x.reshape(2, -1, x.shape[1])[side] for x in (low, high)], axis=0
                         )
                         for side in (0, 1)
                     )
             else:
-                keep, out = held[i].reshape(2, -1, held[i].shape[1])
+                held[i], out = held[i].reshape(2, -1, held[i].shape[1])
             out = out.astype(jnp.float16)
-            held[i] = keep
+            if depth == 0:
+                out = gated(out)
             got[i, depth] = swap(out, order[depth])
             last[0] = out
 
         def take(i, depth):
+            if depth == 0 and plans[i] == 0:
+                s, part = chunks[i]
+                held[i] = whole[s, 0][:, part]
             held[i] = held[i] + gated(got[i, depth]).astype(F32)
             if depth + 1 < deep:
                 halve(i, depth + 1)
@@ -230,19 +236,19 @@
 
         for kind, i, depth in sums_plan(deep):
             if kind == "P":
-                product(i)
+                product(i, depth)
             elif kind == "S":
                 halve(i, 0)
-            else:
+            elif kind == "T":
                 take(i, depth)
-                if depth == 0 and i == 0:
-                    weights, first_moment, second_moment = (
-                        gated(x) for x in (weights, first_moment, second_moment)
-                    )
-                    theirs.append(pick_blocks(gated(activations), [j + 1 for j in blocks_of(orders[1])], rows))
-                    last[0] = theirs[1][0]
-                    mine.append(pick_blocks(gated(activations), blocks_of(orders[1]), rows))
-                    last[0] = mine[1][0]
+            else:
+                weights, first_moment, second_moment = (
+                    gated(x) for x in (weights, first_moment, second_moment)
+                )
+                theirs.append(pick_blocks(gated(activations), [j + 1 for j in blocks_of(orders[1])], rows))
+                last[0] = theirs[1][0]
+                mine.append(pick_blocks(gated(activations), blocks_of(orders[1]), rows))
+                last[0] = mine[1][0]
 
         states, sums = [], []
         for s in range(kinds):
@@ -254,16 +260,16 @@
             states.append((first, second, update))
             sums.append(jnp.sum(update * update, axis=0))
         firsts, seconds, updates = zip(*states)
-        new_first, new_second = (rows_first(jnp.stack(x, axis=1)) for x in (firsts, seconds))
+        new_first, new_second = (jnp.stack(x, axis=1) for x in (firsts, seconds))
         weight_sq = jnp.sum(weights * weights, axis=0)
-        sums = total(jnp.concatenate([jnp.stack(sums), weight_sq], axis=0), [new_first, new_second])
+        sums = total(jnp.concatenate([jnp.stack(sums), weight_sq], axis=0))
         sums = jnp.sum(sums, axis=1, keepdims=True)
         ratios = jnp.sqrt(sums[kinds:]) / (jnp.sqrt(sums[:kinds]) + 1e-06)
         scales = lax.optimization_barrier(jnp.broadcast_to(0.05 * ratios, (kinds, cols)))
         ratios = ratios[:, 0]
         news = [weights[:, s] - scales[s][None, :] * updates[s] for s in range(kinds)]
         halves = [fresh.astype(jnp.bfloat16) for fresh in news]
-        new_weights = rows_first(jnp.stack(news, axis=1))
+        outs = [jnp.stack(news, axis=1), new_first, new_second]
 
         chunks = [(s, slice(low * cols // 4, high * cols // 4)) for s, low, high, _ in GATHER_CHUNKS]
         plans = [plan for *_, plan in GATHER_CHUNKS]
@@ -276,11 +282,11 @@
         for kind, i, depth in gathers_plan(deep):
             if kind == "G":
                 s, part = chunks[i]
-                gathered[i] = halves[s][:, part]
+                gathered[i] = gated(halves[s][:, part])
                 spread(i, deep - 1)
             elif kind == "O":
-                new_weights = gated(new_weights)
-                last[0] = new_weights
+                outs[i] = rows_first(gated(outs[i]))
+                last[0] = outs[i]
             elif kind == "J":
                 value = gated(arrived[i, depth])
                 if depth:
@@ -294,18 +300,24 @@
                 sums_of[i] = multiply([(mine[plans[i]][0], gated(gathered[i]))])
                 last[0] = sums_of[i]
             elif kind == "M":
-                sums_of[i] = multiply([(mine[plans[i]][1], gated(arrived[i, 0]))], sums_of[i])
+                if i in PLAIN:
+                    sums_of[i] = sums_of[i] + dot(mine[plans[i]][1], gated(arrived[i, 0]))
+                else:
+                    sums_of[i] = multiply([(mine[plans[i]][1], gated(arrived[i, 0]))], sums_of[i])
                 last[0] = sums_of[i]
                 added.add(i)
             else:
                 pairs = [] if i in added else [(mine[plans[i]][1], arrived[i, 0])]
                 sides = gated(other[i]).reshape(2, -1, other[i].shape[1])
                 pairs += [(theirs[plans[i]][side], sides[side]) for side in (0, 1)]
-                sums_of[i] = multiply(pairs, sums_of[i], dtype=jnp.bfloat16)
+                if i in PLAIN:
+                    sums_of[i] = sum((dot(*pair) for pair in pairs), sums_of[i]).astype(jnp.bfloat16)
+                else:
+                    sums_of[i] = multiply(pairs, sums_of[i], dtype=jnp.bfloat16)
                 last[0] = sums_of[i]
         places = sorted((s, part.start, i) for i, (s, part) in enumerate(chunks))
         new_kv = jnp.concatenate([sums_of[i] for *_, i in places], axis=1)
-        return (new_weights, new_first, new_second, ratios, new_kv.reshape(-1, kinds, cols))
+        return (*outs, ratios, new_kv.reshape(-1, kinds, cols))
 
     return local
 

time: 155 us -> 152 us (0.981)
  waiting for transfers between devices: 66.1 us -> 56.5 us
  other arithmetic: 6.14 us -> 12.1 us
  Pallas kernels: 21.4 us -> 16.9 us
  starting transfers between devices: 43.2 us -> 47.5 us
  matrix products: 4.05 us -> 7.53 us
  local copies, waits for them, and re-layouts: 11.5 us -> 9.32 us
    ppermute x32, waiting for transfers between devices: 60.9 us -> 48.9 us  [swap(): return lax.ppermute(value, 'dp', [(i, i ^ 1 << bit) for i in range(n)])]
    another operation x3 -> x0, local copies, waits for them, and re-layouts: 5.34 us -> none  [the longest x2 3.56 us: local(): jnp.stack(x, axis=1)]
    pallas_call x13 -> x9, Pallas kernels: 17.1 us -> 12.6 us  [multiply(): pl.pallas_call(kernel, out_shape=jax.ShapeDtypeStruct((height, wide), dty...]
    ppermute x32, starting transfers between devices: 35.1 us -> 39.4 us  [swap(): return lax.ppermute(value, 'dp', [(i, i ^ 1 << bit) for i in range(n)])]
    dot_general x0 -> x6, matrix products: none -> 3.48 us  [dot(): lax.dot_general(a, w, (((1,), (0,)), ((), ())), preferred_element_type=F32)]
    another operation x12, other arithmetic: 0.76 us -> 3.87 us  [the longest x1 3.2 us: local(): outs = [jnp.stack(news, axis=1), new_first, new_second]]
    sub x1 -> x2, other arithmetic: 0.56 us -> 3.37 us  [local(): weights[:, s] - scales[s][None, :] * updates[s]]
    ppermute x7, waiting for transfers between devices: 5.15 us -> 7.57 us  [fetch(): return lax.ppermute(value, ('dp', 'tensor'), perm)]
  transfers between devices with their start and end apart: 39 -> 39, of which waited for: 23 -> 22; matrix products, arithmetic and copies ran while one was open for 9% -> 13% of each run, Pallas kernels for 12% -> 10%
where the time goes in v4:
time: 152 us
  waiting for transfers between devices  56.5 us (37%)
  starting transfers between devices  47.5 us (31%)
  Pallas kernels  16.9 us (11%)
  other arithmetic  12.1 us (8%)
  local copies, waits for them, and re-layouts  9.32 us (6%)
  matrix products  7.53 us (5%)
  between operations  2.13 us (1%)
    ppermute x32, waiting for transfers between devices, swap(): return lax.ppermute(value, 'dp', [(i, i ^ 1 << bit) for i in range(n)])  48.9 us
    ppermute x32, starting transfers between devices, swap(): return lax.ppermute(value, 'dp', [(i, i ^ 1 << bit) for i in range(n)])  39.4 us
    pallas_call x9, Pallas kernels, multiply(): pl.pallas_call(kernel, out_shape=jax.ShapeDtypeStruct((height, wide), dty...  12.6 us
    ppermute x7, starting transfers between devices, fetch(): return lax.ppermute(value, ('dp', 'tensor'), perm)  8.06 us
    ppermute x7, waiting for transfers between devices, fetch(): return lax.ppermute(value, ('dp', 'tensor'), perm)  7.57 us
    pallas_call x4, Pallas kernels, pick_blocks(): pl.pallas_call(kernel, out_shape=[jax.ShapeDtypeStruct((tokens, half * wi...  4.3 us
    dot_general x4, matrix products, dot_t(): lax.dot_general(a, g, (((0,), (0,)), ((), ())), preferred_element_type=F32)  4.05 us
    dot_general x6, matrix products, dot(): lax.dot_general(a, w, (((1,), (0,)), ((), ())), preferred_element_type=F32)  3.48 us
  transfers between devices with their start and end apart: 39, of which 22 were waited for; matrix products, arithmetic and copies ran while one was open for 13% of the time, Pallas kernels for 10%

profile of v4, /device:TPU:0, one launch (start us, length us, event | category | flops | bytes accessed | tf_op | source)
XLA Modules:
  0.0 151.9 jit_solution(9928618823566134304)
XLA Ops:
  0.6 1.8 %copy.117 = bf16[768,2,512]{2,0,1:T(8,128)(2,1)S(1)} copy(bf16[768,2,512]{2,1,0:T(2,128)(2,1)} %param.7) | data formatting | bytes 3145728 | tf_op args[1]
  3.1 1.9 %collective-permute-done = bf16[768,512]{1,0:T(8,128)(2,1)S(1)} collective-permute-done((bf16[768,512]{1,0:T(8,128)(2,1)S(1)}, bf16[768,512]{1,0:T(8,128)(2,1)S(1)}, u32[]{:S(2)}, u32[]{:S(2)}) %collective-permute-start) | collective-permute-done | bytes 786464 | tf_op jit(solution)/shard_map/ppermute | solution.py:142
  6.6 1.1 shard_map.102
  7.7 1.0 fusion.37
  13.5 2.7 %collective-permute-start.4 = (f16[1024,256]{1,0:T(8,128)(2,1)S(1)}, f16[1024,256]{1,0:T(8,128)(2,1)S(1)}, u32[]{:S(2)}, u32[]{:S(2)}) collective-permute-start(f16[1024,256]{1,0:T(8,128)(2,1)S(1)} %slice.220), channel_id=1, source_target_pairs={{0,4},{2,6},{4,0},{6,2},{8,12},{10,14},{12,8},{14,10},{16,20},{18,... | collective-permute-start | bytes 1572872 | tf_op jit(solution)/shard_map/ppermute | solution.py:142
  16.9 1.6 %collective-permute-start.6 = (f16[1024,256]{1,0:T(8,128)(2,1)S(1)}, f16[1024,256]{1,0:T(8,128)(2,1)S(1)}, u32[]{:S(2)}, u32[]{:S(2)}) collective-permute-start(f16[1024,256]{1,0:T(8,128)(2,1)S(1)} %pad_maximum_fusion.8), channel_id=1, source_target_pairs={{0,8},{2,10},{4,12},{6,14},{8,0},{10,2},{12,4},{14,6},{16,24},{18,... | collective-permute-start | bytes 1572872 | tf_op jit(solution)/shard_map/ppermute | solution.py:142
  18.5 2.5 %shard_map.103 = f32[1024,512]{1,0:T(8,128)S(1)} custom-call(bf16[768,1024]{1,0:T(8,128)(2,1)S(1)} %get-tuple-element.75.refs_0_, bf16[768,512]{1,0:T(8,128)(2,1)S(1)} %get-tuple-element.82.refs_1_, bf16[768,1024]{1,0:T(8,128)(2,1)S(1)} %collective-permute-done.1.refs_2_, bf16[768,512]{1,0:T(8,128)(2,1)S(1)} %collective-permute-done.3.refs_3_), custom_call_target="tpu_custom_call" | custom-call | tf_op jit(solution)/shard_map/pallas_call | solution.py:115
  22.1 2.5 %shard_map.104 = f32[1024,512]{1,0:T(8,128)S(1)} custom-call(bf16[768,1024]{1,0:T(8,128)(2,1)S(1)} %get-tuple-element.74.refs_0_, bf16[768,512]{1,0:T(8,128)(2,1)S(1)} %get-tuple-element.82.refs_1_, bf16[768,1024]{1,0:T(8,128)(2,1)S(1)} %collective-permute-done.2.refs_2_, bf16[768,512]{1,0:T(8,128)(2,1)S(1)} %collective-permute-done.3.refs_3_), custom_call_target="tpu_custom_call" | custom-call | tf_op jit(solution)/shard_map/pallas_call | solution.py:115
  24.6 1.0 shard_map.105
  25.7 1.2 shard_map.106
  26.9 2.0 %collective-permute-done.4 = f16[1024,256]{1,0:T(8,128)(2,1)S(1)} collective-permute-done((f16[1024,256]{1,0:T(8,128)(2,1)S(1)}, f16[1024,256]{1,0:T(8,128)(2,1)S(1)}, u32[]{:S(2)}, u32[]{:S(2)}) %collective-permute-start.4) | collective-permute-done | bytes 524320 | tf_op jit(solution)/shard_map/ppermute | solution.py:142
  29.1 2.1 %collective-permute-start.5 = (f16[512,256]{1,0:T(8,128)(2,1)S(1)}, f16[512,256]{1,0:T(8,128)(2,1)S(1)}, u32[]{:S(2)}, u32[]{:S(2)}) collective-permute-start(f16[512,256]{1,0:T(8,128)(2,1)S(1)} %slice_convert_fusion.4), channel_id=1, source_target_pairs={{0,8},{2,10},{4,12},{6,14},{8,0},{10,2},{12,4},{14,6},{16,24},{18,... | collective-permute-start | bytes 786440 | tf_op jit(solution)/shard_map/ppermute | solution.py:142
  33.8 1.5 collective-permute-start.9
  35.7 2.8 %collective-permute-done.5 = f16[512,256]{1,0:T(8,128)(2,1)S(1)} collective-permute-done((f16[512,256]{1,0:T(8,128)(2,1)S(1)}, f16[512,256]{1,0:T(8,128)(2,1)S(1)}, u32[]{:S(2)}, u32[]{:S(2)}) %collective-permute-start.5) | collective-permute-done | bytes 262176 | tf_op jit(solution)/shard_map/ppermute | solution.py:142
  38.6 3.0 %collective-permute-start.7 = (f16[256,256]{1,0:T(8,128)(2,1)S(1)}, f16[256,256]{1,0:T(8,128)(2,1)S(1)}, u32[]{:S(2)}, u32[]{:S(2)}) collective-permute-start(f16[256,256]{1,0:T(8,128)(2,1)S(1)} %slice_convert_fusion.9), channel_id=1, source_target_pairs={{0,16},{2,18},{4,20},{6,22},{8,24},{10,26},{12,28},{14,30},{16,0},... | collective-permute-start | bytes 393224 | tf_op jit(solution)/shard_map/ppermute | solution.py:142
  41.8 3.1 %collective-permute-start.12 = (f16[512,256]{1,0:T(8,128)(2,1)S(1)}, f16[512,256]{1,0:T(8,128)(2,1)S(1)}, u32[]{:S(2)}, u32[]{:S(2)}) collective-permute-start(f16[512,256]{1,0:T(8,128)(2,1)S(1)} %slice_convert_fusion.1), channel_id=1, source_target_pairs={{0,8},{2,10},{4,12},{6,14},{8,0},{10,2},{12,4},{14,6},{16,24},{18,... | collective-permute-start | bytes 786440 | tf_op jit(solution)/shard_map/ppermute | solution.py:142
  45.6 2.8 %collective-permute-start.13 = (f16[256,256]{1,0:T(8,128)(2,1)S(1)}, f16[256,256]{1,0:T(8,128)(2,1)S(1)}, u32[]{:S(2)}, u32[]{:S(2)}) collective-permute-start(f16[256,256]{1,0:T(8,128)(2,1)S(1)} %slice_convert_fusion.8), channel_id=1, source_target_pairs={{0,16},{2,18},{4,20},{6,22},{8,24},{10,26},{12,28},{14,30},{16,0},... | collective-permute-start | bytes 393224 | tf_op jit(solution)/shard_map/ppermute | solution.py:142
  48.4 7.0 %collective-permute-done.8 = f16[1024,256]{1,0:T(8,128)(2,1)S(1)} collective-permute-done((f16[1024,256]{1,0:T(8,128)(2,1)S(1)}, f16[1024,256]{1,0:T(8,128)(2,1)S(1)}, u32[]{:S(2)}, u32[]{:S(2)}) %collective-permute-start.8) | collective-permute-done | bytes 524320 | tf_op jit(solution)/shard_map/ppermute | solution.py:142
  55.5 2.0 %collective-permute-start.11 = (f16[512,256]{1,0:T(8,128)(2,1)S(1)}, f16[512,256]{1,0:T(8,128)(2,1)S(1)}, u32[]{:S(2)}, u32[]{:S(2)}) collective-permute-start(f16[512,256]{1,0:T(8,128)(2,1)S(1)} %slice_convert_fusion), channel_id=1, source_target_pairs={{0,4},{2,6},{4,0},{6,2},{8,12},{10,14},{12,8},{14,10},{16,20},{18,... | collective-permute-start | bytes 786440 | tf_op jit(solution)/shard_map/ppermute | solution.py:142
  57.5 1.9 %collective-permute-done.12 = f16[512,256]{1,0:T(8,128)(2,1)S(1)} collective-permute-done((f16[512,256]{1,0:T(8,128)(2,1)S(1)}, f16[512,256]{1,0:T(8,128)(2,1)S(1)}, u32[]{:S(2)}, u32[]{:S(2)}) %collective-permute-start.12) | collective-permute-done | bytes 262176 | tf_op jit(solution)/shard_map/ppermute | solution.py:142
  59.5 1.8 %collective-permute-start.14 = (f16[256,256]{1,0:T(8,128)(2,1)S(1)}, f16[256,256]{1,0:T(8,128)(2,1)S(1)}, u32[]{:S(2)}, u32[]{:S(2)}) collective-permute-start(f16[256,256]{1,0:T(8,128)(2,1)S(1)} %slice_convert_fusion.7), channel_id=1, source_target_pairs={{0,16},{2,18},{4,20},{6,22},{8,24},{10,26},{12,28},{14,30},{16,0},... | collective-permute-start | bytes 393224 | tf_op jit(solution)/shard_map/ppermute | solution.py:142
  62.0 2.2 %collective-permute-start.15 = (f16[256,256]{1,0:T(8,128)(2,1)S(1)}, f16[256,256]{1,0:T(8,128)(2,1)S(1)}, u32[]{:S(2)}, u32[]{:S(2)}) collective-permute-start(f16[256,256]{1,0:T(8,128)(2,1)S(1)} %slice_convert_fusion.6), channel_id=1, source_target_pairs={{0,16},{2,18},{4,20},{6,22},{8,24},{10,26},{12,28},{14,30},{16,0},... | collective-permute-start | bytes 393224 | tf_op jit(solution)/shard_map/ppermute | solution.py:142
  64.3 6.7 %collective-permute-done.14 = f16[256,256]{1,0:T(8,128)(2,1)S(1)} collective-permute-done((f16[256,256]{1,0:T(8,128)(2,1)S(1)}, f16[256,256]{1,0:T(8,128)(2,1)S(1)}, u32[]{:S(2)}, u32[]{:S(2)}) %collective-permute-start.14) | collective-permute-done | bytes 131104 | tf_op jit(solution)/shard_map/ppermute | solution.py:142
  71.1 1.7 %collective-permute-done.15 = f16[256,256]{1,0:T(8,128)(2,1)S(1)} collective-permute-done((f16[256,256]{1,0:T(8,128)(2,1)S(1)}, f16[256,256]{1,0:T(8,128)(2,1)S(1)}, u32[]{:S(2)}, u32[]{:S(2)}) %collective-permute-start.15) | collective-permute-done | bytes 131104 | tf_op jit(solution)/shard_map/ppermute | solution.py:142
  73.8 1.0 collective-permute-done.16
  74.9 1.4 collective-permute-start.17
  76.3 1.6 %collective-permute-start.18 = (f32[4,512]{1,0:T(4,128)S(1)}, f32[4,512]{1,0:T(4,128)S(1)}, u32[]{:S(2)}, u32[]{:S(2)}) collective-permute-start(f32[4,512]{1,0:T(4,128)S(1)} %fusion.26), channel_id=1, source_target_pairs={{0,4},{1,5},{2,6},{3,7},{4,0},{5,1},{6,2},{7,3},{8,12},{9,13},{10,... | collective-permute-start | bytes 24584 | tf_op jit(solution)/shard_map/ppermute | solution.py:156
  79.9 2.5 %collective-permute-done.19 = f32[4,512]{1,0:T(4,128)S(1)} collective-permute-done((f32[4,512]{1,0:T(4,128)S(1)}, f32[4,512]{1,0:T(4,128)S(1)}, u32[]{:S(2)}, u32[]{:S(2)}) %collective-permute-start.19) | collective-permute-done | bytes 8224 | tf_op jit(solution)/shard_map/ppermute | solution.py:156
  82.5 2.7 %collective-permute-start.21 = (f32[4,512]{1,0:T(4,128)S(1)}, f32[4,512]{1,0:T(4,128)S(1)}, u32[]{:S(2)}, u32[]{:S(2)}) collective-permute-start(f32[4,512]{1,0:T(4,128)S(1)} %add_add_fusion), channel_id=1, source_target_pairs={{0,16},{1,17},{2,18},{3,19},{4,20},{5,21},{6,22},{7,23},{8,24},{9,... | collective-permute-start | bytes 24584 | tf_op jit(solution)/shard_map/ppermute | solution.py:156
  85.2 1.7 %collective-permute-start.22 = (f32[4,512]{1,0:T(4,128)S(1)}, f32[4,512]{1,0:T(4,128)S(1)}, u32[]{:S(2)}, u32[]{:S(2)}) collective-permute-start(f32[4,512]{1,0:T(4,128)S(1)} %add_add_fusion), channel_id=1, source_target_pairs={{0,24},{1,25},{2,26},{3,27},{4,28},{5,29},{6,30},{7,31},{8,16},{9,... | collective-permute-start | bytes 24584 | tf_op jit(solution)/shard_map/ppermute | solution.py:156
  87.5 3.1 %collective-permute-done.22 = f32[4,512]{1,0:T(4,128)S(1)} collective-permute-done((f32[4,512]{1,0:T(4,128)S(1)}, f32[4,512]{1,0:T(4,128)S(1)}, u32[]{:S(2)}, u32[]{:S(2)}) %collective-permute-start.22) | collective-permute-done | bytes 8224 | tf_op jit(solution)/shard_map/ppermute | solution.py:156
  91.8 1.8 %copy.80 = f32[256,2,512]{2,1,0:T(2,128)} copy(f32[256,2,512]{2,0,1:T(8,128)S(1)} %pad_maximum_fusion.2) | data formatting | bytes 2097152 | tf_op jit(solution)/shard_map/optimization_barrier | solution.py:41
  93.6 3.0 %collective-permute-start.23 = (bf16[256,256]{1,0:T(8,128)(2,1)S(1)}, bf16[256,256]{1,0:T(8,128)(2,1)S(1)}, u32[]{:S(2)}, u32[]{:S(2)}) collective-permute-start(bf16[256,256]{1,0:T(8,128)(2,1)S(1)} %get-tuple-element.105), channel_id=1, source_target_pairs={{0,16},{2,18},{4,20},{6,22},{8,24},{10,26},{12,28},{14,30},{16,0},... | collective-permute-start | bytes 393224 | tf_op jit(solution)/shard_map/ppermute | solution.py:142
  97.5 2.5 %copy_subtract_fusion = (f32[256,1,512]{2,1,0:T(1,128)S(1)}, f32[256,1,512]{2,1,0:T(1,128)S(1)}) fusion(f32[256,1,512]{2,0,1:T(8,128)S(1)} %get-tuple-element.161, f32[256,1,512]{2,0,1:T(8,128)S(1)} %get-tuple-element.160, f32[256,1,512]{2,0,1:T(8,128)S(1)} %get-tuple-element.158, f32[]{:T(128)} %bitcast.6, f32[]{:T(128)} %bitcast.4, f32[512]{0:T(512)S(1)} %bitcast.83, ...), kind=kLoop, calls=%fused_computation.73 | loop fusion | flops 1048576 | bytes 3672072 | tf_op jit(solution)/shard_map/sub | solution.py:270
  100.2 2.3 %collective-permute-start.26 = (bf16[256,256]{1,0:T(8,128)(2,1)S(1)}, bf16[256,256]{1,0:T(8,128)(2,1)S(1)}, u32[]{:S(2)}, u32[]{:S(2)}) collective-permute-start(bf16[256,256]{1,0:T(8,128)(2,1)S(1)} %get-tuple-element.107), channel_id=1, source_target_pairs={{0,16},{2,18},{4,20},{6,22},{8,24},{10,26},{12,28},{14,30},{16,0},... | collective-permute-start | bytes 393224 | tf_op jit(solution)/shard_map/ppermute | solution.py:142
  102.4 1.6 %collective-permute-done.23 = bf16[256,256]{1,0:T(8,128)(2,1)S(1)} collective-permute-done((bf16[256,256]{1,0:T(8,128)(2,1)S(1)}, bf16[256,256]{1,0:T(8,128)(2,1)S(1)}, u32[]{:S(2)}, u32[]{:S(2)}) %collective-permute-start.23) | collective-permute-done | bytes 131104 | tf_op jit(solution)/shard_map/ppermute | solution.py:142
  104.0 1.7 %collective-permute-start.27 = (bf16[512,256]{1,0:T(8,128)(2,1)S(1)}, bf16[512,256]{1,0:T(8,128)(2,1)S(1)}, u32[]{:S(2)}, u32[]{:S(2)}) collective-permute-start(bf16[512,256]{1,0:T(8,128)(2,1)S(1)} %get-tuple-element.180), channel_id=1, source_target_pairs={{0,4},{2,6},{4,0},{6,2},{8,12},{10,14},{12,8},{14,10},{16,20},{18,... | collective-permute-start | bytes 786440 | tf_op jit(solution)/shard_map/ppermute | solution.py:142
  105.9 4.3 %collective-permute-done.28 = bf16[512,256]{1,0:T(8,128)(2,1)S(1)} collective-permute-done((bf16[512,256]{1,0:T(8,128)(2,1)S(1)}, bf16[512,256]{1,0:T(8,128)(2,1)S(1)}, u32[]{:S(2)}, u32[]{:S(2)}) %collective-permute-start.28) | collective-permute-done | bytes 262176 | tf_op jit(solution)/shard_map/ppermute | solution.py:142
  112.3 1.4 collective-permute-start.30
  113.7 2.5 %collective-permute-start.29 = (bf16[512,256]{1,0:T(8,128)(2,1)S(1)}, bf16[512,256]{1,0:T(8,128)(2,1)S(1)}, u32[]{:S(2)}, u32[]{:S(2)}) collective-permute-start(bf16[512,256]{1,0:T(8,128)(2,1)S(1)} %get-tuple-element.172), channel_id=1, source_target_pairs={{0,4},{2,6},{4,0},{6,2},{8,12},{10,14},{12,8},{14,10},{16,20},{18,... | collective-permute-start | bytes 786440 | tf_op jit(solution)/shard_map/ppermute | solution.py:142
  116.3 3.2 %pad_maximum_fusion.1 = (f32[256,2,512]{2,1,0:T(2,128)}, f32[256,2,512]{2,1,0:T(2,128)}) fusion(f32[256,1,512]{2,1,0:T(1,128)S(1)} %get-tuple-element.138, f32[256,1,512]{2,1,0:T(1,128)S(1)} %fusion.21, f32[256,1,512]{2,1,0:T(1,128)S(1)} %get-tuple-element.139, f32[256,1,512]{2,1,0:T(1,128)S(1)} %copy.81), kind=kLoop, calls=%fused_computation.16 | loop fusion | flops 524288 | bytes 4194304 | tf_op jit(solution)/shard_map/stack | solution.py:272
  119.5 9.6 %collective-permute-done.30 = bf16[512,256]{1,0:T(8,128)(2,1)S(1)} collective-permute-done((bf16[512,256]{1,0:T(8,128)(2,1)S(1)}, bf16[512,256]{1,0:T(8,128)(2,1)S(1)}, u32[]{:S(2)}, u32[]{:S(2)}) %collective-permute-start.30) | collective-permute-done | bytes 262176 | tf_op jit(solution)/shard_map/ppermute | solution.py:142
  129.9 1.8 %collective-permute-start.35 = (bf16[1024,256]{1,0:T(8,128)(2,1)S(1)}, bf16[1024,256]{1,0:T(8,128)(2,1)S(1)}, u32[]{:S(2)}, u32[]{:S(2)}) collective-permute-start(bf16[1024,256]{1,0:T(8,128)(2,1)S(1)} %constant_dynamic-update-slice_fusion.14.refs_1_), channel_id=1, source_target_pairs={{0,4},{2,6},{4,0},{6,2},{8,12},{10,14},{12,8},{14,10},{16,20},{18,... | collective-permute-start | bytes 1572872 | tf_op jit(solution)/shard_map/ppermute | solution.py:142
  132.7 1.8 %shard_map.108 = bf16[768,256]{1,0:T(8,128)(2,1)S(1)} custom-call(bf16[768,1024]{1,0:T(8,128)(2,1)S(1)} %get-tuple-element.75.refs_0_, bf16[1024,256]{1,0:T(8,128)(2,1)S(1)} %collective-permute-done.32.refs_1_, bf16[768,1024]{1,0:T(8,128)(2,1)S(1)} %get-tuple-element.71.refs_2_, bf16[1024,256]{1,0:T(8,128)(2,1)S(1)} %get-tuple-element.157.refs_3_, ...), custom_call_target="tpu_custom_call" | custom-call | tf_op jit(solution)/shard_map/pallas_call | solution.py:115
  136.4 1.3 shard_map.111
  139.6 4.3 %collective-permute-done.35 = bf16[1024,256]{1,0:T(8,128)(2,1)S(1)} collective-permute-done((bf16[1024,256]{1,0:T(8,128)(2,1)S(1)}, bf16[1024,256]{1,0:T(8,128)(2,1)S(1)}, u32[]{:S(2)}, u32[]{:S(2)}) %collective-permute-start.35) | collective-permute-done | bytes 524320 | tf_op jit(solution)/shard_map/ppermute | solution.py:142
  144.0 1.3 collective-permute-done.36
  149.6 2.4 %reshape.311 = bf16[768,2,512]{2,1,0:T(2,128)(2,1)} reshape(bf16[768,1024]{1,0:T(8,128)(2,1)S(1)} %pad_maximum_fusion) | data formatting | bytes 3145728 | tf_op jit(solution)/shard_map/reshape | solution.py:320
  (138 shorter events, 31.4 us)
Async XLA Ops:
  0.6 4.4 %copy-start = (bf16[768,4096]{1,0:T(8,128)(2,1)S(1)}, bf16[768,4096]{1,0:T(8,128)(2,1)}, u32[]{:S(2)}) copy-start(bf16[768,4096]{1,0:T(8,128)(2,1)} %src.3) | copy-start | bytes 18874372
  2.6 2.4 %collective-permute-start = (bf16[768,512]{1,0:T(8,128)(2,1)S(1)}, bf16[768,512]{1,0:T(8,128)(2,1)S(1)}, u32[]{:S(2)}, u32[]{:S(2)}) collective-permute-start(bf16[768,512]{1,0:T(8,128)(2,1)S(1)} %get-tuple-element.77), channel_id=1, source_target_pairs={{0,2},{2,0},{4,6},{6,4},{8,10},{10,8},{12,14},{14,12},{16,18},{18,... | collective-permute-start | bytes 2359304 | tf_op jit(solution)/shard_map/ppermute | solution.py:142
  6.0 3.5 %collective-permute-start.1 = (bf16[768,1024]{1,0:T(8,128)(2,1)S(1)}, bf16[768,1024]{1,0:T(8,128)(2,1)S(1)}, u32[]{:S(2)}, u32[]{:S(2)}) collective-permute-start(bf16[768,1024]{1,0:T(8,128)(2,1)S(1)} %get-tuple-element.72.refs_4_), channel_id=1, source_target_pairs={{0,2},{2,0},{4,6},{6,4},{8,10},{10,8},{12,14},{14,12},{16,18},{18,... | collective-permute-start | bytes 4718600 | tf_op jit(solution)/shard_map/ppermute | solution.py:142
  6.5 5.3 %collective-permute-start.2 = (bf16[768,1024]{1,0:T(8,128)(2,1)S(1)}, bf16[768,1024]{1,0:T(8,128)(2,1)S(1)}, u32[]{:S(2)}, u32[]{:S(2)}) collective-permute-start(bf16[768,1024]{1,0:T(8,128)(2,1)S(1)} %get-tuple-element.71.refs_2_), channel_id=1, source_target_pairs={{0,2},{2,0},{4,6},{6,4},{8,10},{10,8},{12,14},{14,12},{16,18},{18,... | collective-permute-start | bytes 4718600 | tf_op jit(solution)/shard_map/ppermute | solution.py:142
  13.0 5.5 %collective-permute-start.3 = (bf16[768,512]{1,0:T(8,128)(2,1)S(1)}, bf16[768,512]{1,0:T(8,128)(2,1)S(1)}, u32[]{:S(2)}, u32[]{:S(2)}) collective-permute-start(bf16[768,512]{1,0:T(8,128)(2,1)S(1)} %get-tuple-element.82.refs_1_), channel_id=1, source_target_pairs={{0,2},{2,0},{4,6},{6,4},{8,10},{10,8},{12,14},{14,12},{16,18},{18,... | collective-permute-start | bytes 2359304 | tf_op jit(solution)/shard_map/ppermute | solution.py:142
  13.5 15.4 %collective-permute-start.4 = (f16[1024,256]{1,0:T(8,128)(2,1)S(1)}, f16[1024,256]{1,0:T(8,128)(2,1)S(1)}, u32[]{:S(2)}, u32[]{:S(2)}) collective-permute-start(f16[1024,256]{1,0:T(8,128)(2,1)S(1)} %slice.220), channel_id=1, source_target_pairs={{0,4},{2,6},{4,0},{6,2},{8,12},{10,14},{12,8},{14,10},{16,20},{18,... | collective-permute-start | bytes 1572872 | tf_op jit(solution)/shard_map/ppermute | solution.py:142
  16.9 14.7 %collective-permute-start.6 = (f16[1024,256]{1,0:T(8,128)(2,1)S(1)}, f16[1024,256]{1,0:T(8,128)(2,1)S(1)}, u32[]{:S(2)}, u32[]{:S(2)}) collective-permute-start(f16[1024,256]{1,0:T(8,128)(2,1)S(1)} %pad_maximum_fusion.8), channel_id=1, source_target_pairs={{0,8},{2,10},{4,12},{6,14},{8,0},{10,2},{12,4},{14,6},{16,24},{18,... | collective-permute-start | bytes 1572872 | tf_op jit(solution)/shard_map/ppermute | solution.py:142
  21.5 20.1 %collective-permute-start.10 = (f16[1024,256]{1,0:T(8,128)(2,1)S(1)}, f16[1024,256]{1,0:T(8,128)(2,1)S(1)}, u32[]{:S(2)}, u32[]{:S(2)}) collective-permute-start(f16[1024,256]{1,0:T(8,128)(2,1)S(1)} %slice.221), channel_id=1, source_target_pairs={{0,4},{2,6},{4,0},{6,2},{8,12},{10,14},{12,8},{14,10},{16,20},{18,... | collective-permute-start | bytes 1572872 | tf_op jit(solution)/shard_map/ppermute | solution.py:142
  29.1 9.4 %collective-permute-start.5 = (f16[512,256]{1,0:T(8,128)(2,1)S(1)}, f16[512,256]{1,0:T(8,128)(2,1)S(1)}, u32[]{:S(2)}, u32[]{:S(2)}) collective-permute-start(f16[512,256]{1,0:T(8,128)(2,1)S(1)} %slice_convert_fusion.4), channel_id=1, source_target_pairs={{0,8},{2,10},{4,12},{6,14},{8,0},{10,2},{12,4},{14,6},{16,24},{18,... | collective-permute-start | bytes 786440 | tf_op jit(solution)/shard_map/ppermute | solution.py:142
  31.4 1.2 copy-start.1
  31.5 23.8 %collective-permute-start.8 = (f16[1024,256]{1,0:T(8,128)(2,1)S(1)}, f16[1024,256]{1,0:T(8,128)(2,1)S(1)}, u32[]{:S(2)}, u32[]{:S(2)}) collective-permute-start(f16[1024,256]{1,0:T(8,128)(2,1)S(1)} %pad_maximum_fusion.9), channel_id=1, source_target_pairs={{0,8},{2,10},{4,12},{6,14},{8,0},{10,2},{12,4},{14,6},{16,24},{18,... | collective-permute-start | bytes 1572872 | tf_op jit(solution)/shard_map/ppermute | solution.py:142
  33.1 2.1 %copy-start.2 = (f32[256,2,512]{2,1,0:T(2,128)S(1)}, f32[256,2,512]{2,1,0:T(2,128)}, u32[]{:S(2)}) copy-start(f32[256,2,512]{2,1,0:T(2,128)} %param.9) | copy-start | bytes 3145732
  33.4 2.1 %copy-start.3 = (f32[256,2,512]{2,1,0:T(2,128)S(1)}, f32[256,2,512]{2,1,0:T(2,128)}, u32[]{:S(2)}) copy-start(f32[256,2,512]{2,1,0:T(2,128)} %param.10) | copy-start | bytes 3145732
  33.8 11.7 %collective-permute-start.9 = (f16[512,256]{1,0:T(8,128)(2,1)S(1)}, f16[512,256]{1,0:T(8,128)(2,1)S(1)}, u32[]{:S(2)}, u32[]{:S(2)}) collective-permute-start(f16[512,256]{1,0:T(8,128)(2,1)S(1)} %slice_convert_fusion.2), channel_id=1, source_target_pairs={{0,4},{2,6},{4,0},{6,2},{8,12},{10,14},{12,8},{14,10},{16,20},{18,... | collective-permute-start | bytes 786440 | tf_op jit(solution)/shard_map/ppermute | solution.py:142
  38.6 25.7 %collective-permute-start.7 = (f16[256,256]{1,0:T(8,128)(2,1)S(1)}, f16[256,256]{1,0:T(8,128)(2,1)S(1)}, u32[]{:S(2)}, u32[]{:S(2)}) collective-permute-start(f16[256,256]{1,0:T(8,128)(2,1)S(1)} %slice_convert_fusion.9), channel_id=1, source_target_pairs={{0,16},{2,18},{4,20},{6,22},{8,24},{10,26},{12,28},{14,30},{16,0},... | collective-permute-start | bytes 393224 | tf_op jit(solution)/shard_map/ppermute | solution.py:142
  41.8 17.5 %collective-permute-start.12 = (f16[512,256]{1,0:T(8,128)(2,1)S(1)}, f16[512,256]{1,0:T(8,128)(2,1)S(1)}, u32[]{:S(2)}, u32[]{:S(2)}) collective-permute-start(f16[512,256]{1,0:T(8,128)(2,1)S(1)} %slice_convert_fusion.1), channel_id=1, source_target_pairs={{0,8},{2,10},{4,12},{6,14},{8,0},{10,2},{12,4},{14,6},{16,24},{18,... | collective-permute-start | bytes 786440 | tf_op jit(solution)/shard_map/ppermute | solution.py:142
  45.6 18.7 %collective-permute-start.13 = (f16[256,256]{1,0:T(8,128)(2,1)S(1)}, f16[256,256]{1,0:T(8,128)(2,1)S(1)}, u32[]{:S(2)}, u32[]{:S(2)}) collective-permute-start(f16[256,256]{1,0:T(8,128)(2,1)S(1)} %slice_convert_fusion.8), channel_id=1, source_target_pairs={{0,16},{2,18},{4,20},{6,22},{8,24},{10,26},{12,28},{14,30},{16,0},... | collective-permute-start | bytes 393224 | tf_op jit(solution)/shard_map/ppermute | solution.py:142
  55.5 6.4 %collective-permute-start.11 = (f16[512,256]{1,0:T(8,128)(2,1)S(1)}, f16[512,256]{1,0:T(8,128)(2,1)S(1)}, u32[]{:S(2)}, u32[]{:S(2)}) collective-permute-start(f16[512,256]{1,0:T(8,128)(2,1)S(1)} %slice_convert_fusion), channel_id=1, source_target_pairs={{0,4},{2,6},{4,0},{6,2},{8,12},{10,14},{12,8},{14,10},{16,20},{18,... | collective-permute-start | bytes 786440 | tf_op jit(solution)/shard_map/ppermute | solution.py:142
  59.5 11.6 %collective-permute-start.14 = (f16[256,256]{1,0:T(8,128)(2,1)S(1)}, f16[256,256]{1,0:T(8,128)(2,1)S(1)}, u32[]{:S(2)}, u32[]{:S(2)}) collective-permute-start(f16[256,256]{1,0:T(8,128)(2,1)S(1)} %slice_convert_fusion.7), channel_id=1, source_target_pairs={{0,16},{2,18},{4,20},{6,22},{8,24},{10,26},{12,28},{14,30},{16,0},... | collective-permute-start | bytes 393224 | tf_op jit(solution)/shard_map/ppermute | solution.py:142
  62.0 10.7 %collective-permute-start.15 = (f16[256,256]{1,0:T(8,128)(2,1)S(1)}, f16[256,256]{1,0:T(8,128)(2,1)S(1)}, u32[]{:S(2)}, u32[]{:S(2)}) collective-permute-start(f16[256,256]{1,0:T(8,128)(2,1)S(1)} %slice_convert_fusion.6), channel_id=1, source_target_pairs={{0,16},{2,18},{4,20},{6,22},{8,24},{10,26},{12,28},{14,30},{16,0},... | collective-permute-start | bytes 393224 | tf_op jit(solution)/shard_map/ppermute | solution.py:142
  73.6 1.2 collective-permute-start.16
  74.9 4.1 %collective-permute-start.17 = (f32[4,512]{1,0:T(4,128)S(1)}, f32[4,512]{1,0:T(4,128)S(1)}, u32[]{:S(2)}, u32[]{:S(2)}) collective-permute-start(f32[4,512]{1,0:T(4,128)S(1)} %fusion.26), channel_id=1, source_target_pairs={{0,1},{1,0},{2,3},{3,2},{4,5},{5,4},{6,7},{7,6},{8,9},{9,8},{10,11... | collective-permute-start | bytes 24584 | tf_op jit(solution)/shard_map/ppermute | solution.py:156
  76.3 3.7 %collective-permute-start.18 = (f32[4,512]{1,0:T(4,128)S(1)}, f32[4,512]{1,0:T(4,128)S(1)}, u32[]{:S(2)}, u32[]{:S(2)}) collective-permute-start(f32[4,512]{1,0:T(4,128)S(1)} %fusion.26), channel_id=1, source_target_pairs={{0,4},{1,5},{2,6},{3,7},{4,0},{5,1},{6,2},{7,3},{8,12},{9,13},{10,... | collective-permute-start | bytes 24584 | tf_op jit(solution)/shard_map/ppermute | solution.py:156
  77.8 4.5 %collective-permute-start.19 = (f32[4,512]{1,0:T(4,128)S(1)}, f32[4,512]{1,0:T(4,128)S(1)}, u32[]{:S(2)}, u32[]{:S(2)}) collective-permute-start(f32[4,512]{1,0:T(4,128)S(1)} %fusion.26), channel_id=1, source_target_pairs={{0,5},{1,4},{2,7},{3,6},{4,1},{5,0},{6,3},{7,2},{8,13},{9,12},{10,... | collective-permute-start | bytes 24584 | tf_op jit(solution)/shard_map/ppermute | solution.py:156
  82.4 5.1 %collective-permute-start.20 = (f32[4,512]{1,0:T(4,128)S(1)}, f32[4,512]{1,0:T(4,128)S(1)}, u32[]{:S(2)}, u32[]{:S(2)}) collective-permute-start(f32[4,512]{1,0:T(4,128)S(1)} %add_add_fusion), channel_id=1, source_target_pairs={{0,8},{1,9},{2,10},{3,11},{4,12},{5,13},{6,14},{7,15},{8,0},{9,1},... | collective-permute-start | bytes 24584 | tf_op jit(solution)/shard_map/ppermute | solution.py:156
  82.5 5.0 %collective-permute-start.21 = (f32[4,512]{1,0:T(4,128)S(1)}, f32[4,512]{1,0:T(4,128)S(1)}, u32[]{:S(2)}, u32[]{:S(2)}) collective-permute-start(f32[4,512]{1,0:T(4,128)S(1)} %add_add_fusion), channel_id=1, source_target_pairs={{0,16},{1,17},{2,18},{3,19},{4,20},{5,21},{6,22},{7,23},{8,24},{9,... | collective-permute-start | bytes 24584 | tf_op jit(solution)/shard_map/ppermute | solution.py:156
  85.2 5.4 %collective-permute-start.22 = (f32[4,512]{1,0:T(4,128)S(1)}, f32[4,512]{1,0:T(4,128)S(1)}, u32[]{:S(2)}, u32[]{:S(2)}) collective-permute-start(f32[4,512]{1,0:T(4,128)S(1)} %add_add_fusion), channel_id=1, source_target_pairs={{0,24},{1,25},{2,26},{3,27},{4,28},{5,29},{6,30},{7,31},{8,16},{9,... | collective-permute-start | bytes 24584 | tf_op jit(solution)/shard_map/ppermute | solution.py:156
  91.8 8.3 %collective-permute-start.24 = (bf16[256,256]{1,0:T(8,128)(2,1)S(1)}, bf16[256,256]{1,0:T(8,128)(2,1)S(1)}, u32[]{:S(2)}, u32[]{:S(2)}) collective-permute-start(bf16[256,256]{1,0:T(8,128)(2,1)S(1)} %get-tuple-element.103), channel_id=1, source_target_pairs={{0,16},{2,18},{4,20},{6,22},{8,24},{10,26},{12,28},{14,30},{16,0},... | collective-permute-start | bytes 393224 | tf_op jit(solution)/shard_map/ppermute | solution.py:142
  93.6 10.4 %collective-permute-start.23 = (bf16[256,256]{1,0:T(8,128)(2,1)S(1)}, bf16[256,256]{1,0:T(8,128)(2,1)S(1)}, u32[]{:S(2)}, u32[]{:S(2)}) collective-permute-start(bf16[256,256]{1,0:T(8,128)(2,1)S(1)} %get-tuple-element.105), channel_id=1, source_target_pairs={{0,16},{2,18},{4,20},{6,22},{8,24},{10,26},{12,28},{14,30},{16,0},... | collective-permute-start | bytes 393224 | tf_op jit(solution)/shard_map/ppermute | solution.py:142
  100.1 10.0 %collective-permute-start.28 = (bf16[512,256]{1,0:T(8,128)(2,1)S(1)}, bf16[512,256]{1,0:T(8,128)(2,1)S(1)}, u32[]{:S(2)}, u32[]{:S(2)}) collective-permute-start(bf16[512,256]{1,0:T(8,128)(2,1)S(1)} %get-tuple-element.176), channel_id=1, source_target_pairs={{0,8},{2,10},{4,12},{6,14},{8,0},{10,2},{12,4},{14,6},{16,24},{18,... | collective-permute-start | bytes 786440 | tf_op jit(solution)/shard_map/ppermute | solution.py:142
  100.2 12.1 %collective-permute-start.26 = (bf16[256,256]{1,0:T(8,128)(2,1)S(1)}, bf16[256,256]{1,0:T(8,128)(2,1)S(1)}, u32[]{:S(2)}, u32[]{:S(2)}) collective-permute-start(bf16[256,256]{1,0:T(8,128)(2,1)S(1)} %get-tuple-element.107), channel_id=1, source_target_pairs={{0,16},{2,18},{4,20},{6,22},{8,24},{10,26},{12,28},{14,30},{16,0},... | collective-permute-start | bytes 393224 | tf_op jit(solution)/shard_map/ppermute | solution.py:142
  104.0 7.4 %collective-permute-start.27 = (bf16[512,256]{1,0:T(8,128)(2,1)S(1)}, bf16[512,256]{1,0:T(8,128)(2,1)S(1)}, u32[]{:S(2)}, u32[]{:S(2)}) collective-permute-start(bf16[512,256]{1,0:T(8,128)(2,1)S(1)} %get-tuple-element.180), channel_id=1, source_target_pairs={{0,4},{2,6},{4,0},{6,2},{8,12},{10,14},{12,8},{14,10},{16,20},{18,... | collective-permute-start | bytes 786440 | tf_op jit(solution)/shard_map/ppermute | solution.py:142
  105.7 8.0 %collective-permute-start.25 = (bf16[256,256]{1,0:T(8,128)(2,1)S(1)}, bf16[256,256]{1,0:T(8,128)(2,1)S(1)}, u32[]{:S(2)}, u32[]{:S(2)}) collective-permute-start(bf16[256,256]{1,0:T(8,128)(2,1)S(1)} %get-tuple-element.109), channel_id=1, source_target_pairs={{0,16},{2,18},{4,20},{6,22},{8,24},{10,26},{12,28},{14,30},{16,0},... | collective-permute-start | bytes 393224 | tf_op jit(solution)/shard_map/ppermute | solution.py:142
  110.1 19.0 %collective-permute-start.32 = (bf16[1024,256]{1,0:T(8,128)(2,1)S(1)}, bf16[1024,256]{1,0:T(8,128)(2,1)S(1)}, u32[]{:S(2)}, u32[]{:S(2)}) collective-permute-start(bf16[1024,256]{1,0:T(8,128)(2,1)S(1)} %constant_dynamic-update-slice_fusion.4.refs_1_), channel_id=1, source_target_pairs={{0,4},{2,6},{4,0},{6,2},{8,12},{10,14},{12,8},{14,10},{16,20},{18,... | collective-permute-start | bytes 1572872 | tf_op jit(solution)/shard_map/ppermute | solution.py:142
  111.5 17.8 %collective-permute-start.31 = (bf16[1024,256]{1,0:T(8,128)(2,1)S(1)}, bf16[1024,256]{1,0:T(8,128)(2,1)S(1)}, u32[]{:S(2)}, u32[]{:S(2)}) collective-permute-start(bf16[1024,256]{1,0:T(8,128)(2,1)S(1)} %constant_dynamic-update-slice_fusion.7.refs_1_), channel_id=1, source_target_pairs={{0,8},{2,10},{4,12},{6,14},{8,0},{10,2},{12,4},{14,6},{16,24},{18,... | collective-permute-start | bytes 1572872 | tf_op jit(solution)/shard_map/ppermute | solution.py:142
  112.3 16.7 %collective-permute-start.30 = (bf16[512,256]{1,0:T(8,128)(2,1)S(1)}, bf16[512,256]{1,0:T(8,128)(2,1)S(1)}, u32[]{:S(2)}, u32[]{:S(2)}) collective-permute-start(bf16[512,256]{1,0:T(8,128)(2,1)S(1)} %get-tuple-element.168), channel_id=1, source_target_pairs={{0,8},{2,10},{4,12},{6,14},{8,0},{10,2},{12,4},{14,6},{16,24},{18,... | collective-permute-start | bytes 786440 | tf_op jit(solution)/shard_map/ppermute | solution.py:142
  113.7 15.3 %collective-permute-start.29 = (bf16[512,256]{1,0:T(8,128)(2,1)S(1)}, bf16[512,256]{1,0:T(8,128)(2,1)S(1)}, u32[]{:S(2)}, u32[]{:S(2)}) collective-permute-start(bf16[512,256]{1,0:T(8,128)(2,1)S(1)} %get-tuple-element.172), channel_id=1, source_target_pairs={{0,4},{2,6},{4,0},{6,2},{8,12},{10,14},{12,8},{14,10},{16,20},{18,... | collective-permute-start | bytes 786440 | tf_op jit(solution)/shard_map/ppermute | solution.py:142
  129.2 3.4 %collective-permute-start.34 = (bf16[2048,256]{1,0:T(8,128)(2,1)S(1)}, bf16[2048,256]{1,0:T(8,128)(2,1)S(1)}, u32[]{:S(2)}, u32[]{:S(2)}) collective-permute-start(bf16[2048,256]{1,0:T(8,128)(2,1)S(1)} %pad_maximum_fusion.5), channel_id=1, source_target_pairs={{0,2},{2,0},{4,6},{6,4},{8,10},{10,8},{12,14},{14,12},{16,18},{18,... | collective-permute-start | bytes 3145736 | tf_op jit(solution)/shard_map/ppermute | solution.py:142
  129.4 7.0 %collective-permute-start.33 = (bf16[2048,256]{1,0:T(8,128)(2,1)S(1)}, bf16[2048,256]{1,0:T(8,128)(2,1)S(1)}, u32[]{:S(2)}, u32[]{:S(2)}) collective-permute-start(bf16[2048,256]{1,0:T(8,128)(2,1)S(1)} %pad_maximum_fusion.4), channel_id=1, source_target_pairs={{0,2},{2,0},{4,6},{6,4},{8,10},{10,8},{12,14},{14,12},{16,18},{18,... | collective-permute-start | bytes 3145736 | tf_op jit(solution)/shard_map/ppermute | solution.py:142
  129.9 14.0 %collective-permute-start.35 = (bf16[1024,256]{1,0:T(8,128)(2,1)S(1)}, bf16[1024,256]{1,0:T(8,128)(2,1)S(1)}, u32[]{:S(2)}, u32[]{:S(2)}) collective-permute-start(bf16[1024,256]{1,0:T(8,128)(2,1)S(1)} %constant_dynamic-update-slice_fusion.14.refs_1_), channel_id=1, source_target_pairs={{0,4},{2,6},{4,0},{6,2},{8,12},{10,14},{12,8},{14,10},{16,20},{18,... | collective-permute-start | bytes 1572872 | tf_op jit(solution)/shard_map/ppermute | solution.py:142
  131.7 13.6 %collective-permute-start.36 = (bf16[1024,256]{1,0:T(8,128)(2,1)S(1)}, bf16[1024,256]{1,0:T(8,128)(2,1)S(1)}, u32[]{:S(2)}, u32[]{:S(2)}) collective-permute-start(bf16[1024,256]{1,0:T(8,128)(2,1)S(1)} %constant_dynamic-update-slice_fusion.17.refs_1_), channel_id=1, source_target_pairs={{0,8},{2,10},{4,12},{6,14},{8,0},{10,2},{12,4},{14,6},{16,24},{18,... | collective-permute-start | bytes 1572872 | tf_op jit(solution)/shard_map/ppermute | solution.py:142
  143.9 2.7 %collective-permute-start.37 = (bf16[2048,256]{1,0:T(8,128)(2,1)S(1)}, bf16[2048,256]{1,0:T(8,128)(2,1)S(1)}, u32[]{:S(2)}, u32[]{:S(2)}) collective-permute-start(bf16[2048,256]{1,0:T(8,128)(2,1)S(1)} %pad_maximum_fusion.6), channel_id=1, source_target_pairs={{0,2},{2,0},{4,6},{6,4},{8,10},{10,8},{12,14},{14,12},{16,18},{18,... | collective-permute-start | bytes 3145736 | tf_op jit(solution)/shard_map/ppermute | solution.py:142
  145.4 2.8 %collective-permute-start.38 = (bf16[2048,256]{1,0:T(8,128)(2,1)S(1)}, bf16[2048,256]{1,0:T(8,128)(2,1)S(1)}, u32[]{:S(2)}, u32[]{:S(2)}) collective-permute-start(bf16[2048,256]{1,0:T(8,128)(2,1)S(1)} %pad_maximum_fusion.7), channel_id=1, source_target_pairs={{0,2},{2,0},{4,6},{6,4},{8,10},{10,8},{12,14},{14,12},{16,18},{18,... | collective-permute-start | bytes 3145736 | tf_op jit(solution)/shard_map/ppermute | solution.py:142

commit v5 on v4

--- a/solution.py
+++ b/solution.py
@@ -142,26 +142,11 @@
         return lax.ppermute(value, "dp", [(i, i ^ (1 << bit)) for i in range(n)])
 
     def total(value):
-        hops = [("dp", 1 << bit) for bit in range(bits)] + [("tensor", 1 << bit) for bit in range(t.bit_length() - 1)]
-        hops = hops[:1] + [hop for pair in zip(hops[bits:], hops[1:bits]) for hop in pair] + [
-            hop for hop in hops[1:] if hop not in [x for pair in zip(hops[bits:], hops[1:bits]) for x in pair]
-        ]
-        rounds = [hops[:1]] + [hops[i : i + 2] for i in range(1, len(hops), 2)]
-
-        def fetch(*flips):
-            flip = {"dp": 0, "tensor": 0}
-            for axis, amount in flips:
-                flip[axis] ^= amount
-            perm = [(i, ((i // t) ^ flip["dp"]) * t + ((i % t) ^ flip["tensor"])) for i in range(n * t)]
-            return lax.ppermute(value, ("dp", "tensor"), perm)
-
-        for around in rounds:
-            others = [fetch(around[0])]
-            if len(around) > 1:
-                others += [fetch(around[1]), fetch(*around)]
-            value = value + others[0]
-            if len(around) > 1:
-                value = value + (others[1] + others[2])
+        hops = [("dp", 0, n)]
+        hops += [("tensor", bit, t) for bit in range(t.bit_length() - 1)]
+        hops += [("dp", bit, n) for bit in links]
+        for axis, bit, size in hops:
+            value = value + lax.ppermute(value, axis, [(i, i ^ (1 << bit)) for i in range(size)])
         return value
 
     def dot_t(a, g):

time: 152 us -> 151 us (level)
  starting transfers between devices: 47.5 us -> 42.9 us
  waiting for transfers between devices: 56.5 us -> 60.4 us
    ppermute x7 -> x5, starting transfers between devices: 8.06 us -> 3.58 us  [total(): lax.ppermute(value, axis, [(i, i ^ 1 << bit) for i in range(size)])]
    ppermute x7 -> x5, waiting for transfers between devices: 7.57 us -> 11.9 us  [total(): lax.ppermute(value, axis, [(i, i ^ 1 << bit) for i in range(size)])]
  transfers between devices with their start and end apart: 39 -> 37, of which waited for: 22 -> 23; matrix products, arithmetic and copies ran while one was open for 13% -> 13% of each run, Pallas kernels for 10% -> 11%
where the time goes in v5:
time: 151 us
  waiting for transfers between devices  60.4 us (40%)
  starting transfers between devices  42.9 us (28%)
  Pallas kernels  16.9 us (11%)
  other arithmetic  12.1 us (8%)
  local copies, waits for them, and re-layouts  9.32 us (6%)
  matrix products  7.53 us (5%)
  between operations  2.11 us (1%)
    ppermute x32, waiting for transfers between devices, swap(): return lax.ppermute(value, 'dp', [(i, i ^ 1 << bit) for i in range(n)])  48.5 us
    ppermute x32, starting transfers between devices, swap(): return lax.ppermute(value, 'dp', [(i, i ^ 1 << bit) for i in range(n)])  39.3 us
    pallas_call x9, Pallas kernels, multiply(): pl.pallas_call(kernel, out_shape=jax.ShapeDtypeStruct((height, wide), dty...  12.6 us
    ppermute x5, waiting for transfers between devices, total(): lax.ppermute(value, axis, [(i, i ^ 1 << bit) for i in range(size)])  11.9 us
    pallas_call x4, Pallas kernels, pick_blocks(): pl.pallas_call(kernel, out_shape=[jax.ShapeDtypeStruct((tokens, half * wi...  4.3 us
    dot_general x4, matrix products, dot_t(): lax.dot_general(a, g, (((0,), (0,)), ((), ())), preferred_element_type=F32)  4.05 us
    ppermute x5, starting transfers between devices, total(): lax.ppermute(value, axis, [(i, i ^ 1 << bit) for i in range(size)])  3.58 us
    dot_general x6, matrix products, dot(): lax.dot_general(a, w, (((1,), (0,)), ((), ())), preferred_element_type=F32)  3.48 us
  transfers between devices with their start and end apart: 37, of which 23 were waited for; matrix products, arithmetic and copies ran while one was open for 13% of the time, Pallas kernels for 11%

profile of v5, /device:TPU:0, one launch (start us, length us, event | category | flops | bytes accessed | tf_op | source)
XLA Modules:
  0.0 151.3 jit_solution(8094479515292321811)
XLA Ops:
  0.6 1.8 %copy.117 = bf16[768,2,512]{2,0,1:T(8,128)(2,1)S(1)} copy(bf16[768,2,512]{2,1,0:T(2,128)(2,1)} %param.7) | data formatting | bytes 3145728 | tf_op args[1]
  3.1 1.9 %collective-permute-done = bf16[768,512]{1,0:T(8,128)(2,1)S(1)} collective-permute-done((bf16[768,512]{1,0:T(8,128)(2,1)S(1)}, bf16[768,512]{1,0:T(8,128)(2,1)S(1)}, u32[]{:S(2)}, u32[]{:S(2)}) %collective-permute-start) | collective-permute-done | bytes 786464 | tf_op jit(solution)/shard_map/ppermute | solution.py:142
  6.6 1.1 shard_map.102
  13.5 2.7 %collective-permute-start.4 = (f16[1024,256]{1,0:T(8,128)(2,1)S(1)}, f16[1024,256]{1,0:T(8,128)(2,1)S(1)}, u32[]{:S(2)}, u32[]{:S(2)}) collective-permute-start(f16[1024,256]{1,0:T(8,128)(2,1)S(1)} %slice.220), channel_id=1, source_target_pairs={{0,4},{2,6},{4,0},{6,2},{8,12},{10,14},{12,8},{14,10},{16,20},{18,... | collective-permute-start | bytes 1572872 | tf_op jit(solution)/shard_map/ppermute | solution.py:142
  16.9 1.6 %collective-permute-start.6 = (f16[1024,256]{1,0:T(8,128)(2,1)S(1)}, f16[1024,256]{1,0:T(8,128)(2,1)S(1)}, u32[]{:S(2)}, u32[]{:S(2)}) collective-permute-start(f16[1024,256]{1,0:T(8,128)(2,1)S(1)} %pad_maximum_fusion.8), channel_id=1, source_target_pairs={{0,8},{2,10},{4,12},{6,14},{8,0},{10,2},{12,4},{14,6},{16,24},{18,... | collective-permute-start | bytes 1572872 | tf_op jit(solution)/shard_map/ppermute | solution.py:142
  18.5 2.5 %shard_map.103 = f32[1024,512]{1,0:T(8,128)S(1)} custom-call(bf16[768,1024]{1,0:T(8,128)(2,1)S(1)} %get-tuple-element.75.refs_0_, bf16[768,512]{1,0:T(8,128)(2,1)S(1)} %get-tuple-element.82.refs_1_, bf16[768,1024]{1,0:T(8,128)(2,1)S(1)} %collective-permute-done.1.refs_2_, bf16[768,512]{1,0:T(8,128)(2,1)S(1)} %collective-permute-done.3.refs_3_), custom_call_target="tpu_custom_call" | custom-call | tf_op jit(solution)/shard_map/pallas_call | solution.py:115
  22.1 2.5 %shard_map.104 = f32[1024,512]{1,0:T(8,128)S(1)} custom-call(bf16[768,1024]{1,0:T(8,128)(2,1)S(1)} %get-tuple-element.74.refs_0_, bf16[768,512]{1,0:T(8,128)(2,1)S(1)} %get-tuple-element.82.refs_1_, bf16[768,1024]{1,0:T(8,128)(2,1)S(1)} %collective-permute-done.2.refs_2_, bf16[768,512]{1,0:T(8,128)(2,1)S(1)} %collective-permute-done.3.refs_3_), custom_call_target="tpu_custom_call" | custom-call | tf_op jit(solution)/shard_map/pallas_call | solution.py:115
  24.6 1.0 shard_map.105
  25.7 1.2 shard_map.106
  26.9 2.0 %collective-permute-done.4 = f16[1024,256]{1,0:T(8,128)(2,1)S(1)} collective-permute-done((f16[1024,256]{1,0:T(8,128)(2,1)S(1)}, f16[1024,256]{1,0:T(8,128)(2,1)S(1)}, u32[]{:S(2)}, u32[]{:S(2)}) %collective-permute-start.4) | collective-permute-done | bytes 524320 | tf_op jit(solution)/shard_map/ppermute | solution.py:142
  29.1 2.1 %collective-permute-start.5 = (f16[512,256]{1,0:T(8,128)(2,1)S(1)}, f16[512,256]{1,0:T(8,128)(2,1)S(1)}, u32[]{:S(2)}, u32[]{:S(2)}) collective-permute-start(f16[512,256]{1,0:T(8,128)(2,1)S(1)} %slice_convert_fusion.4), channel_id=1, source_target_pairs={{0,8},{2,10},{4,12},{6,14},{8,0},{10,2},{12,4},{14,6},{16,24},{18,... | collective-permute-start | bytes 786440 | tf_op jit(solution)/shard_map/ppermute | solution.py:142
  33.8 1.5 collective-permute-start.9
  35.7 2.8 %collective-permute-done.5 = f16[512,256]{1,0:T(8,128)(2,1)S(1)} collective-permute-done((f16[512,256]{1,0:T(8,128)(2,1)S(1)}, f16[512,256]{1,0:T(8,128)(2,1)S(1)}, u32[]{:S(2)}, u32[]{:S(2)}) %collective-permute-start.5) | collective-permute-done | bytes 262176 | tf_op jit(solution)/shard_map/ppermute | solution.py:142
  38.6 3.0 %collective-permute-start.7 = (f16[256,256]{1,0:T(8,128)(2,1)S(1)}, f16[256,256]{1,0:T(8,128)(2,1)S(1)}, u32[]{:S(2)}, u32[]{:S(2)}) collective-permute-start(f16[256,256]{1,0:T(8,128)(2,1)S(1)} %slice_convert_fusion.9), channel_id=1, source_target_pairs={{0,16},{2,18},{4,20},{6,22},{8,24},{10,26},{12,28},{14,30},{16,0},... | collective-permute-start | bytes 393224 | tf_op jit(solution)/shard_map/ppermute | solution.py:142
  41.8 3.1 %collective-permute-start.12 = (f16[512,256]{1,0:T(8,128)(2,1)S(1)}, f16[512,256]{1,0:T(8,128)(2,1)S(1)}, u32[]{:S(2)}, u32[]{:S(2)}) collective-permute-start(f16[512,256]{1,0:T(8,128)(2,1)S(1)} %slice_convert_fusion.1), channel_id=1, source_target_pairs={{0,8},{2,10},{4,12},{6,14},{8,0},{10,2},{12,4},{14,6},{16,24},{18,... | collective-permute-start | bytes 786440 | tf_op jit(solution)/shard_map/ppermute | solution.py:142
  45.6 2.8 %collective-permute-start.13 = (f16[256,256]{1,0:T(8,128)(2,1)S(1)}, f16[256,256]{1,0:T(8,128)(2,1)S(1)}, u32[]{:S(2)}, u32[]{:S(2)}) collective-permute-start(f16[256,256]{1,0:T(8,128)(2,1)S(1)} %slice_convert_fusion.8), channel_id=1, source_target_pairs={{0,16},{2,18},{4,20},{6,22},{8,24},{10,26},{12,28},{14,30},{16,0},... | collective-permute-start | bytes 393224 | tf_op jit(solution)/shard_map/ppermute | solution.py:142
  48.4 7.0 %collective-permute-done.8 = f16[1024,256]{1,0:T(8,128)(2,1)S(1)} collective-permute-done((f16[1024,256]{1,0:T(8,128)(2,1)S(1)}, f16[1024,256]{1,0:T(8,128)(2,1)S(1)}, u32[]{:S(2)}, u32[]{:S(2)}) %collective-permute-start.8) | collective-permute-done | bytes 524320 | tf_op jit(solution)/shard_map/ppermute | solution.py:142
  55.5 2.0 %collective-permute-start.11 = (f16[512,256]{1,0:T(8,128)(2,1)S(1)}, f16[512,256]{1,0:T(8,128)(2,1)S(1)}, u32[]{:S(2)}, u32[]{:S(2)}) collective-permute-start(f16[512,256]{1,0:T(8,128)(2,1)S(1)} %slice_convert_fusion), channel_id=1, source_target_pairs={{0,4},{2,6},{4,0},{6,2},{8,12},{10,14},{12,8},{14,10},{16,20},{18,... | collective-permute-start | bytes 786440 | tf_op jit(solution)/shard_map/ppermute | solution.py:142
  57.5 1.9 %collective-permute-done.12 = f16[512,256]{1,0:T(8,128)(2,1)S(1)} collective-permute-done((f16[512,256]{1,0:T(8,128)(2,1)S(1)}, f16[512,256]{1,0:T(8,128)(2,1)S(1)}, u32[]{:S(2)}, u32[]{:S(2)}) %collective-permute-start.12) | collective-permute-done | bytes 262176 | tf_op jit(solution)/shard_map/ppermute | solution.py:142
  59.5 1.8 %collective-permute-start.14 = (f16[256,256]{1,0:T(8,128)(2,1)S(1)}, f16[256,256]{1,0:T(8,128)(2,1)S(1)}, u32[]{:S(2)}, u32[]{:S(2)}) collective-permute-start(f16[256,256]{1,0:T(8,128)(2,1)S(1)} %slice_convert_fusion.7), channel_id=1, source_target_pairs={{0,16},{2,18},{4,20},{6,22},{8,24},{10,26},{12,28},{14,30},{16,0},... | collective-permute-start | bytes 393224 | tf_op jit(solution)/shard_map/ppermute | solution.py:142
  62.0 2.2 %collective-permute-start.15 = (f16[256,256]{1,0:T(8,128)(2,1)S(1)}, f16[256,256]{1,0:T(8,128)(2,1)S(1)}, u32[]{:S(2)}, u32[]{:S(2)}) collective-permute-start(f16[256,256]{1,0:T(8,128)(2,1)S(1)} %slice_convert_fusion.6), channel_id=1, source_target_pairs={{0,16},{2,18},{4,20},{6,22},{8,24},{10,26},{12,28},{14,30},{16,0},... | collective-permute-start | bytes 393224 | tf_op jit(solution)/shard_map/ppermute | solution.py:142
  64.3 6.7 %collective-permute-done.14 = f16[256,256]{1,0:T(8,128)(2,1)S(1)} collective-permute-done((f16[256,256]{1,0:T(8,128)(2,1)S(1)}, f16[256,256]{1,0:T(8,128)(2,1)S(1)}, u32[]{:S(2)}, u32[]{:S(2)}) %collective-permute-start.14) | collective-permute-done | bytes 131104 | tf_op jit(solution)/shard_map/ppermute | solution.py:142
  71.1 1.7 %collective-permute-done.15 = f16[256,256]{1,0:T(8,128)(2,1)S(1)} collective-permute-done((f16[256,256]{1,0:T(8,128)(2,1)S(1)}, f16[256,256]{1,0:T(8,128)(2,1)S(1)}, u32[]{:S(2)}, u32[]{:S(2)}) %collective-permute-start.15) | collective-permute-done | bytes 131104 | tf_op jit(solution)/shard_map/ppermute | solution.py:142
  73.7 1.2 collective-permute-done.16
  74.9 1.4 collective-permute-start.17
  76.3 2.3 %collective-permute-done.17 = f32[4,512]{1,0:T(4,128)S(1)} collective-permute-done((f32[4,512]{1,0:T(4,128)S(1)}, f32[4,512]{1,0:T(4,128)S(1)}, u32[]{:S(2)}, u32[]{:S(2)}) %collective-permute-start.17) | collective-permute-done | bytes 8224 | tf_op jit(solution)/shard_map/ppermute | solution.py:149
  78.6 1.4 collective-permute-start.18
  80.1 2.1 %collective-permute-done.18 = f32[4,512]{1,0:T(4,128)S(1)} collective-permute-done((f32[4,512]{1,0:T(4,128)S(1)}, f32[4,512]{1,0:T(4,128)S(1)}, u32[]{:S(2)}, u32[]{:S(2)}) %collective-permute-start.18) | collective-permute-done | bytes 8224 | tf_op jit(solution)/shard_map/ppermute | solution.py:149
  82.8 3.1 %collective-permute-done.19 = f32[4,512]{1,0:T(4,128)S(1)} collective-permute-done((f32[4,512]{1,0:T(4,128)S(1)}, f32[4,512]{1,0:T(4,128)S(1)}, u32[]{:S(2)}, u32[]{:S(2)}) %collective-permute-start.19) | collective-permute-done | bytes 8224 | tf_op jit(solution)/shard_map/ppermute | solution.py:149
  87.3 3.2 %collective-permute-done.20 = f32[4,512]{1,0:T(4,128)S(1)} collective-permute-done((f32[4,512]{1,0:T(4,128)S(1)}, f32[4,512]{1,0:T(4,128)S(1)}, u32[]{:S(2)}, u32[]{:S(2)}) %collective-permute-start.20) | collective-permute-done | bytes 8224 | tf_op jit(solution)/shard_map/ppermute | solution.py:149
  92.4 1.8 %copy.80 = f32[256,2,512]{2,1,0:T(2,128)} copy(f32[256,2,512]{2,0,1:T(8,128)S(1)} %pad_maximum_fusion.2) | data formatting | bytes 2097152 | tf_op jit(solution)/shard_map/optimization_barrier | solution.py:41
  94.2 2.3 %collective-permute-start.21 = (bf16[256,256]{1,0:T(8,128)(2,1)S(1)}, bf16[256,256]{1,0:T(8,128)(2,1)S(1)}, u32[]{:S(2)}, u32[]{:S(2)}) collective-permute-start(bf16[256,256]{1,0:T(8,128)(2,1)S(1)} %get-tuple-element.105), channel_id=1, source_target_pairs={{0,16},{2,18},{4,20},{6,22},{8,24},{10,26},{12,28},{14,30},{16,0},... | collective-permute-start | bytes 393224 | tf_op jit(solution)/shard_map/ppermute | solution.py:142
  97.4 2.5 %copy_subtract_fusion = (f32[256,1,512]{2,1,0:T(1,128)S(1)}, f32[256,1,512]{2,1,0:T(1,128)S(1)}) fusion(f32[256,1,512]{2,0,1:T(8,128)S(1)} %get-tuple-element.161, f32[256,1,512]{2,0,1:T(8,128)S(1)} %get-tuple-element.160, f32[256,1,512]{2,0,1:T(8,128)S(1)} %get-tuple-element.158, f32[]{:T(128)} %bitcast.6, f32[]{:T(128)} %bitcast.4, f32[512]{0:T(512)S(1)} %bitcast.83, ...), kind=kLoop, calls=%fused_computation.73 | loop fusion | flops 1048576 | bytes 3672072 | tf_op jit(solution)/shard_map/sub | solution.py:255
  100.0 2.8 %collective-permute-start.24 = (bf16[256,256]{1,0:T(8,128)(2,1)S(1)}, bf16[256,256]{1,0:T(8,128)(2,1)S(1)}, u32[]{:S(2)}, u32[]{:S(2)}) collective-permute-start(bf16[256,256]{1,0:T(8,128)(2,1)S(1)} %get-tuple-element.107), channel_id=1, source_target_pairs={{0,16},{2,18},{4,20},{6,22},{8,24},{10,26},{12,28},{14,30},{16,0},... | collective-permute-start | bytes 393224 | tf_op jit(solution)/shard_map/ppermute | solution.py:142
  102.8 3.4 %collective-permute-done.21 = bf16[256,256]{1,0:T(8,128)(2,1)S(1)} collective-permute-done((bf16[256,256]{1,0:T(8,128)(2,1)S(1)}, bf16[256,256]{1,0:T(8,128)(2,1)S(1)}, u32[]{:S(2)}, u32[]{:S(2)}) %collective-permute-start.21) | collective-permute-done | bytes 131104 | tf_op jit(solution)/shard_map/ppermute | solution.py:142
  106.2 1.3 collective-permute-start.25
  107.6 3.7 %collective-permute-done.26 = bf16[512,256]{1,0:T(8,128)(2,1)S(1)} collective-permute-done((bf16[512,256]{1,0:T(8,128)(2,1)S(1)}, bf16[512,256]{1,0:T(8,128)(2,1)S(1)}, u32[]{:S(2)}, u32[]{:S(2)}) %collective-permute-start.26) | collective-permute-done | bytes 262176 | tf_op jit(solution)/shard_map/ppermute | solution.py:142
  111.4 1.4 collective-permute-start.30
  112.8 2.7 %collective-permute-done.25 = bf16[512,256]{1,0:T(8,128)(2,1)S(1)} collective-permute-done((bf16[512,256]{1,0:T(8,128)(2,1)S(1)}, bf16[512,256]{1,0:T(8,128)(2,1)S(1)}, u32[]{:S(2)}, u32[]{:S(2)}) %collective-permute-start.25) | collective-permute-done | bytes 262176 | tf_op jit(solution)/shard_map/ppermute | solution.py:142
  115.7 2.1 %collective-permute-start.28 = (bf16[512,256]{1,0:T(8,128)(2,1)S(1)}, bf16[512,256]{1,0:T(8,128)(2,1)S(1)}, u32[]{:S(2)}, u32[]{:S(2)}) collective-permute-start(bf16[512,256]{1,0:T(8,128)(2,1)S(1)} %get-tuple-element.168), channel_id=1, source_target_pairs={{0,8},{2,10},{4,12},{6,14},{8,0},{10,2},{12,4},{14,6},{16,24},{18,... | collective-permute-start | bytes 786440 | tf_op jit(solution)/shard_map/ppermute | solution.py:142
  117.8 1.3 collective-permute-start.27
  119.1 3.2 %pad_maximum_fusion.1 = (f32[256,2,512]{2,1,0:T(2,128)}, f32[256,2,512]{2,1,0:T(2,128)}) fusion(f32[256,1,512]{2,1,0:T(1,128)S(1)} %get-tuple-element.138, f32[256,1,512]{2,1,0:T(1,128)S(1)} %fusion.21, f32[256,1,512]{2,1,0:T(1,128)S(1)} %get-tuple-element.139, f32[256,1,512]{2,1,0:T(1,128)S(1)} %copy.81), kind=kLoop, calls=%fused_computation.16 | loop fusion | flops 524288 | bytes 4194304 | tf_op jit(solution)/shard_map/stack | solution.py:257
  122.3 6.2 %collective-permute-done.28 = bf16[512,256]{1,0:T(8,128)(2,1)S(1)} collective-permute-done((bf16[512,256]{1,0:T(8,128)(2,1)S(1)}, bf16[512,256]{1,0:T(8,128)(2,1)S(1)}, u32[]{:S(2)}, u32[]{:S(2)}) %collective-permute-start.28) | collective-permute-done | bytes 262176 | tf_op jit(solution)/shard_map/ppermute | solution.py:142
  129.3 1.3 collective-permute-start.33
  131.6 1.8 %shard_map.108 = bf16[768,256]{1,0:T(8,128)(2,1)S(1)} custom-call(bf16[768,1024]{1,0:T(8,128)(2,1)S(1)} %get-tuple-element.75.refs_0_, bf16[1024,256]{1,0:T(8,128)(2,1)S(1)} %collective-permute-done.30.refs_1_, bf16[768,1024]{1,0:T(8,128)(2,1)S(1)} %get-tuple-element.71.refs_2_, bf16[1024,256]{1,0:T(8,128)(2,1)S(1)} %get-tuple-element.157.refs_3_, ...), custom_call_target="tpu_custom_call" | custom-call | tf_op jit(solution)/shard_map/pallas_call | solution.py:115
  135.3 1.3 shard_map.111
  138.5 4.7 %collective-permute-done.33 = bf16[1024,256]{1,0:T(8,128)(2,1)S(1)} collective-permute-done((bf16[1024,256]{1,0:T(8,128)(2,1)S(1)}, bf16[1024,256]{1,0:T(8,128)(2,1)S(1)}, u32[]{:S(2)}, u32[]{:S(2)}) %collective-permute-start.33) | collective-permute-done | bytes 524320 | tf_op jit(solution)/shard_map/ppermute | solution.py:142
  148.9 2.4 %reshape.311 = bf16[768,2,512]{2,1,0:T(2,128)(2,1)} reshape(bf16[768,1024]{1,0:T(8,128)(2,1)S(1)} %pad_maximum_fusion) | data formatting | bytes 3145728 | tf_op jit(solution)/shard_map/reshape | solution.py:305
  (136 shorter events, 31.5 us)
Async XLA Ops:
  0.6 4.4 %copy-start = (bf16[768,4096]{1,0:T(8,128)(2,1)S(1)}, bf16[768,4096]{1,0:T(8,128)(2,1)}, u32[]{:S(2)}) copy-start(bf16[768,4096]{1,0:T(8,128)(2,1)} %src.3) | copy-start | bytes 18874372
  2.6 2.4 %collective-permute-start = (bf16[768,512]{1,0:T(8,128)(2,1)S(1)}, bf16[768,512]{1,0:T(8,128)(2,1)S(1)}, u32[]{:S(2)}, u32[]{:S(2)}) collective-permute-start(bf16[768,512]{1,0:T(8,128)(2,1)S(1)} %get-tuple-element.77), channel_id=1, source_target_pairs={{0,2},{2,0},{4,6},{6,4},{8,10},{10,8},{12,14},{14,12},{16,18},{18,... | collective-permute-start | bytes 2359304 | tf_op jit(solution)/shard_map/ppermute | solution.py:142
  6.0 3.5 %collective-permute-start.1 = (bf16[768,1024]{1,0:T(8,128)(2,1)S(1)}, bf16[768,1024]{1,0:T(8,128)(2,1)S(1)}, u32[]{:S(2)}, u32[]{:S(2)}) collective-permute-start(bf16[768,1024]{1,0:T(8,128)(2,1)S(1)} %get-tuple-element.72.refs_4_), channel_id=1, source_target_pairs={{0,2},{2,0},{4,6},{6,4},{8,10},{10,8},{12,14},{14,12},{16,18},{18,... | collective-permute-start | bytes 4718600 | tf_op jit(solution)/shard_map/ppermute | solution.py:142
  6.5 5.3 %collective-permute-start.2 = (bf16[768,1024]{1,0:T(8,128)(2,1)S(1)}, bf16[768,1024]{1,0:T(8,128)(2,1)S(1)}, u32[]{:S(2)}, u32[]{:S(2)}) collective-permute-start(bf16[768,1024]{1,0:T(8,128)(2,1)S(1)} %get-tuple-element.71.refs_2_), channel_id=1, source_target_pairs={{0,2},{2,0},{4,6},{6,4},{8,10},{10,8},{12,14},{14,12},{16,18},{18,... | collective-permute-start | bytes 4718600 | tf_op jit(solution)/shard_map/ppermute | solution.py:142
  13.0 5.5 %collective-permute-start.3 = (bf16[768,512]{1,0:T(8,128)(2,1)S(1)}, bf16[768,512]{1,0:T(8,128)(2,1)S(1)}, u32[]{:S(2)}, u32[]{:S(2)}) collective-permute-start(bf16[768,512]{1,0:T(8,128)(2,1)S(1)} %get-tuple-element.82.refs_1_), channel_id=1, source_target_pairs={{0,2},{2,0},{4,6},{6,4},{8,10},{10,8},{12,14},{14,12},{16,18},{18,... | collective-permute-start | bytes 2359304 | tf_op jit(solution)/shard_map/ppermute | solution.py:142
  13.5 15.4 %collective-permute-start.4 = (f16[1024,256]{1,0:T(8,128)(2,1)S(1)}, f16[1024,256]{1,0:T(8,128)(2,1)S(1)}, u32[]{:S(2)}, u32[]{:S(2)}) collective-permute-start(f16[1024,256]{1,0:T(8,128)(2,1)S(1)} %slice.220), channel_id=1, source_target_pairs={{0,4},{2,6},{4,0},{6,2},{8,12},{10,14},{12,8},{14,10},{16,20},{18,... | collective-permute-start | bytes 1572872 | tf_op jit(solution)/shard_map/ppermute | solution.py:142
  16.9 14.7 %collective-permute-start.6 = (f16[1024,256]{1,0:T(8,128)(2,1)S(1)}, f16[1024,256]{1,0:T(8,128)(2,1)S(1)}, u32[]{:S(2)}, u32[]{:S(2)}) collective-permute-start(f16[1024,256]{1,0:T(8,128)(2,1)S(1)} %pad_maximum_fusion.8), channel_id=1, source_target_pairs={{0,8},{2,10},{4,12},{6,14},{8,0},{10,2},{12,4},{14,6},{16,24},{18,... | collective-permute-start | bytes 1572872 | tf_op jit(solution)/shard_map/ppermute | solution.py:142
  21.5 20.1 %collective-permute-start.10 = (f16[1024,256]{1,0:T(8,128)(2,1)S(1)}, f16[1024,256]{1,0:T(8,128)(2,1)S(1)}, u32[]{:S(2)}, u32[]{:S(2)}) collective-permute-start(f16[1024,256]{1,0:T(8,128)(2,1)S(1)} %slice.221), channel_id=1, source_target_pairs={{0,4},{2,6},{4,0},{6,2},{8,12},{10,14},{12,8},{14,10},{16,20},{18,... | collective-permute-start | bytes 1572872 | tf_op jit(solution)/shard_map/ppermute | solution.py:142
  29.1 9.4 %collective-permute-start.5 = (f16[512,256]{1,0:T(8,128)(2,1)S(1)}, f16[512,256]{1,0:T(8,128)(2,1)S(1)}, u32[]{:S(2)}, u32[]{:S(2)}) collective-permute-start(f16[512,256]{1,0:T(8,128)(2,1)S(1)} %slice_convert_fusion.4), channel_id=1, source_target_pairs={{0,8},{2,10},{4,12},{6,14},{8,0},{10,2},{12,4},{14,6},{16,24},{18,... | collective-permute-start | bytes 786440 | tf_op jit(solution)/shard_map/ppermute | solution.py:142
  31.4 1.2 copy-start.1
  31.5 23.8 %collective-permute-start.8 = (f16[1024,256]{1,0:T(8,128)(2,1)S(1)}, f16[1024,256]{1,0:T(8,128)(2,1)S(1)}, u32[]{:S(2)}, u32[]{:S(2)}) collective-permute-start(f16[1024,256]{1,0:T(8,128)(2,1)S(1)} %pad_maximum_fusion.9), channel_id=1, source_target_pairs={{0,8},{2,10},{4,12},{6,14},{8,0},{10,2},{12,4},{14,6},{16,24},{18,... | collective-permute-start | bytes 1572872 | tf_op jit(solution)/shard_map/ppermute | solution.py:142
  33.1 2.1 %copy-start.2 = (f32[256,2,512]{2,1,0:T(2,128)S(1)}, f32[256,2,512]{2,1,0:T(2,128)}, u32[]{:S(2)}) copy-start(f32[256,2,512]{2,1,0:T(2,128)} %param.9) | copy-start | bytes 3145732
  33.4 2.1 %copy-start.3 = (f32[256,2,512]{2,1,0:T(2,128)S(1)}, f32[256,2,512]{2,1,0:T(2,128)}, u32[]{:S(2)}) copy-start(f32[256,2,512]{2,1,0:T(2,128)} %param.10) | copy-start | bytes 3145732
  33.8 11.7 %collective-permute-start.9 = (f16[512,256]{1,0:T(8,128)(2,1)S(1)}, f16[512,256]{1,0:T(8,128)(2,1)S(1)}, u32[]{:S(2)}, u32[]{:S(2)}) collective-permute-start(f16[512,256]{1,0:T(8,128)(2,1)S(1)} %slice_convert_fusion.2), channel_id=1, source_target_pairs={{0,4},{2,6},{4,0},{6,2},{8,12},{10,14},{12,8},{14,10},{16,20},{18,... | collective-permute-start | bytes 786440 | tf_op jit(solution)/shard_map/ppermute | solution.py:142
  38.6 25.7 %collective-permute-start.7 = (f16[256,256]{1,0:T(8,128)(2,1)S(1)}, f16[256,256]{1,0:T(8,128)(2,1)S(1)}, u32[]{:S(2)}, u32[]{:S(2)}) collective-permute-start(f16[256,256]{1,0:T(8,128)(2,1)S(1)} %slice_convert_fusion.9), channel_id=1, source_target_pairs={{0,16},{2,18},{4,20},{6,22},{8,24},{10,26},{12,28},{14,30},{16,0},... | collective-permute-start | bytes 393224 | tf_op jit(solution)/shard_map/ppermute | solution.py:142
  41.8 17.5 %collective-permute-start.12 = (f16[512,256]{1,0:T(8,128)(2,1)S(1)}, f16[512,256]{1,0:T(8,128)(2,1)S(1)}, u32[]{:S(2)}, u32[]{:S(2)}) collective-permute-start(f16[512,256]{1,0:T(8,128)(2,1)S(1)} %slice_convert_fusion.1), channel_id=1, source_target_pairs={{0,8},{2,10},{4,12},{6,14},{8,0},{10,2},{12,4},{14,6},{16,24},{18,... | collective-permute-start | bytes 786440 | tf_op jit(solution)/shard_map/ppermute | solution.py:142
  45.6 18.7 %collective-permute-start.13 = (f16[256,256]{1,0:T(8,128)(2,1)S(1)}, f16[256,256]{1,0:T(8,128)(2,1)S(1)}, u32[]{:S(2)}, u32[]{:S(2)}) collective-permute-start(f16[256,256]{1,0:T(8,128)(2,1)S(1)} %slice_convert_fusion.8), channel_id=1, source_target_pairs={{0,16},{2,18},{4,20},{6,22},{8,24},{10,26},{12,28},{14,30},{16,0},... | collective-permute-start | bytes 393224 | tf_op jit(solution)/shard_map/ppermute | solution.py:142
  55.5 6.4 %collective-permute-start.11 = (f16[512,256]{1,0:T(8,128)(2,1)S(1)}, f16[512,256]{1,0:T(8,128)(2,1)S(1)}, u32[]{:S(2)}, u32[]{:S(2)}) collective-permute-start(f16[512,256]{1,0:T(8,128)(2,1)S(1)} %slice_convert_fusion), channel_id=1, source_target_pairs={{0,4},{2,6},{4,0},{6,2},{8,12},{10,14},{12,8},{14,10},{16,20},{18,... | collective-permute-start | bytes 786440 | tf_op jit(solution)/shard_map/ppermute | solution.py:142
  59.5 11.6 %collective-permute-start.14 = (f16[256,256]{1,0:T(8,128)(2,1)S(1)}, f16[256,256]{1,0:T(8,128)(2,1)S(1)}, u32[]{:S(2)}, u32[]{:S(2)}) collective-permute-start(f16[256,256]{1,0:T(8,128)(2,1)S(1)} %slice_convert_fusion.7), channel_id=1, source_target_pairs={{0,16},{2,18},{4,20},{6,22},{8,24},{10,26},{12,28},{14,30},{16,0},... | collective-permute-start | bytes 393224 | tf_op jit(solution)/shard_map/ppermute | solution.py:142
  62.0 10.7 %collective-permute-start.15 = (f16[256,256]{1,0:T(8,128)(2,1)S(1)}, f16[256,256]{1,0:T(8,128)(2,1)S(1)}, u32[]{:S(2)}, u32[]{:S(2)}) collective-permute-start(f16[256,256]{1,0:T(8,128)(2,1)S(1)} %slice_convert_fusion.6), channel_id=1, source_target_pairs={{0,16},{2,18},{4,20},{6,22},{8,24},{10,26},{12,28},{14,30},{16,0},... | collective-permute-start | bytes 393224 | tf_op jit(solution)/shard_map/ppermute | solution.py:142
  73.6 1.2 collective-permute-start.16
  74.9 3.7 %collective-permute-start.17 = (f32[4,512]{1,0:T(4,128)S(1)}, f32[4,512]{1,0:T(4,128)S(1)}, u32[]{:S(2)}, u32[]{:S(2)}) collective-permute-start(f32[4,512]{1,0:T(4,128)S(1)} %fusion.26), channel_id=1, source_target_pairs={{0,1},{1,0},{2,3},{3,2},{4,5},{5,4},{6,7},{7,6},{8,9},{9,8},{10,11... | collective-permute-start | bytes 24584 | tf_op jit(solution)/shard_map/ppermute | solution.py:149
  78.6 3.7 %collective-permute-start.18 = (f32[4,512]{1,0:T(4,128)S(1)}, f32[4,512]{1,0:T(4,128)S(1)}, u32[]{:S(2)}, u32[]{:S(2)}) collective-permute-start(f32[4,512]{1,0:T(4,128)S(1)} %add.154), channel_id=1, source_target_pairs={{0,4},{2,6},{4,0},{6,2},{8,12},{10,14},{12,8},{14,10},{16,20},{18,... | collective-permute-start | bytes 24584 | tf_op jit(solution)/shard_map/ppermute | solution.py:149
  82.3 3.7 %collective-permute-start.19 = (f32[4,512]{1,0:T(4,128)S(1)}, f32[4,512]{1,0:T(4,128)S(1)}, u32[]{:S(2)}, u32[]{:S(2)}) collective-permute-start(f32[4,512]{1,0:T(4,128)S(1)} %add.155), channel_id=1, source_target_pairs={{0,8},{2,10},{4,12},{6,14},{8,0},{10,2},{12,4},{14,6},{16,24},{18,... | collective-permute-start | bytes 24584 | tf_op jit(solution)/shard_map/ppermute | solution.py:149
  85.9 4.6 %collective-permute-start.20 = (f32[4,512]{1,0:T(4,128)S(1)}, f32[4,512]{1,0:T(4,128)S(1)}, u32[]{:S(2)}, u32[]{:S(2)}) collective-permute-start(f32[4,512]{1,0:T(4,128)S(1)} %add.156), channel_id=1, source_target_pairs={{0,16},{2,18},{4,20},{6,22},{8,24},{10,26},{12,28},{14,30},{16,0},... | collective-permute-start | bytes 24584 | tf_op jit(solution)/shard_map/ppermute | solution.py:149
  91.6 8.3 %collective-permute-start.22 = (bf16[256,256]{1,0:T(8,128)(2,1)S(1)}, bf16[256,256]{1,0:T(8,128)(2,1)S(1)}, u32[]{:S(2)}, u32[]{:S(2)}) collective-permute-start(bf16[256,256]{1,0:T(8,128)(2,1)S(1)} %get-tuple-element.103), channel_id=1, source_target_pairs={{0,16},{2,18},{4,20},{6,22},{8,24},{10,26},{12,28},{14,30},{16,0},... | collective-permute-start | bytes 393224 | tf_op jit(solution)/shard_map/ppermute | solution.py:142
  94.2 12.0 %collective-permute-start.21 = (bf16[256,256]{1,0:T(8,128)(2,1)S(1)}, bf16[256,256]{1,0:T(8,128)(2,1)S(1)}, u32[]{:S(2)}, u32[]{:S(2)}) collective-permute-start(bf16[256,256]{1,0:T(8,128)(2,1)S(1)} %get-tuple-element.105), channel_id=1, source_target_pairs={{0,16},{2,18},{4,20},{6,22},{8,24},{10,26},{12,28},{14,30},{16,0},... | collective-permute-start | bytes 393224 | tf_op jit(solution)/shard_map/ppermute | solution.py:142
  99.9 11.4 %collective-permute-start.26 = (bf16[512,256]{1,0:T(8,128)(2,1)S(1)}, bf16[512,256]{1,0:T(8,128)(2,1)S(1)}, u32[]{:S(2)}, u32[]{:S(2)}) collective-permute-start(bf16[512,256]{1,0:T(8,128)(2,1)S(1)} %get-tuple-element.176), channel_id=1, source_target_pairs={{0,8},{2,10},{4,12},{6,14},{8,0},{10,2},{12,4},{14,6},{16,24},{18,... | collective-permute-start | bytes 786440 | tf_op jit(solution)/shard_map/ppermute | solution.py:142
  100.0 15.6 %collective-permute-start.24 = (bf16[256,256]{1,0:T(8,128)(2,1)S(1)}, bf16[256,256]{1,0:T(8,128)(2,1)S(1)}, u32[]{:S(2)}, u32[]{:S(2)}) collective-permute-start(bf16[256,256]{1,0:T(8,128)(2,1)S(1)} %get-tuple-element.107), channel_id=1, source_target_pairs={{0,16},{2,18},{4,20},{6,22},{8,24},{10,26},{12,28},{14,30},{16,0},... | collective-permute-start | bytes 393224 | tf_op jit(solution)/shard_map/ppermute | solution.py:142
  106.2 9.3 %collective-permute-start.25 = (bf16[512,256]{1,0:T(8,128)(2,1)S(1)}, bf16[512,256]{1,0:T(8,128)(2,1)S(1)}, u32[]{:S(2)}, u32[]{:S(2)}) collective-permute-start(bf16[512,256]{1,0:T(8,128)(2,1)S(1)} %get-tuple-element.180), channel_id=1, source_target_pairs={{0,4},{2,6},{4,0},{6,2},{8,12},{10,14},{12,8},{14,10},{16,20},{18,... | collective-permute-start | bytes 786440 | tf_op jit(solution)/shard_map/ppermute | solution.py:142
  107.5 10.2 %collective-permute-start.23 = (bf16[256,256]{1,0:T(8,128)(2,1)S(1)}, bf16[256,256]{1,0:T(8,128)(2,1)S(1)}, u32[]{:S(2)}, u32[]{:S(2)}) collective-permute-start(bf16[256,256]{1,0:T(8,128)(2,1)S(1)} %get-tuple-element.109), channel_id=1, source_target_pairs={{0,16},{2,18},{4,20},{6,22},{8,24},{10,26},{12,28},{14,30},{16,0},... | collective-permute-start | bytes 393224 | tf_op jit(solution)/shard_map/ppermute | solution.py:142
  111.4 17.1 %collective-permute-start.30 = (bf16[1024,256]{1,0:T(8,128)(2,1)S(1)}, bf16[1024,256]{1,0:T(8,128)(2,1)S(1)}, u32[]{:S(2)}, u32[]{:S(2)}) collective-permute-start(bf16[1024,256]{1,0:T(8,128)(2,1)S(1)} %constant_dynamic-update-slice_fusion.4.refs_1_), channel_id=1, source_target_pairs={{0,4},{2,6},{4,0},{6,2},{8,12},{10,14},{12,8},{14,10},{16,20},{18,... | collective-permute-start | bytes 1572872 | tf_op jit(solution)/shard_map/ppermute | solution.py:142
  115.5 13.1 %collective-permute-start.29 = (bf16[1024,256]{1,0:T(8,128)(2,1)S(1)}, bf16[1024,256]{1,0:T(8,128)(2,1)S(1)}, u32[]{:S(2)}, u32[]{:S(2)}) collective-permute-start(bf16[1024,256]{1,0:T(8,128)(2,1)S(1)} %constant_dynamic-update-slice_fusion.7.refs_1_), channel_id=1, source_target_pairs={{0,8},{2,10},{4,12},{6,14},{8,0},{10,2},{12,4},{14,6},{16,24},{18,... | collective-permute-start | bytes 1572872 | tf_op jit(solution)/shard_map/ppermute | solution.py:142
  115.7 12.8 %collective-permute-start.28 = (bf16[512,256]{1,0:T(8,128)(2,1)S(1)}, bf16[512,256]{1,0:T(8,128)(2,1)S(1)}, u32[]{:S(2)}, u32[]{:S(2)}) collective-permute-start(bf16[512,256]{1,0:T(8,128)(2,1)S(1)} %get-tuple-element.168), channel_id=1, source_target_pairs={{0,8},{2,10},{4,12},{6,14},{8,0},{10,2},{12,4},{14,6},{16,24},{18,... | collective-permute-start | bytes 786440 | tf_op jit(solution)/shard_map/ppermute | solution.py:142
  117.8 10.7 %collective-permute-start.27 = (bf16[512,256]{1,0:T(8,128)(2,1)S(1)}, bf16[512,256]{1,0:T(8,128)(2,1)S(1)}, u32[]{:S(2)}, u32[]{:S(2)}) collective-permute-start(bf16[512,256]{1,0:T(8,128)(2,1)S(1)} %get-tuple-element.172), channel_id=1, source_target_pairs={{0,4},{2,6},{4,0},{6,2},{8,12},{10,14},{12,8},{14,10},{16,20},{18,... | collective-permute-start | bytes 786440 | tf_op jit(solution)/shard_map/ppermute | solution.py:142
  128.6 3.0 %collective-permute-start.32 = (bf16[2048,256]{1,0:T(8,128)(2,1)S(1)}, bf16[2048,256]{1,0:T(8,128)(2,1)S(1)}, u32[]{:S(2)}, u32[]{:S(2)}) collective-permute-start(bf16[2048,256]{1,0:T(8,128)(2,1)S(1)} %pad_maximum_fusion.5), channel_id=1, source_target_pairs={{0,2},{2,0},{4,6},{6,4},{8,10},{10,8},{12,14},{14,12},{16,18},{18,... | collective-permute-start | bytes 3145736 | tf_op jit(solution)/shard_map/ppermute | solution.py:142
  128.7 6.5 %collective-permute-start.31 = (bf16[2048,256]{1,0:T(8,128)(2,1)S(1)}, bf16[2048,256]{1,0:T(8,128)(2,1)S(1)}, u32[]{:S(2)}, u32[]{:S(2)}) collective-permute-start(bf16[2048,256]{1,0:T(8,128)(2,1)S(1)} %pad_maximum_fusion.4), channel_id=1, source_target_pairs={{0,2},{2,0},{4,6},{6,4},{8,10},{10,8},{12,14},{14,12},{16,18},{18,... | collective-permute-start | bytes 3145736 | tf_op jit(solution)/shard_map/ppermute | solution.py:142
  129.3 13.9 %collective-permute-start.33 = (bf16[1024,256]{1,0:T(8,128)(2,1)S(1)}, bf16[1024,256]{1,0:T(8,128)(2,1)S(1)}, u32[]{:S(2)}, u32[]{:S(2)}) collective-permute-start(bf16[1024,256]{1,0:T(8,128)(2,1)S(1)} %constant_dynamic-update-slice_fusion.14.refs_1_), channel_id=1, source_target_pairs={{0,4},{2,6},{4,0},{6,2},{8,12},{10,14},{12,8},{14,10},{16,20},{18,... | collective-permute-start | bytes 1572872 | tf_op jit(solution)/shard_map/ppermute | solution.py:142
  130.6 13.6 %collective-permute-start.34 = (bf16[1024,256]{1,0:T(8,128)(2,1)S(1)}, bf16[1024,256]{1,0:T(8,128)(2,1)S(1)}, u32[]{:S(2)}, u32[]{:S(2)}) collective-permute-start(bf16[1024,256]{1,0:T(8,128)(2,1)S(1)} %constant_dynamic-update-slice_fusion.17.refs_1_), channel_id=1, source_target_pairs={{0,8},{2,10},{4,12},{6,14},{8,0},{10,2},{12,4},{14,6},{16,24},{18,... | collective-permute-start | bytes 1572872 | tf_op jit(solution)/shard_map/ppermute | solution.py:142
  143.3 2.7 %collective-permute-start.35 = (bf16[2048,256]{1,0:T(8,128)(2,1)S(1)}, bf16[2048,256]{1,0:T(8,128)(2,1)S(1)}, u32[]{:S(2)}, u32[]{:S(2)}) collective-permute-start(bf16[2048,256]{1,0:T(8,128)(2,1)S(1)} %pad_maximum_fusion.6), channel_id=1, source_target_pairs={{0,2},{2,0},{4,6},{6,4},{8,10},{10,8},{12,14},{14,12},{16,18},{18,... | collective-permute-start | bytes 3145736 | tf_op jit(solution)/shard_map/ppermute | solution.py:142
  144.3 3.2 %collective-permute-start.36 = (bf16[2048,256]{1,0:T(8,128)(2,1)S(1)}, bf16[2048,256]{1,0:T(8,128)(2,1)S(1)}, u32[]{:S(2)}, u32[]{:S(2)}) collective-permute-start(bf16[2048,256]{1,0:T(8,128)(2,1)S(1)} %pad_maximum_fusion.7), channel_id=1, source_target_pairs={{0,2},{2,0},{4,6},{6,4},{8,10},{10,8},{12,14},{14,12},{16,18},{18,... | collective-permute-start | bytes 3145736 | tf_op jit(solution)/shard_map/ppermute | solution.py:142

commit v6 on v5

--- a/solution.py
+++ b/solution.py
@@ -31,7 +31,7 @@
     last = deep - 1
     plan = [("G", 0, 0), ("O", 1, 0), ("G", 1, 0), ("J", 0, last), ("G", 2, 0), ("J", 1, last), ("G", 3, 0)]
     for depth in reversed(range(1, last)):
-        plan += [("J", 0, depth), ("J", 1, depth), ("J", 2, depth + 1), ("J", 3, depth + 1)]
+        plan += [("J", 0, depth), ("J", 2, depth + 1), ("J", 1, depth), ("J", 3, depth + 1)]
     plan += [("O", 0, 0), ("J", 2, 1), ("J", 3, 1), ("J", 0, 0), ("J", 1, 0)]
     plan += [("H", 0, 0), ("K", 0, 0), ("H", 1, 0), ("M", 1, 0), ("K", 1, 0), ("H", 2, 0), ("H", 3, 0), ("O", 2, 0)]
     return plan + [("J", 2, 0), ("J", 3, 0), ("M", 2, 0), ("M", 3, 0), ("K", 2, 0), ("K", 3, 0)]

time: 151 us -> 151 us (level)
  starting transfers between devices: 42.9 us -> 40.4 us
  waiting for transfers between devices: 60.4 us -> 62.6 us
    ppermute x32, starting transfers between devices: 39.3 us -> 36.8 us  [swap(): return lax.ppermute(value, 'dp', [(i, i ^ 1 << bit) for i in range(n)])]
    ppermute x32, waiting for transfers between devices: 48.5 us -> 50.7 us  [swap(): return lax.ppermute(value, 'dp', [(i, i ^ 1 << bit) for i in range(n)])]
  transfers between devices with their start and end apart: 37 -> 37, of which waited for: 23 -> 25; matrix products, arithmetic and copies ran while one was open for 13% -> 13% of each run, Pallas kernels for 11% -> 11%
where the time goes in v6:
time: 151 us
  waiting for transfers between devices  62.6 us (41%)
  starting transfers between devices  40.4 us (27%)
  Pallas kernels  16.9 us (11%)
  other arithmetic  12.1 us (8%)
  local copies, waits for them, and re-layouts  9.32 us (6%)
  matrix products  7.52 us (5%)
  between operations  2.09 us (1%)
    ppermute x32, waiting for transfers between devices, swap(): return lax.ppermute(value, 'dp', [(i, i ^ 1 << bit) for i in range(n)])  50.7 us
    ppermute x32, starting transfers between devices, swap(): return lax.ppermute(value, 'dp', [(i, i ^ 1 << bit) for i in range(n)])  36.8 us
    pallas_call x9, Pallas kernels, multiply(): pl.pallas_call(kernel, out_shape=jax.ShapeDtypeStruct((height, wide), dty...  12.6 us
    ppermute x5, waiting for transfers between devices, total(): lax.ppermute(value, axis, [(i, i ^ 1 << bit) for i in range(size)])  11.9 us
    pallas_call x4, Pallas kernels, pick_blocks(): pl.pallas_call(kernel, out_shape=[jax.ShapeDtypeStruct((tokens, half * wi...  4.3 us
    dot_general x4, matrix products, dot_t(): lax.dot_general(a, g, (((0,), (0,)), ((), ())), preferred_element_type=F32)  4.05 us
    ppermute x5, starting transfers between devices, total(): lax.ppermute(value, axis, [(i, i ^ 1 << bit) for i in range(size)])  3.58 us
    dot_general x6, matrix products, dot(): lax.dot_general(a, w, (((1,), (0,)), ((), ())), preferred_element_type=F32)  3.48 us
  transfers between devices with their start and end apart: 37, of which 25 were waited for; matrix products, arithmetic and copies ran while one was open for 13% of the time, Pallas kernels for 11%

profile of v6, /device:TPU:0, one launch (start us, length us, event | category | flops | bytes accessed | tf_op | source)
XLA Modules:
  0.0 151.0 jit_solution(13078775183240762069)
XLA Ops:
  0.6 1.8 %copy.117 = bf16[768,2,512]{2,0,1:T(8,128)(2,1)S(1)} copy(bf16[768,2,512]{2,1,0:T(2,128)(2,1)} %param.7) | data formatting | bytes 3145728 | tf_op args[1]
  3.1 1.9 %collective-permute-done = bf16[768,512]{1,0:T(8,128)(2,1)S(1)} collective-permute-done((bf16[768,512]{1,0:T(8,128)(2,1)S(1)}, bf16[768,512]{1,0:T(8,128)(2,1)S(1)}, u32[]{:S(2)}, u32[]{:S(2)}) %collective-permute-start) | collective-permute-done | bytes 786464 | tf_op jit(solution)/shard_map/ppermute | solution.py:142
  6.6 1.1 shard_map.102
  13.5 2.7 %collective-permute-start.4 = (f16[1024,256]{1,0:T(8,128)(2,1)S(1)}, f16[1024,256]{1,0:T(8,128)(2,1)S(1)}, u32[]{:S(2)}, u32[]{:S(2)}) collective-permute-start(f16[1024,256]{1,0:T(8,128)(2,1)S(1)} %slice.220), channel_id=1, source_target_pairs={{0,4},{2,6},{4,0},{6,2},{8,12},{10,14},{12,8},{14,10},{16,20},{18,... | collective-permute-start | bytes 1572872 | tf_op jit(solution)/shard_map/ppermute | solution.py:142
  16.9 1.6 %collective-permute-start.6 = (f16[1024,256]{1,0:T(8,128)(2,1)S(1)}, f16[1024,256]{1,0:T(8,128)(2,1)S(1)}, u32[]{:S(2)}, u32[]{:S(2)}) collective-permute-start(f16[1024,256]{1,0:T(8,128)(2,1)S(1)} %pad_maximum_fusion.8), channel_id=1, source_target_pairs={{0,8},{2,10},{4,12},{6,14},{8,0},{10,2},{12,4},{14,6},{16,24},{18,... | collective-permute-start | bytes 1572872 | tf_op jit(solution)/shard_map/ppermute | solution.py:142
  18.5 2.5 %shard_map.103 = f32[1024,512]{1,0:T(8,128)S(1)} custom-call(bf16[768,1024]{1,0:T(8,128)(2,1)S(1)} %get-tuple-element.75.refs_0_, bf16[768,512]{1,0:T(8,128)(2,1)S(1)} %get-tuple-element.82.refs_1_, bf16[768,1024]{1,0:T(8,128)(2,1)S(1)} %collective-permute-done.1.refs_2_, bf16[768,512]{1,0:T(8,128)(2,1)S(1)} %collective-permute-done.3.refs_3_), custom_call_target="tpu_custom_call" | custom-call | tf_op jit(solution)/shard_map/pallas_call | solution.py:115
  22.1 2.5 %shard_map.104 = f32[1024,512]{1,0:T(8,128)S(1)} custom-call(bf16[768,1024]{1,0:T(8,128)(2,1)S(1)} %get-tuple-element.74.refs_0_, bf16[768,512]{1,0:T(8,128)(2,1)S(1)} %get-tuple-element.82.refs_1_, bf16[768,1024]{1,0:T(8,128)(2,1)S(1)} %collective-permute-done.2.refs_2_, bf16[768,512]{1,0:T(8,128)(2,1)S(1)} %collective-permute-done.3.refs_3_), custom_call_target="tpu_custom_call" | custom-call | tf_op jit(solution)/shard_map/pallas_call | solution.py:115
  25.7 1.2 shard_map.106
  26.9 2.0 %collective-permute-done.4 = f16[1024,256]{1,0:T(8,128)(2,1)S(1)} collective-permute-done((f16[1024,256]{1,0:T(8,128)(2,1)S(1)}, f16[1024,256]{1,0:T(8,128)(2,1)S(1)}, u32[]{:S(2)}, u32[]{:S(2)}) %collective-permute-start.4) | collective-permute-done | bytes 524320 | tf_op jit(solution)/shard_map/ppermute | solution.py:142
  29.1 2.1 %collective-permute-start.5 = (f16[512,256]{1,0:T(8,128)(2,1)S(1)}, f16[512,256]{1,0:T(8,128)(2,1)S(1)}, u32[]{:S(2)}, u32[]{:S(2)}) collective-permute-start(f16[512,256]{1,0:T(8,128)(2,1)S(1)} %slice_convert_fusion.4), channel_id=1, source_target_pairs={{0,8},{2,10},{4,12},{6,14},{8,0},{10,2},{12,4},{14,6},{16,24},{18,... | collective-permute-start | bytes 786440 | tf_op jit(solution)/shard_map/ppermute | solution.py:142
  33.8 1.5 collective-permute-start.9
  35.7 2.8 %collective-permute-done.5 = f16[512,256]{1,0:T(8,128)(2,1)S(1)} collective-permute-done((f16[512,256]{1,0:T(8,128)(2,1)S(1)}, f16[512,256]{1,0:T(8,128)(2,1)S(1)}, u32[]{:S(2)}, u32[]{:S(2)}) %collective-permute-start.5) | collective-permute-done | bytes 262176 | tf_op jit(solution)/shard_map/ppermute | solution.py:142
  38.6 3.0 %collective-permute-start.7 = (f16[256,256]{1,0:T(8,128)(2,1)S(1)}, f16[256,256]{1,0:T(8,128)(2,1)S(1)}, u32[]{:S(2)}, u32[]{:S(2)}) collective-permute-start(f16[256,256]{1,0:T(8,128)(2,1)S(1)} %slice_convert_fusion.9), channel_id=1, source_target_pairs={{0,16},{2,18},{4,20},{6,22},{8,24},{10,26},{12,28},{14,30},{16,0},... | collective-permute-start | bytes 393224 | tf_op jit(solution)/shard_map/ppermute | solution.py:142
  41.8 3.1 %collective-permute-start.12 = (f16[512,256]{1,0:T(8,128)(2,1)S(1)}, f16[512,256]{1,0:T(8,128)(2,1)S(1)}, u32[]{:S(2)}, u32[]{:S(2)}) collective-permute-start(f16[512,256]{1,0:T(8,128)(2,1)S(1)} %slice_convert_fusion.1), channel_id=1, source_target_pairs={{0,8},{2,10},{4,12},{6,14},{8,0},{10,2},{12,4},{14,6},{16,24},{18,... | collective-permute-start | bytes 786440 | tf_op jit(solution)/shard_map/ppermute | solution.py:142
  45.6 2.8 %collective-permute-start.13 = (f16[256,256]{1,0:T(8,128)(2,1)S(1)}, f16[256,256]{1,0:T(8,128)(2,1)S(1)}, u32[]{:S(2)}, u32[]{:S(2)}) collective-permute-start(f16[256,256]{1,0:T(8,128)(2,1)S(1)} %slice_convert_fusion.8), channel_id=1, source_target_pairs={{0,16},{2,18},{4,20},{6,22},{8,24},{10,26},{12,28},{14,30},{16,0},... | collective-permute-start | bytes 393224 | tf_op jit(solution)/shard_map/ppermute | solution.py:142
  48.4 7.0 %collective-permute-done.8 = f16[1024,256]{1,0:T(8,128)(2,1)S(1)} collective-permute-done((f16[1024,256]{1,0:T(8,128)(2,1)S(1)}, f16[1024,256]{1,0:T(8,128)(2,1)S(1)}, u32[]{:S(2)}, u32[]{:S(2)}) %collective-permute-start.8) | collective-permute-done | bytes 524320 | tf_op jit(solution)/shard_map/ppermute | solution.py:142
  55.5 2.0 %collective-permute-start.11 = (f16[512,256]{1,0:T(8,128)(2,1)S(1)}, f16[512,256]{1,0:T(8,128)(2,1)S(1)}, u32[]{:S(2)}, u32[]{:S(2)}) collective-permute-start(f16[512,256]{1,0:T(8,128)(2,1)S(1)} %slice_convert_fusion), channel_id=1, source_target_pairs={{0,4},{2,6},{4,0},{6,2},{8,12},{10,14},{12,8},{14,10},{16,20},{18,... | collective-permute-start | bytes 786440 | tf_op jit(solution)/shard_map/ppermute | solution.py:142
  57.5 1.9 %collective-permute-done.12 = f16[512,256]{1,0:T(8,128)(2,1)S(1)} collective-permute-done((f16[512,256]{1,0:T(8,128)(2,1)S(1)}, f16[512,256]{1,0:T(8,128)(2,1)S(1)}, u32[]{:S(2)}, u32[]{:S(2)}) %collective-permute-start.12) | collective-permute-done | bytes 262176 | tf_op jit(solution)/shard_map/ppermute | solution.py:142
  59.5 1.8 %collective-permute-start.14 = (f16[256,256]{1,0:T(8,128)(2,1)S(1)}, f16[256,256]{1,0:T(8,128)(2,1)S(1)}, u32[]{:S(2)}, u32[]{:S(2)}) collective-permute-start(f16[256,256]{1,0:T(8,128)(2,1)S(1)} %slice_convert_fusion.7), channel_id=1, source_target_pairs={{0,16},{2,18},{4,20},{6,22},{8,24},{10,26},{12,28},{14,30},{16,0},... | collective-permute-start | bytes 393224 | tf_op jit(solution)/shard_map/ppermute | solution.py:142
  62.0 2.2 %collective-permute-start.15 = (f16[256,256]{1,0:T(8,128)(2,1)S(1)}, f16[256,256]{1,0:T(8,128)(2,1)S(1)}, u32[]{:S(2)}, u32[]{:S(2)}) collective-permute-start(f16[256,256]{1,0:T(8,128)(2,1)S(1)} %slice_convert_fusion.6), channel_id=1, source_target_pairs={{0,16},{2,18},{4,20},{6,22},{8,24},{10,26},{12,28},{14,30},{16,0},... | collective-permute-start | bytes 393224 | tf_op jit(solution)/shard_map/ppermute | solution.py:142
  64.3 6.7 %collective-permute-done.14 = f16[256,256]{1,0:T(8,128)(2,1)S(1)} collective-permute-done((f16[256,256]{1,0:T(8,128)(2,1)S(1)}, f16[256,256]{1,0:T(8,128)(2,1)S(1)}, u32[]{:S(2)}, u32[]{:S(2)}) %collective-permute-start.14) | collective-permute-done | bytes 131104 | tf_op jit(solution)/shard_map/ppermute | solution.py:142
  71.1 1.7 %collective-permute-done.15 = f16[256,256]{1,0:T(8,128)(2,1)S(1)} collective-permute-done((f16[256,256]{1,0:T(8,128)(2,1)S(1)}, f16[256,256]{1,0:T(8,128)(2,1)S(1)}, u32[]{:S(2)}, u32[]{:S(2)}) %collective-permute-start.15) | collective-permute-done | bytes 131104 | tf_op jit(solution)/shard_map/ppermute | solution.py:142
  73.7 1.2 collective-permute-done.16
  74.9 1.4 collective-permute-start.17
  76.3 2.3 %collective-permute-done.17 = f32[4,512]{1,0:T(4,128)S(1)} collective-permute-done((f32[4,512]{1,0:T(4,128)S(1)}, f32[4,512]{1,0:T(4,128)S(1)}, u32[]{:S(2)}, u32[]{:S(2)}) %collective-permute-start.17) | collective-permute-done | bytes 8224 | tf_op jit(solution)/shard_map/ppermute | solution.py:149
  78.6 1.4 collective-permute-start.18
  80.1 2.1 %collective-permute-done.18 = f32[4,512]{1,0:T(4,128)S(1)} collective-permute-done((f32[4,512]{1,0:T(4,128)S(1)}, f32[4,512]{1,0:T(4,128)S(1)}, u32[]{:S(2)}, u32[]{:S(2)}) %collective-permute-start.18) | collective-permute-done | bytes 8224 | tf_op jit(solution)/shard_map/ppermute | solution.py:149
  82.8 3.1 %collective-permute-done.19 = f32[4,512]{1,0:T(4,128)S(1)} collective-permute-done((f32[4,512]{1,0:T(4,128)S(1)}, f32[4,512]{1,0:T(4,128)S(1)}, u32[]{:S(2)}, u32[]{:S(2)}) %collective-permute-start.19) | collective-permute-done | bytes 8224 | tf_op jit(solution)/shard_map/ppermute | solution.py:149
  87.3 3.2 %collective-permute-done.20 = f32[4,512]{1,0:T(4,128)S(1)} collective-permute-done((f32[4,512]{1,0:T(4,128)S(1)}, f32[4,512]{1,0:T(4,128)S(1)}, u32[]{:S(2)}, u32[]{:S(2)}) %collective-permute-start.20) | collective-permute-done | bytes 8224 | tf_op jit(solution)/shard_map/ppermute | solution.py:149
  92.4 1.8 %copy.80 = f32[256,2,512]{2,1,0:T(2,128)} copy(f32[256,2,512]{2,0,1:T(8,128)S(1)} %pad_maximum_fusion.2) | data formatting | bytes 2097152 | tf_op jit(solution)/shard_map/optimization_barrier | solution.py:41
  94.2 2.3 %collective-permute-start.21 = (bf16[256,256]{1,0:T(8,128)(2,1)S(1)}, bf16[256,256]{1,0:T(8,128)(2,1)S(1)}, u32[]{:S(2)}, u32[]{:S(2)}) collective-permute-start(bf16[256,256]{1,0:T(8,128)(2,1)S(1)} %get-tuple-element.105), channel_id=1, source_target_pairs={{0,16},{2,18},{4,20},{6,22},{8,24},{10,26},{12,28},{14,30},{16,0},... | collective-permute-start | bytes 393224 | tf_op jit(solution)/shard_map/ppermute | solution.py:142
  97.4 2.5 %copy_subtract_fusion = (f32[256,1,512]{2,1,0:T(1,128)S(1)}, f32[256,1,512]{2,1,0:T(1,128)S(1)}) fusion(f32[256,1,512]{2,0,1:T(8,128)S(1)} %get-tuple-element.161, f32[256,1,512]{2,0,1:T(8,128)S(1)} %get-tuple-element.160, f32[256,1,512]{2,0,1:T(8,128)S(1)} %get-tuple-element.158, f32[]{:T(128)} %bitcast.6, f32[]{:T(128)} %bitcast.4, f32[512]{0:T(512)S(1)} %bitcast.83, ...), kind=kLoop, calls=%fused_computation.73 | loop fusion | flops 1048576 | bytes 3672072 | tf_op jit(solution)/shard_map/sub | solution.py:255
  100.0 2.8 %collective-permute-start.25 = (bf16[256,256]{1,0:T(8,128)(2,1)S(1)}, bf16[256,256]{1,0:T(8,128)(2,1)S(1)}, u32[]{:S(2)}, u32[]{:S(2)}) collective-permute-start(bf16[256,256]{1,0:T(8,128)(2,1)S(1)} %get-tuple-element.107), channel_id=1, source_target_pairs={{0,16},{2,18},{4,20},{6,22},{8,24},{10,26},{12,28},{14,30},{16,0},... | collective-permute-start | bytes 393224 | tf_op jit(solution)/shard_map/ppermute | solution.py:142
  102.8 3.4 %collective-permute-done.21 = bf16[256,256]{1,0:T(8,128)(2,1)S(1)} collective-permute-done((bf16[256,256]{1,0:T(8,128)(2,1)S(1)}, bf16[256,256]{1,0:T(8,128)(2,1)S(1)}, u32[]{:S(2)}, u32[]{:S(2)}) %collective-permute-start.21) | collective-permute-done | bytes 131104 | tf_op jit(solution)/shard_map/ppermute | solution.py:142
  106.2 1.3 collective-permute-start.24
  107.6 3.8 %collective-permute-done.26 = bf16[512,256]{1,0:T(8,128)(2,1)S(1)} collective-permute-done((bf16[512,256]{1,0:T(8,128)(2,1)S(1)}, bf16[512,256]{1,0:T(8,128)(2,1)S(1)}, u32[]{:S(2)}, u32[]{:S(2)}) %collective-permute-start.26) | collective-permute-done | bytes 262176 | tf_op jit(solution)/shard_map/ppermute | solution.py:142
  111.4 1.4 collective-permute-start.30
  112.9 2.6 %collective-permute-done.24 = bf16[512,256]{1,0:T(8,128)(2,1)S(1)} collective-permute-done((bf16[512,256]{1,0:T(8,128)(2,1)S(1)}, bf16[512,256]{1,0:T(8,128)(2,1)S(1)}, u32[]{:S(2)}, u32[]{:S(2)}) %collective-permute-start.24) | collective-permute-done | bytes 262176 | tf_op jit(solution)/shard_map/ppermute | solution.py:142
  115.7 1.3 collective-permute-start.27
  117.0 3.2 %pad_maximum_fusion.1 = (f32[256,2,512]{2,1,0:T(2,128)}, f32[256,2,512]{2,1,0:T(2,128)}) fusion(f32[256,1,512]{2,1,0:T(1,128)S(1)} %get-tuple-element.138, f32[256,1,512]{2,1,0:T(1,128)S(1)} %fusion.21, f32[256,1,512]{2,1,0:T(1,128)S(1)} %get-tuple-element.139, f32[256,1,512]{2,1,0:T(1,128)S(1)} %copy.81), kind=kLoop, calls=%fused_computation.16 | loop fusion | flops 524288 | bytes 4194304 | tf_op jit(solution)/shard_map/stack | solution.py:257
  120.2 2.0 %collective-permute-done.28 = bf16[512,256]{1,0:T(8,128)(2,1)S(1)} collective-permute-done((bf16[512,256]{1,0:T(8,128)(2,1)S(1)}, bf16[512,256]{1,0:T(8,128)(2,1)S(1)}, u32[]{:S(2)}, u32[]{:S(2)}) %collective-permute-start.28) | collective-permute-done | bytes 262176 | tf_op jit(solution)/shard_map/ppermute | solution.py:142
  122.1 4.1 %collective-permute-done.27 = bf16[512,256]{1,0:T(8,128)(2,1)S(1)} collective-permute-done((bf16[512,256]{1,0:T(8,128)(2,1)S(1)}, bf16[512,256]{1,0:T(8,128)(2,1)S(1)}, u32[]{:S(2)}, u32[]{:S(2)}) %collective-permute-start.27) | collective-permute-done | bytes 262176 | tf_op jit(solution)/shard_map/ppermute | solution.py:142
  126.5 2.0 %collective-permute-done.29.refs_1_ = bf16[1024,256]{1,0:T(8,128)(2,1)S(1)} collective-permute-done((bf16[1024,256]{1,0:T(8,128)(2,1)S(1)}, bf16[1024,256]{1,0:T(8,128)(2,1)S(1)}, u32[]{:S(2)}, u32[]{:S(2)}) %collective-permute-start.29) | collective-permute-done | bytes 524320 | tf_op jit(solution)/shard_map/ppermute | solution.py:142
  128.6 1.4 collective-permute-start.33
  131.0 1.8 %shard_map.108 = bf16[768,256]{1,0:T(8,128)(2,1)S(1)} custom-call(bf16[768,1024]{1,0:T(8,128)(2,1)S(1)} %get-tuple-element.75.refs_0_, bf16[1024,256]{1,0:T(8,128)(2,1)S(1)} %collective-permute-done.30.refs_1_, bf16[768,1024]{1,0:T(8,128)(2,1)S(1)} %get-tuple-element.71.refs_2_, bf16[1024,256]{1,0:T(8,128)(2,1)S(1)} %get-tuple-element.157.refs_3_, ...), custom_call_target="tpu_custom_call" | custom-call | tf_op jit(solution)/shard_map/pallas_call | solution.py:115
  134.7 1.3 shard_map.111
  137.9 5.0 %collective-permute-done.33 = bf16[1024,256]{1,0:T(8,128)(2,1)S(1)} collective-permute-done((bf16[1024,256]{1,0:T(8,128)(2,1)S(1)}, bf16[1024,256]{1,0:T(8,128)(2,1)S(1)}, u32[]{:S(2)}, u32[]{:S(2)}) %collective-permute-start.33) | collective-permute-done | bytes 524320 | tf_op jit(solution)/shard_map/ppermute | solution.py:142
  148.6 2.4 %reshape.311 = bf16[768,2,512]{2,1,0:T(2,128)(2,1)} reshape(bf16[768,1024]{1,0:T(8,128)(2,1)S(1)} %pad_maximum_fusion) | data formatting | bytes 3145728 | tf_op jit(solution)/shard_map/reshape | solution.py:305
  (136 shorter events, 32.1 us)
Async XLA Ops:
  0.6 4.4 %copy-start = (bf16[768,4096]{1,0:T(8,128)(2,1)S(1)}, bf16[768,4096]{1,0:T(8,128)(2,1)}, u32[]{:S(2)}) copy-start(bf16[768,4096]{1,0:T(8,128)(2,1)} %src.3) | copy-start | bytes 18874372
  2.6 2.4 %collective-permute-start = (bf16[768,512]{1,0:T(8,128)(2,1)S(1)}, bf16[768,512]{1,0:T(8,128)(2,1)S(1)}, u32[]{:S(2)}, u32[]{:S(2)}) collective-permute-start(bf16[768,512]{1,0:T(8,128)(2,1)S(1)} %get-tuple-element.77), channel_id=1, source_target_pairs={{0,2},{2,0},{4,6},{6,4},{8,10},{10,8},{12,14},{14,12},{16,18},{18,... | collective-permute-start | bytes 2359304 | tf_op jit(solution)/shard_map/ppermute | solution.py:142
  6.0 3.5 %collective-permute-start.1 = (bf16[768,1024]{1,0:T(8,128)(2,1)S(1)}, bf16[768,1024]{1,0:T(8,128)(2,1)S(1)}, u32[]{:S(2)}, u32[]{:S(2)}) collective-permute-start(bf16[768,1024]{1,0:T(8,128)(2,1)S(1)} %get-tuple-element.72.refs_4_), channel_id=1, source_target_pairs={{0,2},{2,0},{4,6},{6,4},{8,10},{10,8},{12,14},{14,12},{16,18},{18,... | collective-permute-start | bytes 4718600 | tf_op jit(solution)/shard_map/ppermute | solution.py:142
  6.5 5.3 %collective-permute-start.2 = (bf16[768,1024]{1,0:T(8,128)(2,1)S(1)}, bf16[768,1024]{1,0:T(8,128)(2,1)S(1)}, u32[]{:S(2)}, u32[]{:S(2)}) collective-permute-start(bf16[768,1024]{1,0:T(8,128)(2,1)S(1)} %get-tuple-element.71.refs_2_), channel_id=1, source_target_pairs={{0,2},{2,0},{4,6},{6,4},{8,10},{10,8},{12,14},{14,12},{16,18},{18,... | collective-permute-start | bytes 4718600 | tf_op jit(solution)/shard_map/ppermute | solution.py:142
  13.0 5.5 %collective-permute-start.3 = (bf16[768,512]{1,0:T(8,128)(2,1)S(1)}, bf16[768,512]{1,0:T(8,128)(2,1)S(1)}, u32[]{:S(2)}, u32[]{:S(2)}) collective-permute-start(bf16[768,512]{1,0:T(8,128)(2,1)S(1)} %get-tuple-element.82.refs_1_), channel_id=1, source_target_pairs={{0,2},{2,0},{4,6},{6,4},{8,10},{10,8},{12,14},{14,12},{16,18},{18,... | collective-permute-start | bytes 2359304 | tf_op jit(solution)/shard_map/ppermute | solution.py:142
  13.5 15.4 %collective-permute-start.4 = (f16[1024,256]{1,0:T(8,128)(2,1)S(1)}, f16[1024,256]{1,0:T(8,128)(2,1)S(1)}, u32[]{:S(2)}, u32[]{:S(2)}) collective-permute-start(f16[1024,256]{1,0:T(8,128)(2,1)S(1)} %slice.220), channel_id=1, source_target_pairs={{0,4},{2,6},{4,0},{6,2},{8,12},{10,14},{12,8},{14,10},{16,20},{18,... | collective-permute-start | bytes 1572872 | tf_op jit(solution)/shard_map/ppermute | solution.py:142
  16.9 14.7 %collective-permute-start.6 = (f16[1024,256]{1,0:T(8,128)(2,1)S(1)}, f16[1024,256]{1,0:T(8,128)(2,1)S(1)}, u32[]{:S(2)}, u32[]{:S(2)}) collective-permute-start(f16[1024,256]{1,0:T(8,128)(2,1)S(1)} %pad_maximum_fusion.8), channel_id=1, source_target_pairs={{0,8},{2,10},{4,12},{6,14},{8,0},{10,2},{12,4},{14,6},{16,24},{18,... | collective-permute-start | bytes 1572872 | tf_op jit(solution)/shard_map/ppermute | solution.py:142
  21.5 20.1 %collective-permute-start.10 = (f16[1024,256]{1,0:T(8,128)(2,1)S(1)}, f16[1024,256]{1,0:T(8,128)(2,1)S(1)}, u32[]{:S(2)}, u32[]{:S(2)}) collective-permute-start(f16[1024,256]{1,0:T(8,128)(2,1)S(1)} %slice.221), channel_id=1, source_target_pairs={{0,4},{2,6},{4,0},{6,2},{8,12},{10,14},{12,8},{14,10},{16,20},{18,... | collective-permute-start | bytes 1572872 | tf_op jit(solution)/shard_map/ppermute | solution.py:142
  29.1 9.4 %collective-permute-start.5 = (f16[512,256]{1,0:T(8,128)(2,1)S(1)}, f16[512,256]{1,0:T(8,128)(2,1)S(1)}, u32[]{:S(2)}, u32[]{:S(2)}) collective-permute-start(f16[512,256]{1,0:T(8,128)(2,1)S(1)} %slice_convert_fusion.4), channel_id=1, source_target_pairs={{0,8},{2,10},{4,12},{6,14},{8,0},{10,2},{12,4},{14,6},{16,24},{18,... | collective-permute-start | bytes 786440 | tf_op jit(solution)/shard_map/ppermute | solution.py:142
  31.4 1.2 copy-start.1
  31.5 23.8 %collective-permute-start.8 = (f16[1024,256]{1,0:T(8,128)(2,1)S(1)}, f16[1024,256]{1,0:T(8,128)(2,1)S(1)}, u32[]{:S(2)}, u32[]{:S(2)}) collective-permute-start(f16[1024,256]{1,0:T(8,128)(2,1)S(1)} %pad_maximum_fusion.9), channel_id=1, source_target_pairs={{0,8},{2,10},{4,12},{6,14},{8,0},{10,2},{12,4},{14,6},{16,24},{18,... | collective-permute-start | bytes 1572872 | tf_op jit(solution)/shard_map/ppermute | solution.py:142
  33.1 2.1 %copy-start.2 = (f32[256,2,512]{2,1,0:T(2,128)S(1)}, f32[256,2,512]{2,1,0:T(2,128)}, u32[]{:S(2)}) copy-start(f32[256,2,512]{2,1,0:T(2,128)} %param.9) | copy-start | bytes 3145732
  33.4 2.1 %copy-start.3 = (f32[256,2,512]{2,1,0:T(2,128)S(1)}, f32[256,2,512]{2,1,0:T(2,128)}, u32[]{:S(2)}) copy-start(f32[256,2,512]{2,1,0:T(2,128)} %param.10) | copy-start | bytes 3145732
  33.8 11.7 %collective-permute-start.9 = (f16[512,256]{1,0:T(8,128)(2,1)S(1)}, f16[512,256]{1,0:T(8,128)(2,1)S(1)}, u32[]{:S(2)}, u32[]{:S(2)}) collective-permute-start(f16[512,256]{1,0:T(8,128)(2,1)S(1)} %slice_convert_fusion.2), channel_id=1, source_target_pairs={{0,4},{2,6},{4,0},{6,2},{8,12},{10,14},{12,8},{14,10},{16,20},{18,... | collective-permute-start | bytes 786440 | tf_op jit(solution)/shard_map/ppermute | solution.py:142
  38.6 25.7 %collective-permute-start.7 = (f16[256,256]{1,0:T(8,128)(2,1)S(1)}, f16[256,256]{1,0:T(8,128)(2,1)S(1)}, u32[]{:S(2)}, u32[]{:S(2)}) collective-permute-start(f16[256,256]{1,0:T(8,128)(2,1)S(1)} %slice_convert_fusion.9), channel_id=1, source_target_pairs={{0,16},{2,18},{4,20},{6,22},{8,24},{10,26},{12,28},{14,30},{16,0},... | collective-permute-start | bytes 393224 | tf_op jit(solution)/shard_map/ppermute | solution.py:142
  41.8 17.5 %collective-permute-start.12 = (f16[512,256]{1,0:T(8,128)(2,1)S(1)}, f16[512,256]{1,0:T(8,128)(2,1)S(1)}, u32[]{:S(2)}, u32[]{:S(2)}) collective-permute-start(f16[512,256]{1,0:T(8,128)(2,1)S(1)} %slice_convert_fusion.1), channel_id=1, source_target_pairs={{0,8},{2,10},{4,12},{6,14},{8,0},{10,2},{12,4},{14,6},{16,24},{18,... | collective-permute-start | bytes 786440 | tf_op jit(solution)/shard_map/ppermute | solution.py:142
  45.6 18.7 %collective-permute-start.13 = (f16[256,256]{1,0:T(8,128)(2,1)S(1)}, f16[256,256]{1,0:T(8,128)(2,1)S(1)}, u32[]{:S(2)}, u32[]{:S(2)}) collective-permute-start(f16[256,256]{1,0:T(8,128)(2,1)S(1)} %slice_convert_fusion.8), channel_id=1, source_target_pairs={{0,16},{2,18},{4,20},{6,22},{8,24},{10,26},{12,28},{14,30},{16,0},... | collective-permute-start | bytes 393224 | tf_op jit(solution)/shard_map/ppermute | solution.py:142
  55.5 6.4 %collective-permute-start.11 = (f16[512,256]{1,0:T(8,128)(2,1)S(1)}, f16[512,256]{1,0:T(8,128)(2,1)S(1)}, u32[]{:S(2)}, u32[]{:S(2)}) collective-permute-start(f16[512,256]{1,0:T(8,128)(2,1)S(1)} %slice_convert_fusion), channel_id=1, source_target_pairs={{0,4},{2,6},{4,0},{6,2},{8,12},{10,14},{12,8},{14,10},{16,20},{18,... | collective-permute-start | bytes 786440 | tf_op jit(solution)/shard_map/ppermute | solution.py:142
  59.5 11.6 %collective-permute-start.14 = (f16[256,256]{1,0:T(8,128)(2,1)S(1)}, f16[256,256]{1,0:T(8,128)(2,1)S(1)}, u32[]{:S(2)}, u32[]{:S(2)}) collective-permute-start(f16[256,256]{1,0:T(8,128)(2,1)S(1)} %slice_convert_fusion.7), channel_id=1, source_target_pairs={{0,16},{2,18},{4,20},{6,22},{8,24},{10,26},{12,28},{14,30},{16,0},... | collective-permute-start | bytes 393224 | tf_op jit(solution)/shard_map/ppermute | solution.py:142
  62.0 10.7 %collective-permute-start.15 = (f16[256,256]{1,0:T(8,128)(2,1)S(1)}, f16[256,256]{1,0:T(8,128)(2,1)S(1)}, u32[]{:S(2)}, u32[]{:S(2)}) collective-permute-start(f16[256,256]{1,0:T(8,128)(2,1)S(1)} %slice_convert_fusion.6), channel_id=1, source_target_pairs={{0,16},{2,18},{4,20},{6,22},{8,24},{10,26},{12,28},{14,30},{16,0},... | collective-permute-start | bytes 393224 | tf_op jit(solution)/shard_map/ppermute | solution.py:142
  73.6 1.2 collective-permute-start.16
  74.9 3.7 %collective-permute-start.17 = (f32[4,512]{1,0:T(4,128)S(1)}, f32[4,512]{1,0:T(4,128)S(1)}, u32[]{:S(2)}, u32[]{:S(2)}) collective-permute-start(f32[4,512]{1,0:T(4,128)S(1)} %fusion.26), channel_id=1, source_target_pairs={{0,1},{1,0},{2,3},{3,2},{4,5},{5,4},{6,7},{7,6},{8,9},{9,8},{10,11... | collective-permute-start | bytes 24584 | tf_op jit(solution)/shard_map/ppermute | solution.py:149
  78.6 3.7 %collective-permute-start.18 = (f32[4,512]{1,0:T(4,128)S(1)}, f32[4,512]{1,0:T(4,128)S(1)}, u32[]{:S(2)}, u32[]{:S(2)}) collective-permute-start(f32[4,512]{1,0:T(4,128)S(1)} %add.154), channel_id=1, source_target_pairs={{0,4},{2,6},{4,0},{6,2},{8,12},{10,14},{12,8},{14,10},{16,20},{18,... | collective-permute-start | bytes 24584 | tf_op jit(solution)/shard_map/ppermute | solution.py:149
  82.3 3.7 %collective-permute-start.19 = (f32[4,512]{1,0:T(4,128)S(1)}, f32[4,512]{1,0:T(4,128)S(1)}, u32[]{:S(2)}, u32[]{:S(2)}) collective-permute-start(f32[4,512]{1,0:T(4,128)S(1)} %add.155), channel_id=1, source_target_pairs={{0,8},{2,10},{4,12},{6,14},{8,0},{10,2},{12,4},{14,6},{16,24},{18,... | collective-permute-start | bytes 24584 | tf_op jit(solution)/shard_map/ppermute | solution.py:149
  85.9 4.6 %collective-permute-start.20 = (f32[4,512]{1,0:T(4,128)S(1)}, f32[4,512]{1,0:T(4,128)S(1)}, u32[]{:S(2)}, u32[]{:S(2)}) collective-permute-start(f32[4,512]{1,0:T(4,128)S(1)} %add.156), channel_id=1, source_target_pairs={{0,16},{2,18},{4,20},{6,22},{8,24},{10,26},{12,28},{14,30},{16,0},... | collective-permute-start | bytes 24584 | tf_op jit(solution)/shard_map/ppermute | solution.py:149
  91.6 8.3 %collective-permute-start.22 = (bf16[256,256]{1,0:T(8,128)(2,1)S(1)}, bf16[256,256]{1,0:T(8,128)(2,1)S(1)}, u32[]{:S(2)}, u32[]{:S(2)}) collective-permute-start(bf16[256,256]{1,0:T(8,128)(2,1)S(1)} %get-tuple-element.103), channel_id=1, source_target_pairs={{0,16},{2,18},{4,20},{6,22},{8,24},{10,26},{12,28},{14,30},{16,0},... | collective-permute-start | bytes 393224 | tf_op jit(solution)/shard_map/ppermute | solution.py:142
  94.2 12.0 %collective-permute-start.21 = (bf16[256,256]{1,0:T(8,128)(2,1)S(1)}, bf16[256,256]{1,0:T(8,128)(2,1)S(1)}, u32[]{:S(2)}, u32[]{:S(2)}) collective-permute-start(bf16[256,256]{1,0:T(8,128)(2,1)S(1)} %get-tuple-element.105), channel_id=1, source_target_pairs={{0,16},{2,18},{4,20},{6,22},{8,24},{10,26},{12,28},{14,30},{16,0},... | collective-permute-start | bytes 393224 | tf_op jit(solution)/shard_map/ppermute | solution.py:142
  99.9 11.4 %collective-permute-start.26 = (bf16[512,256]{1,0:T(8,128)(2,1)S(1)}, bf16[512,256]{1,0:T(8,128)(2,1)S(1)}, u32[]{:S(2)}, u32[]{:S(2)}) collective-permute-start(bf16[512,256]{1,0:T(8,128)(2,1)S(1)} %get-tuple-element.176), channel_id=1, source_target_pairs={{0,8},{2,10},{4,12},{6,14},{8,0},{10,2},{12,4},{14,6},{16,24},{18,... | collective-permute-start | bytes 786440 | tf_op jit(solution)/shard_map/ppermute | solution.py:142
  100.0 12.8 %collective-permute-start.25 = (bf16[256,256]{1,0:T(8,128)(2,1)S(1)}, bf16[256,256]{1,0:T(8,128)(2,1)S(1)}, u32[]{:S(2)}, u32[]{:S(2)}) collective-permute-start(bf16[256,256]{1,0:T(8,128)(2,1)S(1)} %get-tuple-element.107), channel_id=1, source_target_pairs={{0,16},{2,18},{4,20},{6,22},{8,24},{10,26},{12,28},{14,30},{16,0},... | collective-permute-start | bytes 393224 | tf_op jit(solution)/shard_map/ppermute | solution.py:142
  106.2 9.3 %collective-permute-start.24 = (bf16[512,256]{1,0:T(8,128)(2,1)S(1)}, bf16[512,256]{1,0:T(8,128)(2,1)S(1)}, u32[]{:S(2)}, u32[]{:S(2)}) collective-permute-start(bf16[512,256]{1,0:T(8,128)(2,1)S(1)} %get-tuple-element.180), channel_id=1, source_target_pairs={{0,4},{2,6},{4,0},{6,2},{8,12},{10,14},{12,8},{14,10},{16,20},{18,... | collective-permute-start | bytes 786440 | tf_op jit(solution)/shard_map/ppermute | solution.py:142
  107.5 8.1 %collective-permute-start.23 = (bf16[256,256]{1,0:T(8,128)(2,1)S(1)}, bf16[256,256]{1,0:T(8,128)(2,1)S(1)}, u32[]{:S(2)}, u32[]{:S(2)}) collective-permute-start(bf16[256,256]{1,0:T(8,128)(2,1)S(1)} %get-tuple-element.109), channel_id=1, source_target_pairs={{0,16},{2,18},{4,20},{6,22},{8,24},{10,26},{12,28},{14,30},{16,0},... | collective-permute-start | bytes 393224 | tf_op jit(solution)/shard_map/ppermute | solution.py:142
  111.4 14.9 %collective-permute-start.30 = (bf16[1024,256]{1,0:T(8,128)(2,1)S(1)}, bf16[1024,256]{1,0:T(8,128)(2,1)S(1)}, u32[]{:S(2)}, u32[]{:S(2)}) collective-permute-start(bf16[1024,256]{1,0:T(8,128)(2,1)S(1)} %constant_dynamic-update-slice_fusion.4.refs_1_), channel_id=1, source_target_pairs={{0,4},{2,6},{4,0},{6,2},{8,12},{10,14},{12,8},{14,10},{16,20},{18,... | collective-permute-start | bytes 1572872 | tf_op jit(solution)/shard_map/ppermute | solution.py:142
  112.8 9.3 %collective-permute-start.28 = (bf16[512,256]{1,0:T(8,128)(2,1)S(1)}, bf16[512,256]{1,0:T(8,128)(2,1)S(1)}, u32[]{:S(2)}, u32[]{:S(2)}) collective-permute-start(bf16[512,256]{1,0:T(8,128)(2,1)S(1)} %get-tuple-element.168), channel_id=1, source_target_pairs={{0,8},{2,10},{4,12},{6,14},{8,0},{10,2},{12,4},{14,6},{16,24},{18,... | collective-permute-start | bytes 786440 | tf_op jit(solution)/shard_map/ppermute | solution.py:142
  115.5 12.9 %collective-permute-start.29 = (bf16[1024,256]{1,0:T(8,128)(2,1)S(1)}, bf16[1024,256]{1,0:T(8,128)(2,1)S(1)}, u32[]{:S(2)}, u32[]{:S(2)}) collective-permute-start(bf16[1024,256]{1,0:T(8,128)(2,1)S(1)} %constant_dynamic-update-slice_fusion.9.refs_1_), channel_id=1, source_target_pairs={{0,8},{2,10},{4,12},{6,14},{8,0},{10,2},{12,4},{14,6},{16,24},{18,... | collective-permute-start | bytes 1572872 | tf_op jit(solution)/shard_map/ppermute | solution.py:142
  115.7 10.6 %collective-permute-start.27 = (bf16[512,256]{1,0:T(8,128)(2,1)S(1)}, bf16[512,256]{1,0:T(8,128)(2,1)S(1)}, u32[]{:S(2)}, u32[]{:S(2)}) collective-permute-start(bf16[512,256]{1,0:T(8,128)(2,1)S(1)} %get-tuple-element.172), channel_id=1, source_target_pairs={{0,4},{2,6},{4,0},{6,2},{8,12},{10,14},{12,8},{14,10},{16,20},{18,... | collective-permute-start | bytes 786440 | tf_op jit(solution)/shard_map/ppermute | solution.py:142
  126.4 4.5 %collective-permute-start.32 = (bf16[2048,256]{1,0:T(8,128)(2,1)S(1)}, bf16[2048,256]{1,0:T(8,128)(2,1)S(1)}, u32[]{:S(2)}, u32[]{:S(2)}) collective-permute-start(bf16[2048,256]{1,0:T(8,128)(2,1)S(1)} %pad_maximum_fusion.5), channel_id=1, source_target_pairs={{0,2},{2,0},{4,6},{6,4},{8,10},{10,8},{12,14},{14,12},{16,18},{18,... | collective-permute-start | bytes 3145736 | tf_op jit(solution)/shard_map/ppermute | solution.py:142
  128.5 6.1 %collective-permute-start.31 = (bf16[2048,256]{1,0:T(8,128)(2,1)S(1)}, bf16[2048,256]{1,0:T(8,128)(2,1)S(1)}, u32[]{:S(2)}, u32[]{:S(2)}) collective-permute-start(bf16[2048,256]{1,0:T(8,128)(2,1)S(1)} %pad_maximum_fusion.4), channel_id=1, source_target_pairs={{0,2},{2,0},{4,6},{6,4},{8,10},{10,8},{12,14},{14,12},{16,18},{18,... | collective-permute-start | bytes 3145736 | tf_op jit(solution)/shard_map/ppermute | solution.py:142
  128.6 14.3 %collective-permute-start.33 = (bf16[1024,256]{1,0:T(8,128)(2,1)S(1)}, bf16[1024,256]{1,0:T(8,128)(2,1)S(1)}, u32[]{:S(2)}, u32[]{:S(2)}) collective-permute-start(bf16[1024,256]{1,0:T(8,128)(2,1)S(1)} %constant_dynamic-update-slice_fusion.14.refs_1_), channel_id=1, source_target_pairs={{0,4},{2,6},{4,0},{6,2},{8,12},{10,14},{12,8},{14,10},{16,20},{18,... | collective-permute-start | bytes 1572872 | tf_op jit(solution)/shard_map/ppermute | solution.py:142
  130.0 14.0 %collective-permute-start.34 = (bf16[1024,256]{1,0:T(8,128)(2,1)S(1)}, bf16[1024,256]{1,0:T(8,128)(2,1)S(1)}, u32[]{:S(2)}, u32[]{:S(2)}) collective-permute-start(bf16[1024,256]{1,0:T(8,128)(2,1)S(1)} %constant_dynamic-update-slice_fusion.17.refs_1_), channel_id=1, source_target_pairs={{0,8},{2,10},{4,12},{6,14},{8,0},{10,2},{12,4},{14,6},{16,24},{18,... | collective-permute-start | bytes 1572872 | tf_op jit(solution)/shard_map/ppermute | solution.py:142
  143.0 2.7 %collective-permute-start.35 = (bf16[2048,256]{1,0:T(8,128)(2,1)S(1)}, bf16[2048,256]{1,0:T(8,128)(2,1)S(1)}, u32[]{:S(2)}, u32[]{:S(2)}) collective-permute-start(bf16[2048,256]{1,0:T(8,128)(2,1)S(1)} %pad_maximum_fusion.6), channel_id=1, source_target_pairs={{0,2},{2,0},{4,6},{6,4},{8,10},{10,8},{12,14},{14,12},{16,18},{18,... | collective-permute-start | bytes 3145736 | tf_op jit(solution)/shard_map/ppermute | solution.py:142
  144.0 3.2 %collective-permute-start.36 = (bf16[2048,256]{1,0:T(8,128)(2,1)S(1)}, bf16[2048,256]{1,0:T(8,128)(2,1)S(1)}, u32[]{:S(2)}, u32[]{:S(2)}) collective-permute-start(bf16[2048,256]{1,0:T(8,128)(2,1)S(1)} %pad_maximum_fusion.7), channel_id=1, source_target_pairs={{0,2},{2,0},{4,6},{6,4},{8,10},{10,8},{12,14},{14,12},{16,18},{18,... | collective-permute-start | bytes 3145736 | tf_op jit(solution)/shard_map/ppermute | solution.py:142
